TPU v7x, 32 devices: a whole 2x2x4 slice. The times are simulated.
32 devices in a mesh: sec: 4 (over x, core), term: 8 (over z, y).
Axes of the slice: x: 2, y: 2, z: 4, core: 2. Of those that a mesh axis runs over, the one named last changes fastest.
Arguments:
- env_blocks: bfloat16 [8, 8, 256, 256], P('term', 'sec'), may hold values from -6 to 6
- core_blocks: bfloat16 [256, 256, 256], P('sec', 'term'), may hold values from -0.375 to 0.375
- mpo_coeffs: bfloat16 [8, 8, 256], P(None, None, 'sec'), may hold values from -2 to 2
- pair_left: int32 [256], P('sec'), may hold values from 0 to 1
- pair_right: int32 [256], P('sec'), may hold values from 0 to 7
- block_dims: int32 [8], replicated, may hold values from 1 to 256, 1536 in all
Outputs:
- new_env: float32 [8, 8, 256, 256], P('term', 'sec')
Inputs may be any that keep to these rules, and one draw needn't show every extreme that they name: `pair_left`: A pair's left block is one of the 2 blocks of the sec index that holds the pair.
All inputs are finite; a program needn't handle non-finite values.
Results may differ from a plain program's by a relative error of at most 0.004.
Values may be sent and summed in bfloat16 or wider, within the bound.
No kernel may reach another device: no remote copies, remote signals or barrier semaphores. Data moves between devices by JAX's collectives and lax.ppermute only.
A program may use at most 128 MiB of HBM per device.

v0:
```python
import jax
import jax.numpy as jnp
from jax import lax
from jax.sharding import PartitionSpec as P


def per_device(env_blocks, core_blocks, mpo_coeffs, pair_left, pair_right, block_dims):
    nb_local = env_blocks.shape[1]
    blk = env_blocks.shape[2]
    pairs_local = core_blocks.shape[0]
    total_blocks = block_dims.shape[0]
    sec_index = lax.axis_index("sec")
    term_index = lax.axis_index("term")
    core_full = lax.all_gather(core_blocks, "term", axis=1, tiled=True)
    block_ids = jnp.arange(total_blocks)
    left_global = sec_index * nb_local + pair_left
    dims_left = jnp.sum(
        jnp.where(left_global[:, None] == block_ids[None, :], block_dims[None, :], 0), axis=1
    )
    right_match = pair_right[:, None] == block_ids[None, :]
    dims_right = jnp.sum(jnp.where(right_match, block_dims[None, :], 0), axis=1)
    rows = jnp.arange(blk)
    keep = (rows[None, :, None] < dims_left[:, None, None]) & (
        rows[None, None, :] < dims_right[:, None, None]
    )
    masked = jnp.where(keep, core_full, jnp.zeros((), core_full.dtype))
    left_onehot = (pair_left[:, None] == jnp.arange(nb_local)[None, :]).astype(jnp.bfloat16)
    own_coeffs = lax.dynamic_index_in_dim(mpo_coeffs, term_index, 1, keepdims=False)
    piece = lax.all_gather(env_blocks, "term", axis=0, tiled=True)
    count = piece.shape[0]
    weights = own_coeffs[:, :, None] * left_onehot[None, :, :]
    flat = piece.reshape(count, nb_local, blk * blk)
    summed_terms = jnp.einsum("wpi,wix->px", weights, flat, preferred_element_type=jnp.float32)
    mixed = summed_terms.astype(jnp.bfloat16).reshape(pairs_local, blk, blk)
    half = jnp.einsum("prc,pcd->prd", mixed, masked, preferred_element_type=jnp.float32).astype(
        jnp.bfloat16
    )
    pair_terms = jnp.einsum("prc,prd->pcd", masked, half, preferred_element_type=jnp.float32)
    pair_terms = pair_terms.reshape(pairs_local, blk * blk)
    right_onehot = right_match.astype(jnp.float32)
    owned = lax.psum_scatter(
        jnp.dot(
            right_onehot.T,
            pair_terms,
            precision=lax.Precision.HIGHEST,
            preferred_element_type=jnp.float32,
        ),
        "sec",
        scatter_dimension=0,
        tiled=True,
    )
    return owned.reshape(1, nb_local, blk, blk)


def solution(mesh):
    return jax.shard_map(
        per_device,
        mesh=mesh,
        in_specs=(
            P("term", "sec", None, None),
            P("sec", "term", None),
            P(None, None, "sec"),
            P("sec"),
            P("sec"),
            P(),
        ),
        out_specs=P("term", "sec", None, None),
        check_vma=False,
    )
```

profile of v0, /device:TPU:1, one launch (start us, length us, event | category | flops | bytes accessed | tf_op | source)
XLA Modules:
  0.0 287.1 jit_solution(74491955640020038)
XLA Ops:
  6.5 0.0 copy-start
  6.5 0.7 all-gather.5.cloned.1.call-update
  7.3 0.0 all-gather.3.cloned.1.call-start
  7.3 0.7 all-gather.3.cloned.1.call-update
  8.0 0.0 all-reduce.3.cloned.1.call-start
  8.1 0.7 broadcast_add_fusion
  8.8 0.8 select_reduce_fusion.1
  9.5 0.7 compare_convert_fusion
  10.2 0.1 iota_compare_fusion
  10.3 49.5 %all-gather.5.cloned.1.call-done = bf16[8,2,256,256]{3,2,1,0:T(8,128)(2,1)} async-done(((bf16[1,2,256,256]{3,2,1,0:T(8,128)(2,1)}), bf16[8,2,256,256]{3,2,1,0:T(8,128)(2,1)}) %all-gather.5.cloned.1.call-update) | async-done | bytes 2097168 | tf_op jit(solution)/shard_map/all_gather | solution.py:29
  59.8 2.8 copy.16
  62.6 5.6 %fusion = bf16[64,65536]{1,0:T(8,128)(2,1)} fusion(bf16[8,2,65536]{2,0,1:T(8,128)(2,1)S(1)} %bitcast.30, bf16[64,2]{0,1:T(2,128)(2,1)S(1)} %compare_convert_fusion, bf16[8,64]{1,0:T(8,128)(2,1)S(1)} %bitcast.32), kind=kOutput, calls=%fused_computation.1 | convolution fusion | flops 138413056 | bytes 10487040 | tf_op jit(solution)/shard_map/wpi,wix->px/dot_general | solution.py:33
  68.1 9.6 %copy.20 = bf16[8,8,256,256]{3,2,1,0:T(8,128)(2,1)} copy(bf16[8,8,256,256]{3,1,2,0:T(8,128)(2,1)} %bitcast.28) | data formatting | bytes 16777216
  77.8 108.3 %all-gather.3.cloned.1.call-done = bf16[64,256,256]{2,1,0:T(8,128)(2,1)} async-done(((bf16[64,32,256]{2,1,0:T(8,128)(2,1)}), bf16[64,256,256]{2,1,0:T(8,128)(2,1)}) %all-gather.3.cloned.1.call-update) | async-done | bytes 8388624 | tf_op jit(solution)/shard_map/all_gather | solution.py:14
  186.1 11.1 %fusion.28 = bf16[64,256,256]{2,1,0:T(8,128)(2,1)} fusion(bf16[64,256,256]{2,1,0:T(8,128)(2,1)} %bitcast.29, bf16[64,256,256]{2,1,0:T(8,128)(2,1)} %all-gather.3.cloned.1.call-done, pred[64,256]{1,0:T(8,128)(4,1)S(1)} %get-tuple-element.7, pred[64,256]{1,0:T(8,128)(4,1)S(1)} %get-tuple-element.8), kind=kOutput, calls=%fused_computation.4.clone.2 | convolution fusion | flops 2160066560 | bytes 25198592 | tf_op jit(solution)/shard_map/prc,pcd->prd/dot_general | solution.py:35
  197.2 8.9 %fusion.1 = f32[64,256,256]{2,1,0:T(8,128)S(1)} fusion(bf16[64,256,256]{2,1,0:T(8,128)(2,1)} %all-gather.3.cloned.1.call-done, pred[64,256]{1,0:T(8,128)(4,1)S(1)} %get-tuple-element.7, pred[64,256]{1,0:T(8,128)(4,1)S(1)} %get-tuple-element.8, bf16[64,256,256]{2,1,0:T(8,128)(2,1)} %fusion.28), kind=kOutput, calls=%fused_computation.3 | convolution fusion | flops 2155872256 | bytes 33587200 | tf_op jit(solution)/shard_map/prc,prd->pcd/dot_general | solution.py:38
  206.1 0.0 copy-start.2
  206.1 11.7 %copy.21 = f32[8,8,256,256]{3,1,2,0:T(8,128)} copy(f32[8,8,256,256]{3,2,1,0:T(8,128)S(1)} %bitcast.26) | data formatting | bytes 33554432
  217.8 10.0 %fusion.12 = f32[8,65536]{1,0:T(8,128)} fusion(f32[64,65536]{1,0:T(8,128)} %bitcast.27, s32[64]{0:T(128)S(1)} %copy-done.2), kind=kOutput, calls=%fused_computation.17 | convolution fusion | flops 402653696 | bytes 18874624 | tf_op jit(solution)/shard_map/dot_general | solution.py:42
  227.9 0.0 all-reduce.3.cloned.1.call-update
  227.9 0.6 dynamic-slice
  229.1 48.8 %all-reduce.3.cloned.1.call-done = f32[8,65536]{1,0:T(8,128)} async-done(((f32[8,65536]{1,0:T(8,128)}), f32[8,65536]{1,0:T(8,128)}) %all-reduce.3.cloned.1.call-update) | async-done | bytes 2097168
  277.9 1.8 constant_dynamic-slice_fusion
  279.7 0.8 copy.25
  (9 shorter events, 0.0 us)
Async XLA Ops:
  6.5 1.5 copy-start
  6.5 53.2 %all-gather.5.cloned.1.call-start = ((), (), s32[]{:S(2)}) async-start(), calls=%async_computation.1 | async-start | bytes 2359296 | tf_op jit(solution)/shard_map/all_gather | solution.py:29
  7.3 178.8 %all-gather.3.cloned.1.call-start = ((), (), s32[]{:S(2)}) async-start(), calls=%async_computation | async-start | bytes 9437184 | tf_op jit(solution)/shard_map/all_gather | solution.py:14
  8.0 269.9 %all-reduce.3.cloned.1.call-start = ((), (), s32[]{:S(2)}) async-start(), calls=%async_computation.2 | async-start | bytes 4194304
  206.1 11.7 %copy-start.2 = (s32[64]{0:T(128)S(1)}, s32[64]{0:T(128)}, u32[]{:S(2)}) copy-start(s32[64]{0:T(128)} %param.10) | copy-start | bytes 772
  217.8 62.7 %copy-start.1 = (bf16[8,8,64]{2,1,0:T(8,128)(2,1)S(1)}, bf16[8,8,64]{2,1,0:T(8,128)(2,1)}, u32[]{:S(2)}) copy-start(bf16[8,8,64]{2,1,0:T(8,128)(2,1)} %param.8) | copy-start | bytes 24580
  217.8 10.1 %copy-start.3 = (u32[32]{0:T(128)S(1)}, u32[32]{0:T(128)}, u32[]{:S(2)}) copy-start(u32[32]{0:T(128)} %constant.22) | copy-start | bytes 388
Sparse Core Ops, SparseCore 0:
  9.5 50.2 all-gather.4
  62.0 124.0 all-gather.2
  228.0 49.8 all-reduce.2
where the time goes:
time: 288 us; the launch traced here: 287 us
  waiting for transfers between devices  208 us (72%)
  matrix products  35.6 us (12%)
  local copies, waits for them, and re-layouts  27.3 us (9%)
  between operations  13.8 us (5%)
    all_gather x1, waiting for transfers between devices, per_device(): core_full = lax.all_gather(core_blocks, 'term', axis=1, tiled=True)  108 us
    unnamed x4, waiting for transfers between devices  50.2 us
    all_gather x1, waiting for transfers between devices, per_device(): piece = lax.all_gather(env_blocks, 'term', axis=0, tiled=True)  49.5 us
    unnamed x14, local copies, waits for them, and re-layouts  24.6 us
    dot_general x1, matrix products, per_device(): jnp.einsum('prc,pcd->prd', mixed, masked, preferred_element_type=jnp.floa...  11.1 us
    dot_general x1, matrix products, per_device(): jnp.dot(right_onehot.T, pair_terms, precision=lax.Precision.HIGHEST, pref...  10 us
    dot_general x1, matrix products, per_device(): jnp.einsum('prc,prd->pcd', masked, half, preferred_element_type=jnp.float32)  8.87 us
  transfers between devices with their start and end apart: 3, of which 3 were waited for; matrix products, arithmetic and copies ran while one was open for 7% of the time, Pallas kernels for 0%

commit v1 on v0

v1 whole, which is shorter than its diff:
```python
import functools

import jax
import jax.numpy as jnp
from jax import lax
from jax.experimental import pallas as pl
from jax.experimental.pallas import tpu as pltpu
from jax.sharding import PartitionSpec as P

BF16, F32 = jnp.bfloat16, jnp.float32
TILE = 16


def pair_kernel(plan, pieces, groups, slots, *refs):
    place, info, mix = refs[:3]
    piece_refs = refs[3 : 3 + pieces]
    keep_ref = refs[3 + pieces]
    send_refs = refs[4 + pieces : 4 + pieces + groups - 1]
    core, env, mixed, total, sems = refs[4 + pieces + groups - 1 :]
    pairs, blk = core.shape[0], core.shape[1]
    env_copies, core_copies = [], []
    sem = 0
    for n, (core_first, core_count, env_first, env_count) in enumerate(plan):
        ref = piece_refs[n]
        rows = ref.shape[1]
        if env_count:
            for part in range(rows // TILE):
                at = pl.multiple_of(place[2, n] * TILE, TILE)
                copy = pltpu.make_async_copy(
                    ref.at[pl.ds(env_first, env_count), pl.ds(part * TILE, TILE), :],
                    env.at[:, part, pl.ds(at, TILE), :],
                    sems.at[sem],
                )
                sem += 1
                copy.start()
                env_copies.append(copy)
    for n, (core_first, core_count, env_first, env_count) in enumerate(plan):
        ref = piece_refs[n]
        rows = ref.shape[1]
        if core_count:
            at = pl.multiple_of(place[0, n], rows)
            copy = pltpu.make_async_copy(
                ref.at[pl.ds(core_first, core_count), :, :],
                core.at[pl.ds(place[1, n], core_count), pl.ds(at, rows), :],
                sems.at[sem],
            )
            sem += 1
            copy.start()
            core_copies.append(copy)
    total[...] = jnp.zeros_like(total)
    for copy in env_copies:
        copy.wait()
    parts = env.shape[1]

    def mix_rows(step, carry):
        rows = jnp.dot(mix[...], env[step // parts, step % parts], preferred_element_type=F32)
        at = pl.multiple_of(step * TILE, TILE)
        mixed[:, pl.ds(at, TILE), :] = rows.astype(BF16).reshape(pairs, TILE, blk)
        return carry

    lax.fori_loop(0, blk // TILE, mix_rows, 0, unroll=2)
    for copy in core_copies:
        copy.wait()
    row = lax.broadcasted_iota(jnp.int32, (blk, blk), 0)
    col = lax.broadcasted_iota(jnp.int32, (blk, blk), 1)

    def one_pair(p, carry):
        keep = (row < info[0, p]) & (col < info[1, p])
        masked = jnp.where(keep, core[p].astype(F32), 0.0).astype(BF16)
        half = jnp.dot(mixed[p], masked, preferred_element_type=F32).astype(BF16)
        term = lax.dot_general(
            masked, half, (((0,), (0,)), ((), ())), preferred_element_type=F32
        )
        total[info[2, p]] += term
        return carry

    lax.fori_loop(0, pairs, one_pair, 0, unroll=4)
    keep_ref[...] = total[:slots]
    for f, ref in enumerate(send_refs):
        ref[...] = total[(f + 1) * slots : (f + 2) * slots].astype(BF16)


def pair_sums(plan, place, info, mix, pieces, groups, slots, env_rows):
    pairs = info.shape[1]
    blk = pieces[0].shape[2]
    rows = pieces[0].shape[1]
    copies = sum((1 if c[1] else 0) + (rows // TILE if c[3] else 0) for c in plan)
    smem = pl.BlockSpec(memory_space=pltpu.SMEM)
    vmem = pl.BlockSpec(memory_space=pltpu.VMEM)
    hbm = pl.BlockSpec(memory_space=pl.ANY)
    macs = 3 * pairs * blk * blk * blk
    return pl.pallas_call(
        functools.partial(pair_kernel, plan, len(pieces), groups, slots),
        out_shape=[jax.ShapeDtypeStruct((slots, blk, blk), F32)]
        + [jax.ShapeDtypeStruct((slots, blk, blk), BF16)] * (groups - 1),
        in_specs=[smem, smem, vmem] + [hbm] * len(pieces),
        out_specs=[vmem] * groups,
        scratch_shapes=[
            pltpu.VMEM((pairs, blk, blk), BF16),
            pltpu.VMEM((blk // rows, rows // TILE, env_rows * TILE, blk), BF16),
            pltpu.VMEM((pairs, blk, blk), BF16),
            pltpu.VMEM((groups * slots, blk, blk), F32),
            pltpu.SemaphoreType.DMA((copies,)),
        ],
        compiler_params=pltpu.CompilerParams(vmem_limit_bytes=48 << 20),
        cost_estimate=pl.CostEstimate(flops=2 * macs, bytes_accessed=8 << 20, transcendentals=0),
        name="pair_sums",
    )(place, info, mix, *pieces)


def per_device(secs, terms, env_blocks, core_blocks, mpo_coeffs, pair_left, pair_right, block_dims):
    nx, nz = secs // 2, terms // 2
    half_z = nz // 2
    nb, blk = env_blocks.shape[1], env_blocks.shape[2]
    pairs_local, rows = core_blocks.shape[0], core_blocks.shape[1]
    piece_pairs = pairs_local // nz
    own_nb = nb // 2
    sec, term = lax.axis_index("sec"), lax.axis_index("term")
    x, c, z, y = sec // 2, sec % 2, term // 2, term % 2
    top, rest = z // half_z, z % half_z

    def send(value, to):
        perm = []
        for s in range(secs):
            for t in range(terms):
                d = to(s // 2, s % 2, t // 2, t % 2)
                if d is not None:
                    perm.append((s * terms + t, (d[0] * 2 + d[1]) * terms + d[2] * 2 + d[3]))
        return lax.ppermute(value, ("sec", "term"), perm)

    def other_core(value):
        return send(value, lambda x, c, z, y: (x, 1 - c, z, y))

    facts = jnp.concatenate(
        [
            mpo_coeffs.reshape(-1, pairs_local).astype(F32),
            pair_left[None].astype(F32),
            pair_right[None].astype(F32),
        ]
    )
    facts = jnp.where(c == top, facts, other_core(facts))
    facts = lax.dynamic_slice_in_dim(facts, rest * 2 * piece_pairs, 2 * piece_pairs, 1)
    left, right = facts[-2].astype(jnp.int32), facts[-1].astype(jnp.int32)
    coeffs = facts[:-2].reshape(mpo_coeffs.shape[0], mpo_coeffs.shape[1], -1).astype(BF16)
    left_block = (x * 2 + top) * nb + left
    ids = jnp.arange(block_dims.shape[0])
    dims_left = jnp.sum(jnp.where(left_block[:, None] == ids, block_dims, 0), axis=1)
    dims_right = jnp.sum(jnp.where(right[:, None] == ids, block_dims, 0), axis=1)
    slots = 2 * nb
    slot = ((right // slots) ^ x) * slots + right % slots
    info = jnp.stack([dims_left, dims_right, slot])

    blocks = env_blocks[0].reshape(2, own_nb * (blk // rows), rows, blk)
    pieces, places = [], []
    zm = []
    for m in range(nz):
        g = z ^ m
        own = lax.dynamic_slice_in_dim(core_blocks, g * piece_pairs, piece_pairs, 0)
        message = jnp.concatenate([own, lax.dynamic_index_in_dim(blocks, g % 2, 0, keepdims=False)])
        zm.append(
            send(
                message,
                lambda x, c, z, y, m=m: (x, (z ^ m) % 2, c * half_z + (z ^ m) // 2, y),
            )
        )
    for m in range(nz):
        ym = send(zm[m], lambda x, c, z, y: (x, c, z, 1 - y))
        for k, got in ((c, (zm[m], ym)), (1 - c, (other_core(zm[m]), other_core(ym)))):
            from_z = (2 * rest + k) ^ m
            for from_y, value in zip((y, 1 - y), got):
                pieces.append(value)
                from_term = 2 * from_z + from_y
                places.append((from_term * rows, k * piece_pairs, from_term * nb + k * own_nb))
    place = jnp.stack([jnp.stack(p) for p in zip(*places)])
    env_rows = mpo_coeffs.shape[0] * nb
    if rows % TILE == 0 and own_nb == 1:
        plan = [(0, piece_pairs, piece_pairs, blk // rows)] * len(pieces)
    else:
        cores = jnp.zeros((2 * piece_pairs, blk, blk), BF16)
        envs = jnp.zeros((env_rows, blk, blk), BF16)
        for value, (at, first, which) in zip(pieces, places):
            cores = lax.dynamic_update_slice(cores, value[:piece_pairs], (first, at, 0))
            envs = lax.dynamic_update_slice(
                envs, value[piece_pairs:].reshape(own_nb, blk, blk), (which, 0, 0)
            )
        pieces = [cores] + [envs[n : n + 1] for n in range(env_rows)]
        plan = [(0, 2 * piece_pairs, 0, 0)] + [(0, 0, 0, 1)] * env_rows
        zero = jnp.zeros((1 + env_rows,), jnp.int32)
        place = jnp.stack([zero, zero, jnp.maximum(jnp.arange(1 + env_rows) - 1, 0)])

    onehot = (left[:, None] == jnp.arange(nb)).astype(BF16)
    eye = jnp.eye(TILE, dtype=BF16)

    def partial_sums(e):
        v = 2 * (c * half_z + (rest ^ e)) + y
        own = lax.dynamic_index_in_dim(coeffs, v, 1, keepdims=False)
        weights = own.T[:, :, None] * onehot[:, None, :]
        mix = weights.reshape(-1, 1, env_rows, 1) * eye[None, :, None, :]
        mix = mix.reshape(-1, env_rows * TILE)
        return pair_sums(plan, place, info, mix, pieces, nx, slots, env_rows)

    sums = {}
    for e in reversed(range(half_z)):
        keep, *away = partial_sums(e)
        for f, value in enumerate(away):
            keep = keep + send(value, lambda x, c, z, y, f=f: (x ^ (f + 1), c, z, y)).astype(F32)
        sums[e] = keep
    bit = 1
    while bit < half_z:
        for e in [e for e in sums if e & bit]:
            got = send(sums.pop(e).astype(BF16), lambda x, c, z, y: (x, c, z ^ bit, y))
            sums[e ^ bit] = sums[e ^ bit] + got.astype(F32)
        bit *= 2
    own = sums[0].reshape(2, nb, blk, blk)
    same = lax.dynamic_index_in_dim(own, c, 0, keepdims=False)
    other = lax.dynamic_index_in_dim(own, 1 - c, 0, keepdims=False)
    same16, other16 = same.astype(BF16), other.astype(BF16)

    def over_z(flip):
        def to(x, c, z, y):
            return (x, c ^ flip, z ^ half_z, y) if c != z // half_z else None

        return to

    got = send(same16, over_z(0)).astype(F32) + send(other16, over_z(1)).astype(F32)
    near = send(other16, lambda x, c, z, y: (x, 1 - c, z, y) if c == z // half_z else None)
    result = jnp.where(c == top, same, near.astype(F32)) + got
    return result[None]


def solution(mesh):
    return jax.shard_map(
        functools.partial(per_device, mesh.shape["sec"], mesh.shape["term"]),
        mesh=mesh,
        in_specs=(
            P("term", "sec", None, None),
            P("sec", "term", None),
            P(None, None, "sec"),
            P("sec"),
            P("sec"),
            P(),
        ),
        out_specs=P("term", "sec", None, None),
        check_vma=False,
    )
```

time: 288 us -> 126 us (0.44)
  the two profiles are of different devices: /device:TPU:1 before, /device:TPU:0 now
where the time goes in v1:
time: 126 us
  waiting for transfers between devices  45.5 us (36%)
  starting transfers between devices  40.1 us (32%)
  Pallas kernels  22.6 us (18%)
  local copies, waits for them, and re-layouts  9.36 us (7%)
  other arithmetic  7.47 us (6%)
    ppermute x23, waiting for transfers between devices, send(): return lax.ppermute(value, ('sec', 'term'), perm)  45.5 us
    ppermute x23, starting transfers between devices, send(): return lax.ppermute(value, ('sec', 'term'), perm)  40.1 us
    pallas_call x2, Pallas kernels, pair_sums(): pl.pallas_call(functools.partial(pair_kernel, plan, len(pieces), groups,...  22.6 us
    mul x2, local copies, waits for them, and re-layouts, partial_sums(): mix = weights.reshape(-1, 1, env_rows, 1) * eye[None, :, None, :]  6.38 us
  transfers between devices with their start and end apart: 23, of which 6 were waited for; matrix products, arithmetic and copies ran while one was open for 11% of the time, Pallas kernels for 9%

profile of v1, /device:TPU:0, one launch (start us, length us, event | category | flops | bytes accessed | tf_op | source)
XLA Modules:
  0.0 125.5 jit_solution(15559481881942611440)
XLA Ops:
  3.1 1.3 %constant_dynamic-slice_fusion.1 = (bf16[16,32,256]{2,1,0:T(8,128)(2,1)S(1)}, bf16[16,32,256]{2,1,0:T(8,128)(2,1)S(1)}, bf16[16,32,256]{2,1,0:T(8,128)(2,1)S(1)}, bf16[16,32,256]{2,1,0:T(8,128)(2,1)S(1)}) fusion(bf16[64,32,256]{2,1,0:T(8,128)(2,1)} %param.7, s32[]{:T(128)S(6)} %select_n.140, s32[]{:T(128)S(6)} %select_n.134, s32[]{:T(128)S(6)} %select_n.132, ...), kind=kLoop, calls=%fused_computation.30 | loop fusion | bytes 2097168 | tf_op jit(solution)/shard_map/dynamic_slice | solution.py:158
  5.1 5.1 %collective-permute-start.5 = (bf16[24,32,256]{2,1,0:T(8,128)(2,1)S(1)}, bf16[24,32,256]{2,1,0:T(8,128)(2,1)S(1)}, u32[]{:S(2)}, u32[]{:S(2)}) collective-permute-start(bf16[24,32,256]{2,1,0:T(8,128)(2,1)S(1)} %pad_maximum_fusion.1), channel_id=1, source_target_pairs={{0,8},{1,9},{2,0},{3,1},{4,10},{5,11},{6,2},{7,3},{8,12},{9,13},{1... | collective-permute-start | bytes 1179656 | tf_op jit(solution)/shard_map/ppermute | solution.py:129
  10.4 3.5 %collective-permute-start.13 = (bf16[24,32,256]{2,1,0:T(8,128)(2,1)S(1)}, bf16[24,32,256]{2,1,0:T(8,128)(2,1)S(1)}, u32[]{:S(2)}, u32[]{:S(2)}) collective-permute-start(bf16[24,32,256]{2,1,0:T(8,128)(2,1)S(1)} %pad_maximum_fusion.3), channel_id=1, source_target_pairs={{0,10},{1,11},{2,2},{3,3},{4,8},{5,9},{6,0},{7,1},{8,14},{9,15},{1... | collective-permute-start | bytes 1179656 | tf_op jit(solution)/shard_map/ppermute | solution.py:129
  15.1 1.5 %collective-permute-start.2 = (bf16[24,32,256]{2,1,0:T(8,128)(2,1)S(1)}, bf16[24,32,256]{2,1,0:T(8,128)(2,1)S(1)}, u32[]{:S(2)}, u32[]{:S(2)}) collective-permute-start(bf16[24,32,256]{2,1,0:T(8,128)(2,1)S(1)} %collective-permute-done.1.refs_3_), channel_id=1, source_target_pairs={{0,1},{1,0},{2,3},{3,2},{4,5},{5,4},{6,7},{7,6},{8,9},{9,8},{10,11... | collective-permute-start | bytes 1179656 | tf_op jit(solution)/shard_map/ppermute | solution.py:129
  16.6 2.7 %collective-permute-start.3 = (bf16[24,32,256]{2,1,0:T(8,128)(2,1)S(1)}, bf16[24,32,256]{2,1,0:T(8,128)(2,1)S(1)}, u32[]{:S(2)}, u32[]{:S(2)}) collective-permute-start(bf16[24,32,256]{2,1,0:T(8,128)(2,1)S(1)} %collective-permute-done.1.refs_3_), channel_id=1, source_target_pairs={{0,8},{1,9},{2,10},{3,11},{4,12},{5,13},{6,14},{7,15},{8,0},{9,1},... | collective-permute-start | bytes 1179656 | tf_op jit(solution)/shard_map/ppermute | solution.py:129
  19.4 1.5 %collective-permute-start.6 = (bf16[24,32,256]{2,1,0:T(8,128)(2,1)S(1)}, bf16[24,32,256]{2,1,0:T(8,128)(2,1)S(1)}, u32[]{:S(2)}, u32[]{:S(2)}) collective-permute-start(bf16[24,32,256]{2,1,0:T(8,128)(2,1)S(1)} %collective-permute-done.5.refs_7_), channel_id=1, source_target_pairs={{0,1},{1,0},{2,3},{3,2},{4,5},{5,4},{6,7},{7,6},{8,9},{9,8},{10,11... | collective-permute-start | bytes 1179656 | tf_op jit(solution)/shard_map/ppermute | solution.py:129
  20.9 20.6 %collective-permute-done.9.refs_11_ = bf16[24,32,256]{2,1,0:T(8,128)(2,1)S(1)} collective-permute-done((bf16[24,32,256]{2,1,0:T(8,128)(2,1)S(1)}, bf16[24,32,256]{2,1,0:T(8,128)(2,1)S(1)}, u32[]{:S(2)}, u32[]{:S(2)}) %collective-permute-start.9) | collective-permute-done | bytes 393248 | tf_op jit(solution)/shard_map/ppermute | solution.py:129
  41.5 1.5 %collective-permute-start.10 = (bf16[24,32,256]{2,1,0:T(8,128)(2,1)S(1)}, bf16[24,32,256]{2,1,0:T(8,128)(2,1)}, u32[]{:S(2)}, u32[]{:S(2)}) collective-permute-start(bf16[24,32,256]{2,1,0:T(8,128)(2,1)S(1)} %collective-permute-done.9.refs_11_), channel_id=1, source_target_pairs={{0,1},{1,0},{2,3},{3,2},{4,5},{5,4},{6,7},{7,6},{8,9},{9,8},{10,11... | collective-permute-start | bytes 1179656 | tf_op jit(solution)/shard_map/ppermute | solution.py:129
  43.0 3.7 %collective-permute-start.11 = (bf16[24,32,256]{2,1,0:T(8,128)(2,1)S(1)}, bf16[24,32,256]{2,1,0:T(8,128)(2,1)}, u32[]{:S(2)}, u32[]{:S(2)}) collective-permute-start(bf16[24,32,256]{2,1,0:T(8,128)(2,1)S(1)} %collective-permute-done.9.refs_11_), channel_id=1, source_target_pairs={{0,8},{1,9},{2,10},{3,11},{4,12},{5,13},{6,14},{7,15},{8,0},{9,1},... | collective-permute-start | bytes 1179656 | tf_op jit(solution)/shard_map/ppermute | solution.py:129
  47.5 2.3 %broadcast_multiply_fusion.1 = (bf16[32,16,16,16]{3,2,1,0:T(8,128)(2,1)}, bf16[32,16,16,16]{3,2,1,0:T(8,128)(2,1)}) fusion(bf16[16,16]{1,0:T(8,128)(2,1)S(1)} %fusion.4, bf16[32,16]{1,0:T(8,128)(2,1)S(1)} %copy.12, bf16[32,16]{1,0:T(8,128)(2,1)S(1)} %copy.14), kind=kLoop, calls=%fused_computation.3 | loop fusion | flops 262144 | bytes 526848 | tf_op jit(solution)/shard_map/mul | solution.py:198
  50.5 6.4 %collective-permute-start.8 = (bf16[24,32,256]{2,1,0:T(8,128)(2,1)S(1)}, bf16[24,32,256]{2,1,0:T(8,128)(2,1)}, u32[]{:S(2)}, u32[]{:S(2)}) collective-permute-start(bf16[24,32,256]{2,1,0:T(8,128)(2,1)S(1)} %collective-permute-done.6.refs_8_), channel_id=1, source_target_pairs={{0,8},{1,9},{2,10},{3,11},{4,12},{5,13},{6,14},{7,15},{8,0},{9,1},... | collective-permute-start | bytes 1179656 | tf_op jit(solution)/shard_map/ppermute | solution.py:129
  56.8 2.1 %collective-permute-done.14.refs_16_ = bf16[24,32,256]{2,1,0:T(8,128)(2,1)} collective-permute-done((bf16[24,32,256]{2,1,0:T(8,128)(2,1)S(1)}, bf16[24,32,256]{2,1,0:T(8,128)(2,1)}, u32[]{:S(2)}, u32[]{:S(2)}) %collective-permute-start.14) | collective-permute-done | bytes 393248 | tf_op jit(solution)/shard_map/ppermute | solution.py:129
  58.9 2.9 %collective-permute-start.16 = (bf16[24,32,256]{2,1,0:T(8,128)(2,1)}, bf16[24,32,256]{2,1,0:T(8,128)(2,1)}, u32[]{:S(2)}, u32[]{:S(2)}) collective-permute-start(bf16[24,32,256]{2,1,0:T(8,128)(2,1)} %collective-permute-done.14.refs_16_), channel_id=1, source_target_pairs={{0,8},{1,9},{2,10},{3,11},{4,12},{5,13},{6,14},{7,15},{8,0},{9,1},... | collective-permute-start | bytes 1179656 | tf_op jit(solution)/shard_map/ppermute | solution.py:129
  61.9 3.2 %mul.334.refs_2_ = bf16[512,256]{1,0:T(8,128)(2,1)S(1)} reshape(bf16[32,16,16,16]{3,2,1,0:T(8,128)(2,1)} %get-tuple-element.30) | data formatting | bytes 524288 | tf_op jit(solution)/shard_map/mul | solution.py:198
  65.9 11.3 %pair_sums.3 = (f32[4,256,256]{2,1,0:T(8,128)}, bf16[4,256,256]{2,1,0:T(8,128)(2,1)}) custom-call(s32[3,16]{1,0:T(4,128)S(1)} %pad_add_fusion.refs_0_, s32[3,32]{1,0:T(4,128)S(1)} %pad_add_fusion.1.refs_1_, bf16[512,256]{1,0:T(8,128)(2,1)S(1)} %mul.334.refs_2_, bf16[24,32,256]{2,1,0:T(8,128)(2,1)S(1)} %collective-permute-done.1.refs_3_, ...), custom_call_target="tpu_custom_call" | custom-call | flops 3221225472 | bytes 8388608 | tf_op jit(solution)/shard_map/pair_sums/pallas_call | solution.py:92
  77.2 1.6 %collective-permute-start.18 = (bf16[4,256,256]{2,1,0:T(8,128)(2,1)}, bf16[4,256,256]{2,1,0:T(8,128)(2,1)}, u32[]{:S(2)}, u32[]{:S(2)}) collective-permute-start(bf16[4,256,256]{2,1,0:T(8,128)(2,1)} %get-tuple-element.12), channel_id=1, source_target_pairs={{0,16},{1,17},{2,18},{3,19},{4,20},{5,21},{6,22},{7,23},{8,24},{9,... | collective-permute-start | bytes 1572872 | tf_op jit(solution)/shard_map/ppermute | solution.py:129
  78.7 3.2 %mul.323.refs_2_ = bf16[512,256]{1,0:T(8,128)(2,1)S(1)} reshape(bf16[32,16,16,16]{3,2,1,0:T(8,128)(2,1)} %get-tuple-element.29) | data formatting | bytes 524288 | tf_op jit(solution)/shard_map/mul | solution.py:198
  81.9 11.3 %pair_sums.2 = (f32[4,256,256]{2,1,0:T(8,128)}, bf16[4,256,256]{2,1,0:T(8,128)(2,1)}) custom-call(s32[3,16]{1,0:T(4,128)S(1)} %pad_add_fusion.refs_0_, s32[3,32]{1,0:T(4,128)S(1)} %pad_add_fusion.1.refs_1_, bf16[512,256]{1,0:T(8,128)(2,1)S(1)} %mul.323.refs_2_, bf16[24,32,256]{2,1,0:T(8,128)(2,1)S(1)} %collective-permute-done.1.refs_3_, ...), custom_call_target="tpu_custom_call" | custom-call | flops 3221225472 | bytes 8388608 | tf_op jit(solution)/shard_map/pair_sums/pallas_call | solution.py:92
  93.8 1.2 add_convert_fusion
  95.1 12.0 %collective-permute-done.17 = bf16[4,256,256]{2,1,0:T(8,128)(2,1)S(1)} collective-permute-done((bf16[4,256,256]{2,1,0:T(8,128)(2,1)}, bf16[4,256,256]{2,1,0:T(8,128)(2,1)S(1)}, u32[]{:S(2)}, u32[]{:S(2)}) %collective-permute-start.17) | collective-permute-done | bytes 524320 | tf_op jit(solution)/shard_map/ppermute | solution.py:129
  107.1 1.3 %collective-permute-done.19 = bf16[4,256,256]{2,1,0:T(8,128)(2,1)S(1)} collective-permute-done((bf16[4,256,256]{2,1,0:T(8,128)(2,1)S(1)}, bf16[4,256,256]{2,1,0:T(8,128)(2,1)S(1)}, u32[]{:S(2)}, u32[]{:S(2)}) %collective-permute-start.19) | collective-permute-done | bytes 524320 | tf_op jit(solution)/shard_map/ppermute | solution.py:129
  109.3 1.3 %collective-permute-start.21 = (bf16[2,256,256]{2,1,0:T(8,128)(2,1)S(1)}, bf16[2,256,256]{2,1,0:T(8,128)(2,1)S(1)}, u32[]{:S(2)}, u32[]{:S(2)}) collective-permute-start(bf16[2,256,256]{2,1,0:T(8,128)(2,1)S(1)} %get-tuple-element.15), channel_id=1, source_target_pairs={{4,0},{5,1},{6,2},{7,3},{8,12},{9,13},{10,14},{11,15},{20,16},{21,... | collective-permute-start | bytes 786440 | tf_op jit(solution)/shard_map/ppermute | solution.py:129
  110.6 4.7 %collective-permute-start.20 = (bf16[2,256,256]{2,1,0:T(8,128)(2,1)S(1)}, bf16[2,256,256]{2,1,0:T(8,128)(2,1)S(1)}, u32[]{:S(2)}, u32[]{:S(2)}) collective-permute-start(bf16[2,256,256]{2,1,0:T(8,128)(2,1)S(1)} %get-tuple-element.16), channel_id=1, source_target_pairs={{0,8},{1,9},{2,10},{3,11},{12,4},{13,5},{14,6},{15,7},{16,24},{17,... | collective-permute-start | bytes 786440 | tf_op jit(solution)/shard_map/ppermute | solution.py:129
  115.2 9.4 %collective-permute-done.21 = bf16[2,256,256]{2,1,0:T(8,128)(2,1)S(1)} collective-permute-done((bf16[2,256,256]{2,1,0:T(8,128)(2,1)S(1)}, bf16[2,256,256]{2,1,0:T(8,128)(2,1)S(1)}, u32[]{:S(2)}, u32[]{:S(2)}) %collective-permute-start.21) | collective-permute-done | bytes 262176 | tf_op jit(solution)/shard_map/ppermute | solution.py:129
  (69 shorter events, 9.6 us)
Async XLA Ops:
  1.4 13.0 %collective-permute-start = (f32[66,64]{1,0:T(8,128)S(1)}, f32[66,64]{1,0:T(8,128)S(1)}, u32[]{:S(2)}, u32[]{:S(2)}) collective-permute-start(f32[66,64]{1,0:T(8,128)S(1)} %pad_maximum_fusion.4), channel_id=1, source_target_pairs={{0,8},{1,9},{2,10},{3,11},{4,12},{5,13},{6,14},{7,15},{8,0},{9,1},... | collective-permute-start | bytes 50696 | tf_op jit(solution)/shard_map/ppermute | solution.py:129
  4.4 10.7 %collective-permute-start.1 = (bf16[24,32,256]{2,1,0:T(8,128)(2,1)S(1)}, bf16[24,32,256]{2,1,0:T(8,128)(2,1)S(1)}, u32[]{:S(2)}, u32[]{:S(2)}) collective-permute-start(bf16[24,32,256]{2,1,0:T(8,128)(2,1)S(1)} %pad_maximum_fusion), channel_id=1, source_target_pairs={{0,0},{1,1},{2,8},{3,9},{4,2},{5,3},{6,10},{7,11},{8,4},{9,5},{10,... | collective-permute-start | bytes 1179656 | tf_op jit(solution)/shard_map/ppermute | solution.py:129
  5.1 14.3 %collective-permute-start.5 = (bf16[24,32,256]{2,1,0:T(8,128)(2,1)S(1)}, bf16[24,32,256]{2,1,0:T(8,128)(2,1)S(1)}, u32[]{:S(2)}, u32[]{:S(2)}) collective-permute-start(bf16[24,32,256]{2,1,0:T(8,128)(2,1)S(1)} %pad_maximum_fusion.1), channel_id=1, source_target_pairs={{0,8},{1,9},{2,0},{3,1},{4,10},{5,11},{6,2},{7,3},{8,12},{9,13},{1... | collective-permute-start | bytes 1179656 | tf_op jit(solution)/shard_map/ppermute | solution.py:129
  10.3 31.2 %collective-permute-start.9 = (bf16[24,32,256]{2,1,0:T(8,128)(2,1)S(1)}, bf16[24,32,256]{2,1,0:T(8,128)(2,1)S(1)}, u32[]{:S(2)}, u32[]{:S(2)}) collective-permute-start(bf16[24,32,256]{2,1,0:T(8,128)(2,1)S(1)} %pad_maximum_fusion.2), channel_id=1, source_target_pairs={{0,2},{1,3},{2,10},{3,11},{4,0},{5,1},{6,8},{7,9},{8,6},{9,7},{10,... | collective-permute-start | bytes 1179656 | tf_op jit(solution)/shard_map/ppermute | solution.py:129
  10.4 31.1 %collective-permute-start.13 = (bf16[24,32,256]{2,1,0:T(8,128)(2,1)S(1)}, bf16[24,32,256]{2,1,0:T(8,128)(2,1)S(1)}, u32[]{:S(2)}, u32[]{:S(2)}) collective-permute-start(bf16[24,32,256]{2,1,0:T(8,128)(2,1)S(1)} %pad_maximum_fusion.3), channel_id=1, source_target_pairs={{0,10},{1,11},{2,2},{3,3},{4,8},{5,9},{6,0},{7,1},{8,14},{9,15},{1... | collective-permute-start | bytes 1179656 | tf_op jit(solution)/shard_map/ppermute | solution.py:129
  14.5 32.7 %copy-start.2 = (f32[66,32]{1,0:T(8,128)}, f32[66,32]{1,0:T(8,128)S(1)}, u32[]{:S(2)}) copy-start(f32[66,32]{1,0:T(8,128)S(1)} %dynamic-slice_select_fusion) | copy-start | bytes 25348
  15.1 27.9 %collective-permute-start.2 = (bf16[24,32,256]{2,1,0:T(8,128)(2,1)S(1)}, bf16[24,32,256]{2,1,0:T(8,128)(2,1)S(1)}, u32[]{:S(2)}, u32[]{:S(2)}) collective-permute-start(bf16[24,32,256]{2,1,0:T(8,128)(2,1)S(1)} %collective-permute-done.1.refs_3_), channel_id=1, source_target_pairs={{0,1},{1,0},{2,3},{3,2},{4,5},{5,4},{6,7},{7,6},{8,9},{9,8},{10,11... | collective-permute-start | bytes 1179656 | tf_op jit(solution)/shard_map/ppermute | solution.py:129
  16.6 30.1 %collective-permute-start.3 = (bf16[24,32,256]{2,1,0:T(8,128)(2,1)S(1)}, bf16[24,32,256]{2,1,0:T(8,128)(2,1)S(1)}, u32[]{:S(2)}, u32[]{:S(2)}) collective-permute-start(bf16[24,32,256]{2,1,0:T(8,128)(2,1)S(1)} %collective-permute-done.1.refs_3_), channel_id=1, source_target_pairs={{0,8},{1,9},{2,10},{3,11},{4,12},{5,13},{6,14},{7,15},{8,0},{9,1},... | collective-permute-start | bytes 1179656 | tf_op jit(solution)/shard_map/ppermute | solution.py:129
  19.4 30.4 %collective-permute-start.6 = (bf16[24,32,256]{2,1,0:T(8,128)(2,1)S(1)}, bf16[24,32,256]{2,1,0:T(8,128)(2,1)S(1)}, u32[]{:S(2)}, u32[]{:S(2)}) collective-permute-start(bf16[24,32,256]{2,1,0:T(8,128)(2,1)S(1)} %collective-permute-done.5.refs_7_), channel_id=1, source_target_pairs={{0,1},{1,0},{2,3},{3,2},{4,5},{5,4},{6,7},{7,6},{8,9},{9,8},{10,11... | collective-permute-start | bytes 1179656 | tf_op jit(solution)/shard_map/ppermute | solution.py:129
  41.5 8.3 %collective-permute-start.7 = (bf16[24,32,256]{2,1,0:T(8,128)(2,1)S(1)}, bf16[24,32,256]{2,1,0:T(8,128)(2,1)S(1)}, u32[]{:S(2)}, u32[]{:S(2)}) collective-permute-start(bf16[24,32,256]{2,1,0:T(8,128)(2,1)S(1)} %collective-permute-done.5.refs_7_), channel_id=1, source_target_pairs={{0,8},{1,9},{2,10},{3,11},{4,12},{5,13},{6,14},{7,15},{8,0},{9,1},... | collective-permute-start | bytes 1179656 | tf_op jit(solution)/shard_map/ppermute | solution.py:129
  41.5 9.0 %collective-permute-start.10 = (bf16[24,32,256]{2,1,0:T(8,128)(2,1)S(1)}, bf16[24,32,256]{2,1,0:T(8,128)(2,1)}, u32[]{:S(2)}, u32[]{:S(2)}) collective-permute-start(bf16[24,32,256]{2,1,0:T(8,128)(2,1)S(1)} %collective-permute-done.9.refs_11_), channel_id=1, source_target_pairs={{0,1},{1,0},{2,3},{3,2},{4,5},{5,4},{6,7},{7,6},{8,9},{9,8},{10,11... | collective-permute-start | bytes 1179656 | tf_op jit(solution)/shard_map/ppermute | solution.py:129
  43.0 13.8 %collective-permute-start.11 = (bf16[24,32,256]{2,1,0:T(8,128)(2,1)S(1)}, bf16[24,32,256]{2,1,0:T(8,128)(2,1)}, u32[]{:S(2)}, u32[]{:S(2)}) collective-permute-start(bf16[24,32,256]{2,1,0:T(8,128)(2,1)S(1)} %collective-permute-done.9.refs_11_), channel_id=1, source_target_pairs={{0,8},{1,9},{2,10},{3,11},{4,12},{5,13},{6,14},{7,15},{8,0},{9,1},... | collective-permute-start | bytes 1179656 | tf_op jit(solution)/shard_map/ppermute | solution.py:129
  46.8 12.1 %collective-permute-start.14 = (bf16[24,32,256]{2,1,0:T(8,128)(2,1)S(1)}, bf16[24,32,256]{2,1,0:T(8,128)(2,1)}, u32[]{:S(2)}, u32[]{:S(2)}) collective-permute-start(bf16[24,32,256]{2,1,0:T(8,128)(2,1)S(1)} %collective-permute-done.13.refs_15_), channel_id=1, source_target_pairs={{0,1},{1,0},{2,3},{3,2},{4,5},{5,4},{6,7},{7,6},{8,9},{9,8},{10,11... | collective-permute-start | bytes 1179656 | tf_op jit(solution)/shard_map/ppermute | solution.py:129
  49.8 16.1 %collective-permute-start.15 = (bf16[24,32,256]{2,1,0:T(8,128)(2,1)S(1)}, bf16[24,32,256]{2,1,0:T(8,128)(2,1)}, u32[]{:S(2)}, u32[]{:S(2)}) collective-permute-start(bf16[24,32,256]{2,1,0:T(8,128)(2,1)S(1)} %collective-permute-done.13.refs_15_), channel_id=1, source_target_pairs={{0,8},{1,9},{2,10},{3,11},{4,12},{5,13},{6,14},{7,15},{8,0},{9,1},... | collective-permute-start | bytes 1179656 | tf_op jit(solution)/shard_map/ppermute | solution.py:129
  49.8 16.1 %collective-permute-start.4 = (bf16[24,32,256]{2,1,0:T(8,128)(2,1)S(1)}, bf16[24,32,256]{2,1,0:T(8,128)(2,1)}, u32[]{:S(2)}, u32[]{:S(2)}) collective-permute-start(bf16[24,32,256]{2,1,0:T(8,128)(2,1)S(1)} %collective-permute-done.2.refs_4_), channel_id=1, source_target_pairs={{0,8},{1,9},{2,10},{3,11},{4,12},{5,13},{6,14},{7,15},{8,0},{9,1},... | collective-permute-start | bytes 1179656 | tf_op jit(solution)/shard_map/ppermute | solution.py:129
  50.5 15.4 %collective-permute-start.8 = (bf16[24,32,256]{2,1,0:T(8,128)(2,1)S(1)}, bf16[24,32,256]{2,1,0:T(8,128)(2,1)}, u32[]{:S(2)}, u32[]{:S(2)}) collective-permute-start(bf16[24,32,256]{2,1,0:T(8,128)(2,1)S(1)} %collective-permute-done.6.refs_8_), channel_id=1, source_target_pairs={{0,8},{1,9},{2,10},{3,11},{4,12},{5,13},{6,14},{7,15},{8,0},{9,1},... | collective-permute-start | bytes 1179656 | tf_op jit(solution)/shard_map/ppermute | solution.py:129
  56.8 9.1 %collective-permute-start.12 = (bf16[24,32,256]{2,1,0:T(8,128)(2,1)}, bf16[24,32,256]{2,1,0:T(8,128)(2,1)}, u32[]{:S(2)}, u32[]{:S(2)}) collective-permute-start(bf16[24,32,256]{2,1,0:T(8,128)(2,1)} %collective-permute-done.10.refs_12_), channel_id=1, source_target_pairs={{0,8},{1,9},{2,10},{3,11},{4,12},{5,13},{6,14},{7,15},{8,0},{9,1},... | collective-permute-start | bytes 1179656 | tf_op jit(solution)/shard_map/ppermute | solution.py:129
  58.9 7.0 %collective-permute-start.16 = (bf16[24,32,256]{2,1,0:T(8,128)(2,1)}, bf16[24,32,256]{2,1,0:T(8,128)(2,1)}, u32[]{:S(2)}, u32[]{:S(2)}) collective-permute-start(bf16[24,32,256]{2,1,0:T(8,128)(2,1)} %collective-permute-done.14.refs_16_), channel_id=1, source_target_pairs={{0,8},{1,9},{2,10},{3,11},{4,12},{5,13},{6,14},{7,15},{8,0},{9,1},... | collective-permute-start | bytes 1179656 | tf_op jit(solution)/shard_map/ppermute | solution.py:129
  77.2 16.7 %collective-permute-start.18 = (bf16[4,256,256]{2,1,0:T(8,128)(2,1)}, bf16[4,256,256]{2,1,0:T(8,128)(2,1)}, u32[]{:S(2)}, u32[]{:S(2)}) collective-permute-start(bf16[4,256,256]{2,1,0:T(8,128)(2,1)} %get-tuple-element.12), channel_id=1, source_target_pairs={{0,16},{1,17},{2,18},{3,19},{4,20},{5,21},{6,22},{7,23},{8,24},{9,... | collective-permute-start | bytes 1572872 | tf_op jit(solution)/shard_map/ppermute | solution.py:129
  93.2 13.8 %collective-permute-start.17 = (bf16[4,256,256]{2,1,0:T(8,128)(2,1)}, bf16[4,256,256]{2,1,0:T(8,128)(2,1)S(1)}, u32[]{:S(2)}, u32[]{:S(2)}) collective-permute-start(bf16[4,256,256]{2,1,0:T(8,128)(2,1)} %get-tuple-element.10), channel_id=1, source_target_pairs={{0,16},{1,17},{2,18},{3,19},{4,20},{5,21},{6,22},{7,23},{8,24},{9,... | collective-permute-start | bytes 1572872 | tf_op jit(solution)/shard_map/ppermute | solution.py:129
  95.0 13.3 %collective-permute-start.19 = (bf16[4,256,256]{2,1,0:T(8,128)(2,1)S(1)}, bf16[4,256,256]{2,1,0:T(8,128)(2,1)S(1)}, u32[]{:S(2)}, u32[]{:S(2)}) collective-permute-start(bf16[4,256,256]{2,1,0:T(8,128)(2,1)S(1)} %add_convert_fusion), channel_id=1, source_target_pairs={{0,2},{1,3},{2,0},{3,1},{4,6},{5,7},{6,4},{7,5},{8,10},{9,11},{10,... | collective-permute-start | bytes 1572872 | tf_op jit(solution)/shard_map/ppermute | solution.py:129
  108.6 6.7 %collective-permute-start.22 = (bf16[2,256,256]{2,1,0:T(8,128)(2,1)S(1)}, bf16[2,256,256]{2,1,0:T(8,128)(2,1)S(1)}, u32[]{:S(2)}, u32[]{:S(2)}) collective-permute-start(bf16[2,256,256]{2,1,0:T(8,128)(2,1)S(1)} %get-tuple-element.16), channel_id=1, source_target_pairs={{4,8},{5,9},{6,10},{7,11},{8,4},{9,5},{10,6},{11,7},{20,24},{21,25... | collective-permute-start | bytes 786440 | tf_op jit(solution)/shard_map/ppermute | solution.py:129
  109.3 15.4 %collective-permute-start.21 = (bf16[2,256,256]{2,1,0:T(8,128)(2,1)S(1)}, bf16[2,256,256]{2,1,0:T(8,128)(2,1)S(1)}, u32[]{:S(2)}, u32[]{:S(2)}) collective-permute-start(bf16[2,256,256]{2,1,0:T(8,128)(2,1)S(1)} %get-tuple-element.15), channel_id=1, source_target_pairs={{4,0},{5,1},{6,2},{7,3},{8,12},{9,13},{10,14},{11,15},{20,16},{21,... | collective-permute-start | bytes 786440 | tf_op jit(solution)/shard_map/ppermute | solution.py:129
  110.6 14.1 %collective-permute-start.20 = (bf16[2,256,256]{2,1,0:T(8,128)(2,1)S(1)}, bf16[2,256,256]{2,1,0:T(8,128)(2,1)S(1)}, u32[]{:S(2)}, u32[]{:S(2)}) collective-permute-start(bf16[2,256,256]{2,1,0:T(8,128)(2,1)S(1)} %get-tuple-element.16), channel_id=1, source_target_pairs={{0,8},{1,9},{2,10},{3,11},{12,4},{13,5},{14,6},{15,7},{16,24},{17,... | collective-permute-start | bytes 786440 | tf_op jit(solution)/shard_map/ppermute | solution.py:129
  (4 other events, 55.8 us)

commit v2 on v0

v2 whole, which is shorter than its diff:
```python
import functools

import jax
import jax.numpy as jnp
from jax import lax
from jax.experimental import pallas as pl
from jax.experimental.pallas import tpu as pltpu
from jax.sharding import PartitionSpec as P

BF16, F32 = jnp.bfloat16, jnp.float32
TILE = 16
VMEM_LIMIT = 48 << 20


def mix_kernel(count, flip, weights, *refs):
    envs, outs = refs[:count], refs[count:]
    nb, blk = envs[0].shape[0], envs[0].shape[2]
    combos, depth = weights.shape
    pairs = combos // len(outs)
    wide = depth * TILE
    spread = (
        lax.broadcasted_iota(jnp.int32, (depth, wide), 0)
        == lax.broadcasted_iota(jnp.int32, (depth, wide), 1) // TILE
    )
    spread = jnp.where(spread, 1.0, 0.0).astype(BF16)
    rows = jnp.dot(weights[...], spread, preferred_element_type=F32)
    rows = jnp.broadcast_to(rows[:, None, :], (combos, TILE, wide)).reshape(combos * TILE, wide)
    same = lax.broadcasted_iota(jnp.int32, rows.shape, 0) % TILE == (
        lax.broadcasted_iota(jnp.int32, rows.shape, 1) % TILE
    )
    mix = jnp.where(same, rows, 0.0).astype(BF16)
    order = lax.broadcasted_iota(jnp.int32, (blk, blk), 0) == (
        lax.broadcasted_iota(jnp.int32, (blk, blk), 1) ^ flip[0]
    )
    order = jnp.where(order, 1.0, 0.0).astype(BF16)

    def some_rows(step, carry):
        at = pl.multiple_of(((step * TILE) ^ flip[0]) // TILE * TILE, TILE)
        env = jnp.concatenate(
            [ref[i, pl.ds(at, TILE), :] for ref in envs for i in range(nb)], axis=0
        )
        env = jnp.dot(env, order, preferred_element_type=F32).astype(BF16)
        to = pl.multiple_of(step * TILE, TILE)
        for n, out in enumerate(outs):
            part = mix[n * pairs * TILE : (n + 1) * pairs * TILE]
            got = jnp.dot(part, env, preferred_element_type=F32).astype(BF16)
            out[:, pl.ds(to, TILE), :] = got.reshape(pairs, TILE, blk)
        return carry

    lax.fori_loop(0, blk // TILE, some_rows, 0)


def pair_kernel(count, groups, info, flip, mixed, *refs):
    halves = (refs[:count], refs[count : 2 * count])
    outs = refs[2 * count : -1]
    total = refs[-1]
    pairs, blk = mixed.shape[0], mixed.shape[1]
    total[...] = jnp.zeros_like(total)
    row = lax.broadcasted_iota(jnp.int32, (blk, blk), 0) ^ flip[0]
    col = lax.broadcasted_iota(jnp.int32, (blk, blk), 1)
    for n, half_refs in enumerate(halves):

        def one_pair(q, carry, half_refs=half_refs, first=n * (pairs // 2)):
            p = first + q
            keep = (row < info[0, p]) & (col < info[1, p])
            core = jnp.concatenate([ref[q].astype(F32) for ref in half_refs], axis=0)
            masked = jnp.where(keep, core, 0.0).astype(BF16)
            half = jnp.dot(mixed[p], masked, preferred_element_type=F32).astype(BF16)
            term = lax.dot_general(
                masked, half, (((0,), (0,)), ((), ())), preferred_element_type=F32
            )
            total[info[2, p]] += term
            return carry

        lax.fori_loop(0, pairs // 2, one_pair, 0, unroll=4)
    size = total.shape[0] // len(outs)
    for f, ref in enumerate(outs):
        ref[...] = total[f * size : (f + 1) * size].astype(ref.dtype)


SMEM = pl.BlockSpec(memory_space=pltpu.SMEM)
VMEM = pl.BlockSpec(memory_space=pltpu.VMEM)


def mix_envs(flip, weights, envs, terms):
    combos, depth = weights.shape
    blk = envs[0].shape[2]
    macs = combos * depth * TILE * blk * blk
    return pl.pallas_call(
        functools.partial(mix_kernel, len(envs)),
        out_shape=[jax.ShapeDtypeStruct((combos // terms, blk, blk), BF16)] * terms,
        in_specs=[SMEM] + [VMEM] * (1 + len(envs)),
        out_specs=[VMEM] * terms,
        compiler_params=pltpu.CompilerParams(vmem_limit_bytes=VMEM_LIMIT),
        cost_estimate=pl.CostEstimate(flops=2 * macs, bytes_accessed=10 << 20, transcendentals=0),
        name="mix_envs",
    )(flip, weights, *envs)


def pair_sums(info, flip, mixed, own, others, groups, nb):
    pairs, blk = mixed.shape[:2]
    macs = 2 * pairs * blk * blk * blk
    return pl.pallas_call(
        functools.partial(pair_kernel, len(own), groups),
        out_shape=[jax.ShapeDtypeStruct((nb, blk, blk), F32)] * 2
        + [jax.ShapeDtypeStruct((nb, blk, blk), BF16)] * (2 * groups - 2),
        in_specs=[SMEM, SMEM] + [VMEM] * (1 + len(own) + len(others)),
        out_specs=[VMEM] * (2 * groups),
        scratch_shapes=[pltpu.VMEM((2 * groups * nb, blk, blk), F32)],
        compiler_params=pltpu.CompilerParams(vmem_limit_bytes=VMEM_LIMIT),
        cost_estimate=pl.CostEstimate(flops=2 * macs, bytes_accessed=10 << 20, transcendentals=0),
        name="pair_sums",
    )(info, flip, mixed, *own, *others)


def per_device(secs, terms, env_blocks, core_blocks, mpo_coeffs, pair_left, pair_right, block_dims):
    nx, nz = secs // 2, terms // 2
    half_z = nz // 2
    nb, blk = env_blocks.shape[1], env_blocks.shape[2]
    pairs_local, rows = core_blocks.shape[0], core_blocks.shape[1]
    piece_pairs = pairs_local // nz
    sec, term = lax.axis_index("sec"), lax.axis_index("term")
    x, c, z, y = sec // 2, sec % 2, term // 2, term % 2
    top, rest = z // half_z, z % half_z

    def send(value, to):
        perm = []
        for s in range(secs):
            for t in range(terms):
                d = to(s // 2, s % 2, t // 2, t % 2)
                if d is not None and d != (s // 2, s % 2, t // 2, t % 2):
                    perm.append((s * terms + t, (d[0] * 2 + d[1]) * terms + d[2] * 2 + d[3]))
        return lax.ppermute(value, ("sec", "term"), perm)

    def other_core(value):
        return send(value, lambda x, c, z, y: (x, 1 - c, z, y))

    def other_y(value):
        return send(value, lambda x, c, z, y: (x, c, z, 1 - y))

    envs = [
        jnp.where(
            c == top,
            env_blocks[0],
            send(
                env_blocks[0],
                lambda x, c, z, y: (x, 1 - c, z ^ half_z, y) if c != z // half_z else None,
            ),
        )
    ]
    near = z ^ jnp.where(c == top, 0, half_z)
    from_z, from_y = [0], [0]
    bit = 1
    while bit < half_z:
        envs += [send(v, lambda x, c, z, y: (x, c, z ^ bit, y)) for v in envs]
        from_z += [a ^ bit for a in from_z]
        bit *= 2
    envs += [other_y(v) for v in envs]
    from_y = [0] * len(from_z) + [1] * len(from_z)
    from_z = from_z * 2
    envs += [other_core(v) for v in envs]
    from_y = from_y * 2
    from_z = from_z + [a ^ half_z for a in from_z]
    env_terms = jnp.stack([2 * (near ^ a) + (y ^ b) for a, b in zip(from_z, from_y)])

    own, others = [], []
    for m in range(nz):
        g = z ^ m
        piece = lax.dynamic_slice_in_dim(core_blocks, g * piece_pairs, piece_pairs, 0)
        got = send(
            piece,
            lambda x, c, z, y, m=m: (x, (z ^ m) % 2, c * half_z + (z ^ m) // 2, y),
        )
        stays = (c == g % 2) & (z == c * half_z + g // 2)
        own.append(jnp.where(stays, piece, got))
    own = [[v, other_y(v)] for v in own]
    flip = (2 * rest + c) * 2 * rows
    if rows % TILE == 0:
        flip = flip + y * rows
    else:
        own = [[jnp.where(y == 0, jnp.concatenate(v, 1), jnp.concatenate(v[::-1], 1))] for v in own]
    others = [[other_core(v) for v in pair] for pair in own]
    others = [others[m ^ 1] for m in range(nz)]
    own = [v for pair in own for v in pair]
    others = [v for pair in others for v in pair]
    flip = flip[None].astype(jnp.int32)

    facts = jnp.concatenate(
        [
            mpo_coeffs.reshape(-1, pairs_local).astype(F32),
            pair_left[None].astype(F32),
            pair_right[None].astype(F32),
        ]
    )
    facts = jnp.where(c == top, facts, other_core(facts))
    facts = jnp.concatenate(
        [
            lax.dynamic_slice_in_dim(facts, (2 * rest + k) * piece_pairs, piece_pairs, 1)
            for k in (c, 1 - c)
        ],
        axis=1,
    )
    left, right = facts[-2].astype(jnp.int32), facts[-1].astype(jnp.int32)
    coeffs = facts[:-2].reshape(mpo_coeffs.shape[0], mpo_coeffs.shape[1], -1)
    ids = jnp.arange(block_dims.shape[0])
    left_block = (x * 2 + top) * nb + left
    dims_left = jnp.sum(jnp.where(left_block[:, None] == ids, block_dims, 0), axis=1)
    dims_right = jnp.sum(jnp.where(right[:, None] == ids, block_dims, 0), axis=1)
    to_sec, to_block = right // nb, right % nb
    slot = (((to_sec // 2) ^ x) * 2 + ((to_sec % 2) ^ top)) * nb + to_block
    info = jnp.stack([dims_left, dims_right, slot])

    mine = jnp.stack([2 * (c * half_z + (rest ^ t)) + y for t in range(half_z)])
    pick_w = (env_terms[:, None] == jnp.arange(mpo_coeffs.shape[0])).astype(BF16)
    pick_v = (mine[:, None] == jnp.arange(mpo_coeffs.shape[1])).astype(BF16)
    weights = jnp.einsum("nw,wvp->nvp", pick_w, coeffs.astype(BF16), preferred_element_type=F32)
    weights = jnp.einsum("tv,nvp->tpn", pick_v, weights.astype(BF16), preferred_element_type=F32)
    onehot = left[:, None] == jnp.arange(nb)
    weights = jnp.where(onehot[None, :, None, :], weights[..., None], 0.0).astype(BF16)
    weights = weights.reshape(half_z * left.shape[0], -1)
    mixed = mix_envs(flip, weights, envs, half_z)

    result = None
    for t in reversed(range(half_z)):
        parts = pair_sums(info, flip, mixed[t], own, others, nx, nb)
        for b in range(2):
            part = parts[b]
            for f in range(1, nx):
                got = send(parts[2 * f + b], lambda x, c, z, y: (x ^ f, c, z, y))
                part = part + got.astype(F32)
            got = send(
                part.astype(BF16),
                lambda x, c, z, y: (x, (z // half_z) ^ b, c * half_z + ((z % half_z) ^ t), y),
            ).astype(F32)
            if t == 0 and b == 0:
                got = got + jnp.where(c == top, part, 0.0)
            result = got if result is None else result + got
    return result[None]


def solution(mesh):
    return jax.shard_map(
        functools.partial(per_device, mesh.shape["sec"], mesh.shape["term"]),
        mesh=mesh,
        in_specs=(
            P("term", "sec", None, None),
            P("sec", "term", None),
            P(None, None, "sec"),
            P("sec"),
            P("sec"),
            P(),
        ),
        out_specs=P("term", "sec", None, None),
        check_vma=False,
    )
```

time: 288 us -> 123 us (0.43)
  the two profiles are of different devices: /device:TPU:1 before, /device:TPU:0 now
where the time goes in v2:
time: 123 us; the launch traced here: 122 us
  waiting for transfers between devices  49.7 us (40%)
  starting transfers between devices  36.9 us (30%)
  Pallas kernels  27.3 us (22%)
  other arithmetic  4.21 us (3%)
  local copies, waits for them, and re-layouts  3.26 us (3%)
    ppermute x33, waiting for transfers between devices, send(): return lax.ppermute(value, ('sec', 'term'), perm)  49.7 us
    ppermute x33, starting transfers between devices, send(): return lax.ppermute(value, ('sec', 'term'), perm)  36.9 us
    pallas_call x2, Pallas kernels, pair_sums(): pl.pallas_call(functools.partial(pair_kernel, len(own), groups), out_shap...  14.8 us
    pallas_call x1, Pallas kernels, mix_envs(): pl.pallas_call(functools.partial(mix_kernel, len(envs)), out_shape=[jax.S...  12.5 us
  transfers between devices with their start and end apart: 33, of which 12 were waited for; matrix products, arithmetic and copies ran while one was open for 4% of the time, Pallas kernels for 16%

profile of v2, /device:TPU:0, one launch (start us, length us, event | category | flops | bytes accessed | tf_op | source)
XLA Modules:
  0.0 122.2 jit_solution(13967661549024993637)
XLA Ops:
  2.2 5.5 %collective-permute-start = (f32[66,64]{1,0:T(8,128)S(1)}, f32[66,64]{1,0:T(8,128)S(1)}, u32[]{:S(2)}, u32[]{:S(2)}) collective-permute-start(f32[66,64]{1,0:T(8,128)S(1)} %pad_maximum_fusion), channel_id=1, source_target_pairs={{0,8},{1,9},{2,10},{3,11},{4,12},{5,13},{6,14},{7,15},{8,0},{9,1},... | collective-permute-start | bytes 50696 | tf_op jit(solution)/shard_map/ppermute | solution.py:133
  9.0 3.1 %collective-permute-start.15 = (bf16[16,32,256]{2,1,0:T(8,128)(2,1)S(1)}, bf16[16,32,256]{2,1,0:T(8,128)(2,1)S(1)}, u32[]{:S(2)}, u32[]{:S(2)}) collective-permute-start(bf16[16,32,256]{2,1,0:T(8,128)(2,1)S(1)} %get-tuple-element.31), channel_id=1, source_target_pairs={{0,10},{1,11},{4,8},{5,9},{6,0},{7,1},{8,14},{9,15},{10,6},{11,7},... | collective-permute-start | bytes 786440 | tf_op jit(solution)/shard_map/ppermute | solution.py:133
  15.0 5.5 %collective-permute-start.2 = (bf16[2,256,256]{2,1,0:T(8,128)(2,1)S(1)}, bf16[2,256,256]{2,1,0:T(8,128)(2,1)S(1)}, u32[]{:S(2)}, u32[]{:S(2)}) collective-permute-start(bf16[2,256,256]{2,1,0:T(8,128)(2,1)S(1)} %broadcast_select_fusion.4.refs_0_), channel_id=1, source_target_pairs={{0,2},{1,3},{2,0},{3,1},{4,6},{5,7},{6,4},{7,5},{8,10},{9,11},{10,... | collective-permute-start | bytes 786440 | tf_op jit(solution)/shard_map/ppermute | solution.py:133
  20.5 1.5 %collective-permute-start.3 = (bf16[2,256,256]{2,1,0:T(8,128)(2,1)S(1)}, bf16[2,256,256]{2,1,0:T(8,128)(2,1)}, u32[]{:S(2)}, u32[]{:S(2)}) collective-permute-start(bf16[2,256,256]{2,1,0:T(8,128)(2,1)S(1)} %broadcast_select_fusion.4.refs_0_), channel_id=1, source_target_pairs={{0,1},{1,0},{2,3},{3,2},{4,5},{5,4},{6,7},{7,6},{8,9},{9,8},{10,11... | collective-permute-start | bytes 786440 | tf_op jit(solution)/shard_map/ppermute | solution.py:133
  22.0 2.2 %collective-permute-done.15 = bf16[16,32,256]{2,1,0:T(8,128)(2,1)S(1)} collective-permute-done((bf16[16,32,256]{2,1,0:T(8,128)(2,1)S(1)}, bf16[16,32,256]{2,1,0:T(8,128)(2,1)S(1)}, u32[]{:S(2)}, u32[]{:S(2)}) %collective-permute-start.15) | collective-permute-done | bytes 262176 | tf_op jit(solution)/shard_map/ppermute | solution.py:133
  25.1 5.7 %collective-permute-done.13 = bf16[16,32,256]{2,1,0:T(8,128)(2,1)S(1)} collective-permute-done((bf16[16,32,256]{2,1,0:T(8,128)(2,1)S(1)}, bf16[16,32,256]{2,1,0:T(8,128)(2,1)S(1)}, u32[]{:S(2)}, u32[]{:S(2)}) %collective-permute-start.13) | collective-permute-done | bytes 262176 | tf_op jit(solution)/shard_map/ppermute | solution.py:133
  30.9 1.5 %collective-permute-start.12 = (bf16[16,32,256]{2,1,0:T(8,128)(2,1)S(1)}, bf16[16,32,256]{2,1,0:T(8,128)(2,1)S(1)}, u32[]{:S(2)}, u32[]{:S(2)}) collective-permute-start(bf16[16,32,256]{2,1,0:T(8,128)(2,1)S(1)} %broadcast_select_fusion.2.refs_2_), channel_id=1, source_target_pairs={{0,1},{1,0},{2,3},{3,2},{4,5},{5,4},{6,7},{7,6},{8,9},{9,8},{10,11... | collective-permute-start | bytes 786440 | tf_op jit(solution)/shard_map/ppermute | solution.py:133
  32.5 3.5 %collective-permute-start.17 = (bf16[16,32,256]{2,1,0:T(8,128)(2,1)S(1)}, bf16[16,32,256]{2,1,0:T(8,128)(2,1)S(1)}, u32[]{:S(2)}, u32[]{:S(2)}) collective-permute-start(bf16[16,32,256]{2,1,0:T(8,128)(2,1)S(1)} %broadcast_select_fusion.2.refs_2_), channel_id=1, source_target_pairs={{0,8},{1,9},{2,10},{3,11},{4,12},{5,13},{6,14},{7,15},{8,0},{9,1},... | collective-permute-start | bytes 786440 | tf_op jit(solution)/shard_map/ppermute | solution.py:133
  35.9 2.8 %collective-permute-done.2.refs_1_ = bf16[2,256,256]{2,1,0:T(8,128)(2,1)S(1)} collective-permute-done((bf16[2,256,256]{2,1,0:T(8,128)(2,1)S(1)}, bf16[2,256,256]{2,1,0:T(8,128)(2,1)S(1)}, u32[]{:S(2)}, u32[]{:S(2)}) %collective-permute-start.2) | collective-permute-done | bytes 262176 | tf_op jit(solution)/shard_map/ppermute | solution.py:133
  41.5 1.5 %collective-permute-start.4 = (bf16[2,256,256]{2,1,0:T(8,128)(2,1)S(1)}, bf16[2,256,256]{2,1,0:T(8,128)(2,1)}, u32[]{:S(2)}, u32[]{:S(2)}) collective-permute-start(bf16[2,256,256]{2,1,0:T(8,128)(2,1)S(1)} %collective-permute-done.2.refs_1_), channel_id=1, source_target_pairs={{0,1},{1,0},{2,3},{3,2},{4,5},{5,4},{6,7},{7,6},{8,9},{9,8},{10,11... | collective-permute-start | bytes 786440 | tf_op jit(solution)/shard_map/ppermute | solution.py:133
  43.1 3.1 %collective-permute-done.16.refs_7_ = bf16[16,32,256]{2,1,0:T(8,128)(2,1)S(1)} collective-permute-done((bf16[16,32,256]{2,1,0:T(8,128)(2,1)S(1)}, bf16[16,32,256]{2,1,0:T(8,128)(2,1)S(1)}, u32[]{:S(2)}, u32[]{:S(2)}) %collective-permute-start.16) | collective-permute-done | bytes 262176 | tf_op jit(solution)/shard_map/ppermute | solution.py:133
  46.2 5.6 %collective-permute-done.14.refs_5_ = bf16[16,32,256]{2,1,0:T(8,128)(2,1)S(1)} collective-permute-done((bf16[16,32,256]{2,1,0:T(8,128)(2,1)S(1)}, bf16[16,32,256]{2,1,0:T(8,128)(2,1)S(1)}, u32[]{:S(2)}, u32[]{:S(2)}) %collective-permute-start.14) | collective-permute-done | bytes 262176 | tf_op jit(solution)/shard_map/ppermute | solution.py:133
  51.8 2.5 %collective-permute-start.10 = (bf16[16,32,256]{2,1,0:T(8,128)(2,1)S(1)}, bf16[16,32,256]{2,1,0:T(8,128)(2,1)S(1)}, u32[]{:S(2)}, u32[]{:S(2)}) collective-permute-start(bf16[16,32,256]{2,1,0:T(8,128)(2,1)S(1)} %broadcast_select_fusion.3.refs_0_), channel_id=1, source_target_pairs={{0,1},{1,0},{2,3},{3,2},{4,5},{5,4},{6,7},{7,6},{8,9},{9,8},{10,11... | collective-permute-start | bytes 786440 | tf_op jit(solution)/shard_map/ppermute | solution.py:133
  54.8 2.6 %collective-permute-done.4.refs_3_ = bf16[2,256,256]{2,1,0:T(8,128)(2,1)} collective-permute-done((bf16[2,256,256]{2,1,0:T(8,128)(2,1)S(1)}, bf16[2,256,256]{2,1,0:T(8,128)(2,1)}, u32[]{:S(2)}, u32[]{:S(2)}) %collective-permute-start.4) | collective-permute-done | bytes 262176 | tf_op jit(solution)/shard_map/ppermute | solution.py:133
  58.3 3.6 %collective-permute-done.10.refs_1_ = bf16[16,32,256]{2,1,0:T(8,128)(2,1)S(1)} collective-permute-done((bf16[16,32,256]{2,1,0:T(8,128)(2,1)S(1)}, bf16[16,32,256]{2,1,0:T(8,128)(2,1)S(1)}, u32[]{:S(2)}, u32[]{:S(2)}) %collective-permute-start.10) | collective-permute-done | bytes 262176 | tf_op jit(solution)/shard_map/ppermute | solution.py:133
  63.9 12.5 %mix_envs.1 = (bf16[32,256,256]{2,1,0:T(8,128)(2,1)}, bf16[32,256,256]{2,1,0:T(8,128)(2,1)}) custom-call(s32[1]{0:T(128)} %bitcast.7.flip, bf16[64,16]{1,0:T(8,128)(2,1)S(1)} %copy.24.weights, bf16[2,256,256]{2,1,0:T(8,128)(2,1)S(1)} %broadcast_select_fusion.4.refs_0_, bf16[2,256,256]{2,1,0:T(8,128)(2,1)S(1)} %collective-permute-done.2.refs_1_, ...), custom_call_target="tpu_custom_call" | custom-call | flops 2147483648 | bytes 10485760 | tf_op jit(solution)/shard_map/mix_envs/pallas_call | solution.py:89
  76.4 7.4 %pair_sums.2 = (f32[2,256,256]{2,1,0:T(8,128)S(1)}, f32[2,256,256]{2,1,0:T(8,128)S(1)}, bf16[2,256,256]{2,1,0:T(8,128)(2,1)S(1)}, bf16[2,256,256]{2,1,0:T(8,128)(2,1)S(1)}) custom-call(s32[3,32]{1,0:T(4,128)S(1)} %pad_add_fusion.info, s32[1]{0:T(128)} %bitcast.7.flip, bf16[32,256,256]{2,1,0:T(8,128)(2,1)} %get-tuple-element.15.mixed, ...), custom_call_target="tpu_custom_call" | custom-call | flops 2147483648 | bytes 10485760 | tf_op jit(solution)/shard_map/pair_sums/pallas_call | solution.py:103
  83.9 1.6 %collective-permute-start.25 = (bf16[2,256,256]{2,1,0:T(8,128)(2,1)S(1)}, bf16[2,256,256]{2,1,0:T(8,128)(2,1)S(1)}, u32[]{:S(2)}, u32[]{:S(2)}) collective-permute-start(bf16[2,256,256]{2,1,0:T(8,128)(2,1)S(1)} %get-tuple-element.17), channel_id=1, source_target_pairs={{0,16},{1,17},{2,18},{3,19},{4,20},{5,21},{6,22},{7,23},{8,24},{9,... | collective-permute-start | bytes 786440 | tf_op jit(solution)/shard_map/ppermute | solution.py:133
  86.0 7.4 %pair_sums.3 = (f32[2,256,256]{2,1,0:T(8,128)S(1)}, f32[2,256,256]{2,1,0:T(8,128)S(1)}, bf16[2,256,256]{2,1,0:T(8,128)(2,1)S(1)}, bf16[2,256,256]{2,1,0:T(8,128)(2,1)S(1)}) custom-call(s32[3,32]{1,0:T(4,128)S(1)} %pad_add_fusion.info, s32[1]{0:T(128)} %bitcast.7.flip, bf16[32,256,256]{2,1,0:T(8,128)(2,1)} %get-tuple-element.20.mixed, ...), custom_call_target="tpu_custom_call" | custom-call | flops 2147483648 | bytes 10485760 | tf_op jit(solution)/shard_map/pair_sums/pallas_call | solution.py:103
  93.4 1.6 %collective-permute-start.29 = (bf16[2,256,256]{2,1,0:T(8,128)(2,1)S(1)}, bf16[2,256,256]{2,1,0:T(8,128)(2,1)S(1)}, u32[]{:S(2)}, u32[]{:S(2)}) collective-permute-start(bf16[2,256,256]{2,1,0:T(8,128)(2,1)S(1)} %get-tuple-element.22), channel_id=1, source_target_pairs={{0,16},{1,17},{2,18},{3,19},{4,20},{5,21},{6,22},{7,23},{8,24},{9,... | collective-permute-start | bytes 786440 | tf_op jit(solution)/shard_map/ppermute | solution.py:133
  96.2 2.5 %collective-permute-done.27 = bf16[2,256,256]{2,1,0:T(8,128)(2,1)S(1)} collective-permute-done((bf16[2,256,256]{2,1,0:T(8,128)(2,1)S(1)}, bf16[2,256,256]{2,1,0:T(8,128)(2,1)S(1)}, u32[]{:S(2)}, u32[]{:S(2)}) %collective-permute-start.27) | collective-permute-done | bytes 262176 | tf_op jit(solution)/shard_map/ppermute | solution.py:133
  98.8 5.5 %collective-permute-done.29 = bf16[2,256,256]{2,1,0:T(8,128)(2,1)S(1)} collective-permute-done((bf16[2,256,256]{2,1,0:T(8,128)(2,1)S(1)}, bf16[2,256,256]{2,1,0:T(8,128)(2,1)S(1)}, u32[]{:S(2)}, u32[]{:S(2)}) %collective-permute-start.29) | collective-permute-done | bytes 262176 | tf_op jit(solution)/shard_map/ppermute | solution.py:133
  105.1 4.0 %collective-permute-done.31 = bf16[2,256,256]{2,1,0:T(8,128)(2,1)S(1)} collective-permute-done((bf16[2,256,256]{2,1,0:T(8,128)(2,1)S(1)}, bf16[2,256,256]{2,1,0:T(8,128)(2,1)S(1)}, u32[]{:S(2)}, u32[]{:S(2)}) %collective-permute-start.31) | collective-permute-done | bytes 262176 | tf_op jit(solution)/shard_map/ppermute | solution.py:133
  109.9 11.2 %collective-permute-done.32 = bf16[2,256,256]{2,1,0:T(8,128)(2,1)S(1)} collective-permute-done((bf16[2,256,256]{2,1,0:T(8,128)(2,1)S(1)}, bf16[2,256,256]{2,1,0:T(8,128)(2,1)S(1)}, u32[]{:S(2)}, u32[]{:S(2)}) %collective-permute-start.32) | collective-permute-done | bytes 262176 | tf_op jit(solution)/shard_map/ppermute | solution.py:133
  (81 shorter events, 17.8 us)
Async XLA Ops:
  0.0 14.0 %collective-permute-start.1 = (bf16[2,256,256]{2,1,0:T(8,128)(2,1)}, bf16[2,256,256]{2,1,0:T(8,128)(2,1)S(1)}, u32[]{:S(2)}, u32[]{:S(2)}) collective-permute-start(bf16[2,256,256]{2,1,0:T(8,128)(2,1)} %bitcast.41), channel_id=1, source_target_pairs={{4,8},{5,9},{6,10},{7,11},{8,4},{9,5},{10,6},{11,7},{20,24},{21,25... | collective-permute-start | bytes 786440 | tf_op jit(solution)/shard_map/ppermute | solution.py:133
  8.9 11.6 %collective-permute-start.11 = (bf16[16,32,256]{2,1,0:T(8,128)(2,1)S(1)}, bf16[16,32,256]{2,1,0:T(8,128)(2,1)S(1)}, u32[]{:S(2)}, u32[]{:S(2)}) collective-permute-start(bf16[16,32,256]{2,1,0:T(8,128)(2,1)S(1)} %get-tuple-element.32), channel_id=1, source_target_pairs={{0,8},{1,9},{2,0},{3,1},{4,10},{5,11},{6,2},{7,3},{8,12},{9,13},{1... | collective-permute-start | bytes 786440 | tf_op jit(solution)/shard_map/ppermute | solution.py:133
  9.0 15.2 %collective-permute-start.15 = (bf16[16,32,256]{2,1,0:T(8,128)(2,1)S(1)}, bf16[16,32,256]{2,1,0:T(8,128)(2,1)S(1)}, u32[]{:S(2)}, u32[]{:S(2)}) collective-permute-start(bf16[16,32,256]{2,1,0:T(8,128)(2,1)S(1)} %get-tuple-element.31), channel_id=1, source_target_pairs={{0,10},{1,11},{4,8},{5,9},{6,0},{7,1},{8,14},{9,15},{10,6},{11,7},... | collective-permute-start | bytes 786440 | tf_op jit(solution)/shard_map/ppermute | solution.py:133
  12.2 18.7 %collective-permute-start.13 = (bf16[16,32,256]{2,1,0:T(8,128)(2,1)S(1)}, bf16[16,32,256]{2,1,0:T(8,128)(2,1)S(1)}, u32[]{:S(2)}, u32[]{:S(2)}) collective-permute-start(bf16[16,32,256]{2,1,0:T(8,128)(2,1)S(1)} %get-tuple-element.34), channel_id=1, source_target_pairs={{0,2},{1,3},{2,10},{3,11},{4,0},{5,1},{6,8},{7,9},{8,6},{9,7},{10,... | collective-permute-start | bytes 786440 | tf_op jit(solution)/shard_map/ppermute | solution.py:133
  12.6 19.9 %collective-permute-start.9 = (bf16[16,32,256]{2,1,0:T(8,128)(2,1)S(1)}, bf16[16,32,256]{2,1,0:T(8,128)(2,1)S(1)}, u32[]{:S(2)}, u32[]{:S(2)}) collective-permute-start(bf16[16,32,256]{2,1,0:T(8,128)(2,1)S(1)} %get-tuple-element.33), channel_id=1, source_target_pairs={{2,8},{3,9},{4,2},{5,3},{6,10},{7,11},{8,4},{9,5},{10,12},{11,13},... | collective-permute-start | bytes 786440 | tf_op jit(solution)/shard_map/ppermute | solution.py:133
  15.0 23.7 %collective-permute-start.2 = (bf16[2,256,256]{2,1,0:T(8,128)(2,1)S(1)}, bf16[2,256,256]{2,1,0:T(8,128)(2,1)S(1)}, u32[]{:S(2)}, u32[]{:S(2)}) collective-permute-start(bf16[2,256,256]{2,1,0:T(8,128)(2,1)S(1)} %broadcast_select_fusion.4.refs_0_), channel_id=1, source_target_pairs={{0,2},{1,3},{2,0},{3,1},{4,6},{5,7},{6,4},{7,5},{8,10},{9,11},{10,... | collective-permute-start | bytes 786440 | tf_op jit(solution)/shard_map/ppermute | solution.py:133
  20.5 19.8 %collective-permute-start.3 = (bf16[2,256,256]{2,1,0:T(8,128)(2,1)S(1)}, bf16[2,256,256]{2,1,0:T(8,128)(2,1)}, u32[]{:S(2)}, u32[]{:S(2)}) collective-permute-start(bf16[2,256,256]{2,1,0:T(8,128)(2,1)S(1)} %broadcast_select_fusion.4.refs_0_), channel_id=1, source_target_pairs={{0,1},{1,0},{2,3},{3,2},{4,5},{5,4},{6,7},{7,6},{8,9},{9,8},{10,11... | collective-permute-start | bytes 786440 | tf_op jit(solution)/shard_map/ppermute | solution.py:133
  24.2 16.0 %collective-permute-start.5 = (bf16[2,256,256]{2,1,0:T(8,128)(2,1)S(1)}, bf16[2,256,256]{2,1,0:T(8,128)(2,1)S(1)}, u32[]{:S(2)}, u32[]{:S(2)}) collective-permute-start(bf16[2,256,256]{2,1,0:T(8,128)(2,1)S(1)} %broadcast_select_fusion.4.refs_0_), channel_id=1, source_target_pairs={{0,8},{1,9},{2,10},{3,11},{4,12},{5,13},{6,14},{7,15},{8,0},{9,1},... | collective-permute-start | bytes 786440 | tf_op jit(solution)/shard_map/ppermute | solution.py:133
  32.5 21.8 %collective-permute-start.17 = (bf16[16,32,256]{2,1,0:T(8,128)(2,1)S(1)}, bf16[16,32,256]{2,1,0:T(8,128)(2,1)S(1)}, u32[]{:S(2)}, u32[]{:S(2)}) collective-permute-start(bf16[16,32,256]{2,1,0:T(8,128)(2,1)S(1)} %broadcast_select_fusion.2.refs_2_), channel_id=1, source_target_pairs={{0,8},{1,9},{2,10},{3,11},{4,12},{5,13},{6,14},{7,15},{8,0},{9,1},... | collective-permute-start | bytes 786440 | tf_op jit(solution)/shard_map/ppermute | solution.py:133
  40.2 14.1 %collective-permute-start.21 = (bf16[16,32,256]{2,1,0:T(8,128)(2,1)S(1)}, bf16[16,32,256]{2,1,0:T(8,128)(2,1)S(1)}, u32[]{:S(2)}, u32[]{:S(2)}) collective-permute-start(bf16[16,32,256]{2,1,0:T(8,128)(2,1)S(1)} %broadcast_select_fusion.refs_6_), channel_id=1, source_target_pairs={{0,8},{1,9},{2,10},{3,11},{4,12},{5,13},{6,14},{7,15},{8,0},{9,1},... | collective-permute-start | bytes 786440 | tf_op jit(solution)/shard_map/ppermute | solution.py:133
  41.5 16.0 %collective-permute-start.4 = (bf16[2,256,256]{2,1,0:T(8,128)(2,1)S(1)}, bf16[2,256,256]{2,1,0:T(8,128)(2,1)}, u32[]{:S(2)}, u32[]{:S(2)}) collective-permute-start(bf16[2,256,256]{2,1,0:T(8,128)(2,1)S(1)} %collective-permute-done.2.refs_1_), channel_id=1, source_target_pairs={{0,1},{1,0},{2,3},{3,2},{4,5},{5,4},{6,7},{7,6},{8,9},{9,8},{10,11... | collective-permute-start | bytes 786440 | tf_op jit(solution)/shard_map/ppermute | solution.py:133
  46.2 11.5 %collective-permute-start.23 = (bf16[16,32,256]{2,1,0:T(8,128)(2,1)S(1)}, bf16[16,32,256]{2,1,0:T(8,128)(2,1)S(1)}, u32[]{:S(2)}, u32[]{:S(2)}) collective-permute-start(bf16[16,32,256]{2,1,0:T(8,128)(2,1)S(1)} %broadcast_select_fusion.1.refs_4_), channel_id=1, source_target_pairs={{0,8},{1,9},{2,10},{3,11},{4,12},{5,13},{6,14},{7,15},{8,0},{9,1},... | collective-permute-start | bytes 786440 | tf_op jit(solution)/shard_map/ppermute | solution.py:133
  57.8 18.6 %collective-permute-start.19 = (bf16[16,32,256]{2,1,0:T(8,128)(2,1)S(1)}, bf16[16,32,256]{2,1,0:T(8,128)(2,1)S(1)}, u32[]{:S(2)}, u32[]{:S(2)}) collective-permute-start(bf16[16,32,256]{2,1,0:T(8,128)(2,1)S(1)} %broadcast_select_fusion.3.refs_0_), channel_id=1, source_target_pairs={{0,8},{1,9},{2,10},{3,11},{4,12},{5,13},{6,14},{7,15},{8,0},{9,1},... | collective-permute-start | bytes 786440 | tf_op jit(solution)/shard_map/ppermute | solution.py:133
  61.9 14.5 %collective-permute-start.18 = (bf16[16,32,256]{2,1,0:T(8,128)(2,1)S(1)}, bf16[16,32,256]{2,1,0:T(8,128)(2,1)S(1)}, u32[]{:S(2)}, u32[]{:S(2)}) collective-permute-start(bf16[16,32,256]{2,1,0:T(8,128)(2,1)S(1)} %collective-permute-done.12.refs_3_), channel_id=1, source_target_pairs={{0,8},{1,9},{2,10},{3,11},{4,12},{5,13},{6,14},{7,15},{8,0},{9,1},... | collective-permute-start | bytes 786440 | tf_op jit(solution)/shard_map/ppermute | solution.py:133
  61.9 14.5 %collective-permute-start.22 = (bf16[16,32,256]{2,1,0:T(8,128)(2,1)S(1)}, bf16[16,32,256]{2,1,0:T(8,128)(2,1)S(1)}, u32[]{:S(2)}, u32[]{:S(2)}) collective-permute-start(bf16[16,32,256]{2,1,0:T(8,128)(2,1)S(1)} %collective-permute-done.16.refs_7_), channel_id=1, source_target_pairs={{0,8},{1,9},{2,10},{3,11},{4,12},{5,13},{6,14},{7,15},{8,0},{9,1},... | collective-permute-start | bytes 786440 | tf_op jit(solution)/shard_map/ppermute | solution.py:133
  62.5 14.0 %collective-permute-start.24 = (bf16[16,32,256]{2,1,0:T(8,128)(2,1)S(1)}, bf16[16,32,256]{2,1,0:T(8,128)(2,1)S(1)}, u32[]{:S(2)}, u32[]{:S(2)}) collective-permute-start(bf16[16,32,256]{2,1,0:T(8,128)(2,1)S(1)} %collective-permute-done.14.refs_5_), channel_id=1, source_target_pairs={{0,8},{1,9},{2,10},{3,11},{4,12},{5,13},{6,14},{7,15},{8,0},{9,1},... | collective-permute-start | bytes 786440 | tf_op jit(solution)/shard_map/ppermute | solution.py:133
  62.5 13.9 %collective-permute-start.20 = (bf16[16,32,256]{2,1,0:T(8,128)(2,1)S(1)}, bf16[16,32,256]{2,1,0:T(8,128)(2,1)S(1)}, u32[]{:S(2)}, u32[]{:S(2)}) collective-permute-start(bf16[16,32,256]{2,1,0:T(8,128)(2,1)S(1)} %collective-permute-done.10.refs_1_), channel_id=1, source_target_pairs={{0,8},{1,9},{2,10},{3,11},{4,12},{5,13},{6,14},{7,15},{8,0},{9,1},... | collective-permute-start | bytes 786440 | tf_op jit(solution)/shard_map/ppermute | solution.py:133
  83.9 11.6 %collective-permute-start.25 = (bf16[2,256,256]{2,1,0:T(8,128)(2,1)S(1)}, bf16[2,256,256]{2,1,0:T(8,128)(2,1)S(1)}, u32[]{:S(2)}, u32[]{:S(2)}) collective-permute-start(bf16[2,256,256]{2,1,0:T(8,128)(2,1)S(1)} %get-tuple-element.17), channel_id=1, source_target_pairs={{0,16},{1,17},{2,18},{3,19},{4,20},{5,21},{6,22},{7,23},{8,24},{9,... | collective-permute-start | bytes 786440 | tf_op jit(solution)/shard_map/ppermute | solution.py:133
  85.4 13.3 %collective-permute-start.27 = (bf16[2,256,256]{2,1,0:T(8,128)(2,1)S(1)}, bf16[2,256,256]{2,1,0:T(8,128)(2,1)S(1)}, u32[]{:S(2)}, u32[]{:S(2)}) collective-permute-start(bf16[2,256,256]{2,1,0:T(8,128)(2,1)S(1)} %get-tuple-element.19), channel_id=1, source_target_pairs={{0,16},{1,17},{2,18},{3,19},{4,20},{5,21},{6,22},{7,23},{8,24},{9,... | collective-permute-start | bytes 786440 | tf_op jit(solution)/shard_map/ppermute | solution.py:133
  93.4 11.0 %collective-permute-start.29 = (bf16[2,256,256]{2,1,0:T(8,128)(2,1)S(1)}, bf16[2,256,256]{2,1,0:T(8,128)(2,1)S(1)}, u32[]{:S(2)}, u32[]{:S(2)}) collective-permute-start(bf16[2,256,256]{2,1,0:T(8,128)(2,1)S(1)} %get-tuple-element.22), channel_id=1, source_target_pairs={{0,16},{1,17},{2,18},{3,19},{4,20},{5,21},{6,22},{7,23},{8,24},{9,... | collective-permute-start | bytes 786440 | tf_op jit(solution)/shard_map/ppermute | solution.py:133
  94.9 14.2 %collective-permute-start.31 = (bf16[2,256,256]{2,1,0:T(8,128)(2,1)S(1)}, bf16[2,256,256]{2,1,0:T(8,128)(2,1)S(1)}, u32[]{:S(2)}, u32[]{:S(2)}) collective-permute-start(bf16[2,256,256]{2,1,0:T(8,128)(2,1)S(1)} %get-tuple-element.24), channel_id=1, source_target_pairs={{0,16},{1,17},{2,18},{3,19},{4,20},{5,21},{6,22},{7,23},{8,24},{9,... | collective-permute-start | bytes 786440 | tf_op jit(solution)/shard_map/ppermute | solution.py:133
  95.5 13.7 %collective-permute-start.26 = (bf16[2,256,256]{2,1,0:T(8,128)(2,1)S(1)}, bf16[2,256,256]{2,1,0:T(8,128)(2,1)S(1)}, u32[]{:S(2)}, u32[]{:S(2)}) collective-permute-start(bf16[2,256,256]{2,1,0:T(8,128)(2,1)S(1)} %add_convert_fusion.2), channel_id=1, source_target_pairs={{0,2},{1,3},{2,0},{3,1},{4,10},{5,11},{6,8},{7,9},{8,6},{9,7},{10,... | collective-permute-start | bytes 786440 | tf_op jit(solution)/shard_map/ppermute | solution.py:133
  98.8 11.2 %collective-permute-start.28 = (bf16[2,256,256]{2,1,0:T(8,128)(2,1)S(1)}, bf16[2,256,256]{2,1,0:T(8,128)(2,1)S(1)}, u32[]{:S(2)}, u32[]{:S(2)}) collective-permute-start(bf16[2,256,256]{2,1,0:T(8,128)(2,1)S(1)} %add_convert_fusion.1), channel_id=1, source_target_pairs={{0,10},{1,11},{2,8},{3,9},{4,2},{5,3},{6,0},{7,1},{8,14},{9,15},{1... | collective-permute-start | bytes 786440 | tf_op jit(solution)/shard_map/ppermute | solution.py:133
  109.1 12.0 %collective-permute-start.32 = (bf16[2,256,256]{2,1,0:T(8,128)(2,1)S(1)}, bf16[2,256,256]{2,1,0:T(8,128)(2,1)S(1)}, u32[]{:S(2)}, u32[]{:S(2)}) collective-permute-start(bf16[2,256,256]{2,1,0:T(8,128)(2,1)S(1)} %add_convert_fusion), channel_id=1, source_target_pairs={{0,8},{1,9},{2,10},{3,11},{4,0},{5,1},{6,2},{7,3},{8,12},{9,13},{1... | collective-permute-start | bytes 786440 | tf_op jit(solution)/shard_map/ppermute | solution.py:133
  (12 other events, 135.0 us)

commit v3 on v2

v3 whole, which is shorter than its diff:
```python
import functools

import jax
import jax.numpy as jnp
from jax import lax
from jax.experimental import pallas as pl
from jax.experimental.pallas import tpu as pltpu
from jax.sharding import PartitionSpec as P

BF16, F32 = jnp.bfloat16, jnp.float32
TILE = 16
VMEM_LIMIT = 16 << 20


def mix_kernel(count, flip, dims, weights, *refs):
    envs, outs = refs[:count], refs[count:-2]
    mix, ordered = refs[-2:]
    nb, blk = envs[0].shape[0], envs[0].shape[2]
    combos, depth = weights.shape
    pairs = combos // len(outs)
    wide = depth * TILE
    spread = (
        lax.broadcasted_iota(jnp.int32, (depth, wide), 0)
        == lax.broadcasted_iota(jnp.int32, (depth, wide), 1) // TILE
    )
    spread = jnp.where(spread, 1.0, 0.0).astype(BF16)
    rows = jnp.dot(weights[...], spread, preferred_element_type=F32)
    rows = jnp.broadcast_to(rows[:, None, :], (combos, TILE, wide)).reshape(combos * TILE, wide)
    same = lax.broadcasted_iota(jnp.int32, rows.shape, 0) % TILE == (
        lax.broadcasted_iota(jnp.int32, rows.shape, 1) % TILE
    )
    mix[...] = jnp.where(same, rows, 0.0).astype(BF16)
    order = lax.broadcasted_iota(jnp.int32, (blk, blk), 0) == (
        lax.broadcasted_iota(jnp.int32, (blk, blk), 1) ^ flip[0]
    )
    order = jnp.where(order, 1.0, 0.0).astype(BF16)

    row = lax.broadcasted_iota(jnp.int32, (TILE, blk), 0)
    col = lax.broadcasted_iota(jnp.int32, (TILE, blk), 1)

    def order_rows(step, carry):
        at = pl.multiple_of(((step * TILE) ^ flip[0]) // TILE * TILE, TILE)
        used = [
            jnp.where((row + at < dims[i]) & (col < dims[i]), 1.0, 0.0).astype(BF16)
            for i in range(nb)
        ]
        env = jnp.concatenate(
            [ref[i, pl.ds(at, TILE), :] * used[i] for ref in envs for i in range(nb)], axis=0
        )
        ordered[step] = jnp.dot(env, order, preferred_element_type=F32).astype(BF16)
        return carry

    lax.fori_loop(0, blk // TILE, order_rows, 0, unroll=True)

    def mix_rows(step, carry):
        to = pl.multiple_of(step * TILE, TILE)
        for n, out in enumerate(outs):
            part = mix[n * pairs * TILE : (n + 1) * pairs * TILE, :]
            got = jnp.dot(part, ordered[step], preferred_element_type=F32).astype(BF16)
            out[:, pl.ds(to, TILE), :] = got.reshape(pairs, TILE, blk)
        return carry

    lax.fori_loop(0, blk // TILE, mix_rows, 0, unroll=True)


def pair_kernel(count, slots, dims, mixed, *refs):
    halves = (refs[:count], refs[count : 2 * count])
    outs = refs[2 * count : -1]
    total = refs[-1]
    pairs, blk = mixed.shape[0], mixed.shape[1]
    total[...] = jnp.zeros_like(total)
    for n, half_refs in enumerate(halves):

        def one_pair(q, carry, half_refs=half_refs, first=n * (pairs // 2)):
            p = first + q
            core = jnp.concatenate([ref[q] for ref in half_refs], axis=0)
            half = jnp.dot(mixed[p], core, preferred_element_type=F32).astype(BF16)
            term = lax.dot_general(
                core, half, (((0,), (0,)), ((), ())), preferred_element_type=F32
            )
            total[slots[p]] += term
            return carry

        lax.fori_loop(0, pairs // 2, one_pair, 0, unroll=True)
    row = lax.broadcasted_iota(jnp.int32, (blk, blk), 0)
    col = lax.broadcasted_iota(jnp.int32, (blk, blk), 1)
    size = total.shape[0] // len(outs)
    for f, ref in enumerate(outs):
        for i in range(size):
            s = f * size + i
            keep = (row < dims[s]) & (col < dims[s])
            ref[i] = jnp.where(keep, total[s], 0.0).astype(ref.dtype)


SMEM = pl.BlockSpec(memory_space=pltpu.SMEM)
VMEM = pl.BlockSpec(memory_space=pltpu.VMEM)


def mix_envs(flip, dims, weights, envs, terms):
    combos, depth = weights.shape
    blk = envs[0].shape[2]
    macs = combos * depth * TILE * blk * blk
    return pl.pallas_call(
        functools.partial(mix_kernel, len(envs)),
        out_shape=[jax.ShapeDtypeStruct((combos // terms, blk, blk), BF16)] * terms,
        in_specs=[SMEM, SMEM] + [VMEM] * (1 + len(envs)),
        out_specs=[VMEM] * terms,
        scratch_shapes=[
            pltpu.VMEM((combos * TILE, depth * TILE), BF16),
            pltpu.VMEM((blk // TILE, depth * TILE, blk), BF16),
        ],
        compiler_params=pltpu.CompilerParams(vmem_limit_bytes=VMEM_LIMIT),
        cost_estimate=pl.CostEstimate(flops=2 * macs, bytes_accessed=10 << 20, transcendentals=0),
        name="mix_envs",
    )(flip, dims, weights, *envs)


def pair_sums(slots, dims, mixed, own, others, groups, nb):
    pairs, blk = mixed.shape[:2]
    macs = 2 * pairs * blk * blk * blk
    return pl.pallas_call(
        functools.partial(pair_kernel, len(own)),
        out_shape=[jax.ShapeDtypeStruct((nb, blk, blk), F32)] * 2
        + [jax.ShapeDtypeStruct((nb, blk, blk), BF16)] * (2 * groups - 2),
        in_specs=[SMEM, SMEM] + [VMEM] * (1 + len(own) + len(others)),
        out_specs=[VMEM] * (2 * groups),
        scratch_shapes=[pltpu.VMEM((2 * groups * nb, blk, blk), F32)],
        compiler_params=pltpu.CompilerParams(vmem_limit_bytes=VMEM_LIMIT),
        cost_estimate=pl.CostEstimate(flops=2 * macs, bytes_accessed=10 << 20, transcendentals=0),
        name="pair_sums",
    )(slots, dims, mixed, *own, *others)


def per_device(secs, terms, env_blocks, core_blocks, mpo_coeffs, pair_left, pair_right, block_dims):
    nx, nz = secs // 2, terms // 2
    half_z = nz // 2
    nb, blk = env_blocks.shape[1], env_blocks.shape[2]
    pairs_local, rows = core_blocks.shape[0], core_blocks.shape[1]
    piece_pairs = pairs_local // nz
    sec, term = lax.axis_index("sec"), lax.axis_index("term")
    x, c, z, y = sec // 2, sec % 2, term // 2, term % 2
    top, rest = z // half_z, z % half_z

    def send(value, to):
        perm = []
        for s in range(secs):
            for t in range(terms):
                d = to(s // 2, s % 2, t // 2, t % 2)
                if d is not None and d != (s // 2, s % 2, t // 2, t % 2):
                    perm.append((s * terms + t, (d[0] * 2 + d[1]) * terms + d[2] * 2 + d[3]))
        return lax.ppermute(value, ("sec", "term"), perm)

    def other_core(value):
        return send(value, lambda x, c, z, y: (x, 1 - c, z, y))

    def other_y(value):
        return send(value, lambda x, c, z, y: (x, c, z, 1 - y))

    facts = jnp.concatenate(
        [
            mpo_coeffs.reshape(-1, pairs_local).astype(F32),
            pair_left[None].astype(F32),
            pair_right[None].astype(F32),
        ]
    )

    parts = core_blocks.reshape(half_z, 2, piece_pairs, rows, blk)
    keep = lax.dynamic_index_in_dim(parts, c, 1, keepdims=False)
    got = other_core(lax.dynamic_index_in_dim(parts, 1 - c, 1, keepdims=False))
    pieces = []
    for d in range(nz):
        to = z ^ d
        mine, theirs = (
            lax.dynamic_index_in_dim(v, to % half_z, 0, keepdims=False) for v in (keep, got)
        )
        pieces.append(jnp.where(to // half_z == c, mine, theirs))
    got = send(
        env_blocks[0],
        lambda x, c, z, y: (x, 1 - c, z ^ half_z, y) if c != z // half_z else None,
    )
    early = [send(v, lambda x, c, z, y: (x, c, z ^ d, y)) if d else v for d, v in enumerate(pieces)]
    late = [other_y(v) for v in early]

    got, late[0] = lax.optimization_barrier((got, late[0]))
    envs = [jnp.where(c == top, env_blocks[0], got)]
    near = z ^ jnp.where(c == top, 0, half_z)
    from_z, from_y = [0], [0]
    bit = 1
    while bit < half_z:
        envs += [send(v, lambda x, c, z, y: (x, c, z ^ bit, y)) for v in envs]
        from_z += [a ^ bit for a in from_z]
        bit *= 2
    envs += [other_y(v) for v in envs]
    from_y = [0] * len(from_z) + [1] * len(from_z)
    from_z = from_z * 2
    envs += [other_core(v) for v in envs]
    from_y = from_y * 2
    from_z = from_z + [a ^ half_z for a in from_z]
    env_terms = jnp.stack([2 * (near ^ a) + (y ^ b) for a, b in zip(from_z, from_y)])

    facts = jnp.where(c == top, facts, other_core(facts))
    facts = jnp.concatenate(
        [
            lax.dynamic_slice_in_dim(facts, (2 * rest + k) * piece_pairs, piece_pairs, 1)
            for k in (c, 1 - c)
        ],
        axis=1,
    )
    left, right = facts[-2].astype(jnp.int32), facts[-1].astype(jnp.int32)
    coeffs = facts[:-2].reshape(mpo_coeffs.shape[0], mpo_coeffs.shape[1], -1)
    ids = jnp.arange(block_dims.shape[0])
    left_dims = jnp.sum(
        jnp.where(((x * 2 + top) * nb + jnp.arange(nb))[:, None] == ids, block_dims, 0), axis=1
    )
    to_sec, to_block = right // nb, right % nb
    slots = (((to_sec // 2) ^ x) * 2 + ((to_sec % 2) ^ top)) * nb + to_block
    places = jnp.arange(secs * nb)
    slot_sec = ((places // (2 * nb)) ^ x) * 2 + ((places // nb % 2) ^ top)
    slot_dims = jnp.sum(
        jnp.where((slot_sec * nb + places % nb)[:, None] == ids, block_dims, 0), axis=1
    )

    mine = jnp.stack([2 * (c * half_z + (rest ^ t)) + y for t in range(half_z)])
    pick_w = (env_terms[:, None] == jnp.arange(mpo_coeffs.shape[0])).astype(BF16)
    pick_v = (mine[:, None] == jnp.arange(mpo_coeffs.shape[1])).astype(BF16)
    weights = jnp.einsum("nw,wvp->nvp", pick_w, coeffs.astype(BF16), preferred_element_type=F32)
    weights = jnp.einsum("tv,nvp->tpn", pick_v, weights.astype(BF16), preferred_element_type=F32)
    onehot = left[:, None] == jnp.arange(nb)
    weights = jnp.where(onehot[None, :, None, :], weights[..., None], 0.0).astype(BF16)
    weights = weights.reshape(half_z * left.shape[0], -1)
    flip = z * 2 * rows + (y * rows if rows % TILE == 0 else 0)
    flip = flip[None].astype(jnp.int32)
    mixed = mix_envs(flip, left_dims, weights, envs, half_z)

    early = lax.optimization_barrier(tuple(early))
    early_others = [other_core(v) for v in early]
    late, early_others = lax.optimization_barrier((late, early_others))
    late_others = [other_core(v) for v in late]
    own = list(zip(early, late))
    others = list(zip(early_others, late_others))
    if rows % TILE:
        own, others = (
            [[jnp.where(y == 0, jnp.concatenate(v, 1), jnp.concatenate(v[::-1], 1))] for v in group]
            for group in (own, others)
        )
    own = [v for pair in own for v in pair]
    others = [v for pair in others for v in pair]

    sums = {}
    for t in reversed(range(half_z)):
        parts = pair_sums(slots, slot_dims, mixed[t], own, others, nx, nb)
        for b in range(2):
            part = parts[b]
            for f in range(1, nx):
                got = send(parts[2 * f + b], lambda x, c, z, y: (x ^ f, c, z, y))
                part = part + got.astype(F32)
            sums[t, b] = part
    bit = 1
    while bit < half_z:
        for t, b in [at for at in sums if at[0] & bit]:
            got = send(sums.pop((t, b)).astype(BF16), lambda x, c, z, y: (x, c, z ^ bit, y))
            sums[t ^ bit, b] = sums[t ^ bit, b] + got.astype(F32)
        bit *= 2
    result = jnp.where(c == top, sums[0, 0], 0.0)
    for b in range(2):
        got = send(
            sums[0, b].astype(BF16),
            lambda x, c, z, y: (x, (z // half_z) ^ b, c * half_z + z % half_z, y),
        )
        result = result + got.astype(F32)
    return result[None]


def solution(mesh):
    return jax.shard_map(
        functools.partial(per_device, mesh.shape["sec"], mesh.shape["term"]),
        mesh=mesh,
        in_specs=(
            P("term", "sec", None, None),
            P("sec", "term", None),
            P(None, None, "sec"),
            P("sec"),
            P("sec"),
            P(),
        ),
        out_specs=P("term", "sec", None, None),
        check_vma=False,
    )
```

time: 123 us -> 101 us (0.82)
  the two profiles are of different devices: /device:TPU:0 before, /device:TPU:1 now
where the time goes in v3:
time: 101 us
  waiting for transfers between devices  42.9 us (42%)
  starting transfers between devices  38.2 us (38%)
  Pallas kernels  11.5 us (11%)
  other arithmetic  6.16 us (6%)
  local copies, waits for them, and re-layouts  1.45 us (1%)
    ppermute x33, waiting for transfers between devices, send(): return lax.ppermute(value, ('sec', 'term'), perm)  42.9 us
    ppermute x33, starting transfers between devices, send(): return lax.ppermute(value, ('sec', 'term'), perm)  38.2 us
    pallas_call x2, Pallas kernels, pair_sums(): pl.pallas_call(functools.partial(pair_kernel, len(own)), out_shape=[jax.S...  7.12 us
    pallas_call x1, Pallas kernels, mix_envs(): pl.pallas_call(functools.partial(mix_kernel, len(envs)), out_shape=[jax.S...  4.37 us
  transfers between devices with their start and end apart: 33, of which 11 were waited for; matrix products, arithmetic and copies ran while one was open for 5% of the time, Pallas kernels for 8%

profile of v3, /device:TPU:1, one launch (start us, length us, event | category | flops | bytes accessed | tf_op | source)
XLA Modules:
  0.0 101.0 jit_solution(376573428453193250)
XLA Ops:
  1.6 5.6 %collective-permute-start.1 = (bf16[2,256,256]{2,1,0:T(8,128)(2,1)}, bf16[2,256,256]{2,1,0:T(8,128)(2,1)S(1)}, u32[]{:S(2)}, u32[]{:S(2)}) collective-permute-start(bf16[2,256,256]{2,1,0:T(8,128)(2,1)} %bitcast.70), channel_id=1, source_target_pairs={{4,8},{5,9},{6,10},{7,11},{8,4},{9,5},{10,6},{11,7},{20,24},{21,25... | collective-permute-start | bytes 786440 | tf_op jit(solution)/shard_map/ppermute | solution.py:151
  10.5 1.3 %bitcast_select_fusion = (bf16[16,32,256]{2,1,0:T(8,128)(2,1)S(1)}, bf16[16,32,256]{2,1,0:T(8,128)(2,1)S(1)}, bf16[16,32,256]{2,1,0:T(8,128)(2,1)S(1)}, bf16[16,32,256]{2,1,0:T(8,128)(2,1)S(1)}) fusion(bf16[2,16,32,256]{3,2,1,0:T(8,128)(2,1)S(1)} %collective-permute-done.2, s32[]{:T(128)S(6)} %select_n.261, bf16[2,2,16,32,256]{4,3,2,1,0:T(8,128)(2,1)} %bitcast.69, ...), kind=kLoop, calls=%fused_computation.8 | loop fusion | flops 524288 | bytes 3145768 | tf_op jit(solution)/shard_map/jit(_where)/select_n | solution.py:176
  11.8 1.3 %collective-permute-start.3 = (bf16[16,32,256]{2,1,0:T(8,128)(2,1)S(1)}, bf16[16,32,256]{2,1,0:T(8,128)(2,1)S(1)}, u32[]{:S(2)}, u32[]{:S(2)}) collective-permute-start(bf16[16,32,256]{2,1,0:T(8,128)(2,1)S(1)} %get-tuple-element.31.refs_0_), channel_id=1, source_target_pairs={{0,1},{1,0},{2,3},{3,2},{4,5},{5,4},{6,7},{7,6},{8,9},{9,8},{10,11... | collective-permute-start | bytes 786440 | tf_op jit(solution)/shard_map/ppermute | solution.py:151
  13.1 1.4 %collective-permute-start.11 = (bf16[16,32,256]{2,1,0:T(8,128)(2,1)S(1)}, bf16[16,32,256]{2,1,0:T(8,128)(2,1)S(1)}, u32[]{:S(2)}, u32[]{:S(2)}) collective-permute-start(bf16[16,32,256]{2,1,0:T(8,128)(2,1)S(1)} %get-tuple-element.55), channel_id=1, source_target_pairs={{0,2},{1,3},{2,0},{3,1},{4,6},{5,7},{6,4},{7,5},{8,10},{9,11},{10,... | collective-permute-start | bytes 786440 | tf_op jit(solution)/shard_map/ppermute | solution.py:151
  14.9 2.0 %collective-permute-start.13 = (bf16[16,32,256]{2,1,0:T(8,128)(2,1)S(1)}, bf16[16,32,256]{2,1,0:T(8,128)(2,1)S(1)}, u32[]{:S(2)}, u32[]{:S(2)}) collective-permute-start(bf16[16,32,256]{2,1,0:T(8,128)(2,1)S(1)} %get-tuple-element.53), channel_id=1, source_target_pairs={{0,6},{1,7},{2,4},{3,5},{4,2},{5,3},{6,0},{7,1},{8,14},{9,15},{10,... | collective-permute-start | bytes 786440 | tf_op jit(solution)/shard_map/ppermute | solution.py:151
  16.9 2.6 %collective-permute-done.3.refs_1_ = bf16[16,32,256]{2,1,0:T(8,128)(2,1)S(1)} collective-permute-done((bf16[16,32,256]{2,1,0:T(8,128)(2,1)S(1)}, bf16[16,32,256]{2,1,0:T(8,128)(2,1)S(1)}, u32[]{:S(2)}, u32[]{:S(2)}) %collective-permute-start.3) | collective-permute-done | bytes 262176 | tf_op jit(solution)/shard_map/ppermute | solution.py:151
  19.5 1.4 %collective-permute-start.4 = (bf16[2,256,256]{2,1,0:T(8,128)(2,1)S(1)}, bf16[2,256,256]{2,1,0:T(8,128)(2,1)}, u32[]{:S(2)}, u32[]{:S(2)}) collective-permute-start(bf16[2,256,256]{2,1,0:T(8,128)(2,1)S(1)} %broadcast_select_fusion.refs_0_), channel_id=1, source_target_pairs={{0,2},{1,3},{2,0},{3,1},{4,6},{5,7},{6,4},{7,5},{8,10},{9,11},{10,... | collective-permute-start | bytes 786440 | tf_op jit(solution)/shard_map/ppermute | solution.py:151
  22.1 1.7 %collective-permute-done.11.refs_2_ = bf16[16,32,256]{2,1,0:T(8,128)(2,1)S(1)} collective-permute-done((bf16[16,32,256]{2,1,0:T(8,128)(2,1)S(1)}, bf16[16,32,256]{2,1,0:T(8,128)(2,1)S(1)}, u32[]{:S(2)}, u32[]{:S(2)}) %collective-permute-start.11) | collective-permute-done | bytes 262176 | tf_op jit(solution)/shard_map/ppermute | solution.py:151
  24.0 9.8 %collective-permute-done.12.refs_4_ = bf16[16,32,256]{2,1,0:T(8,128)(2,1)S(1)} collective-permute-done((bf16[16,32,256]{2,1,0:T(8,128)(2,1)S(1)}, bf16[16,32,256]{2,1,0:T(8,128)(2,1)S(1)}, u32[]{:S(2)}, u32[]{:S(2)}) %collective-permute-start.12) | collective-permute-done | bytes 262176 | tf_op jit(solution)/shard_map/ppermute | solution.py:151
  34.3 3.3 %collective-permute-start.17 = (bf16[16,32,256]{2,1,0:T(8,128)(2,1)S(1)}, bf16[16,32,256]{2,1,0:T(8,128)(2,1)S(1)}, u32[]{:S(2)}, u32[]{:S(2)}) collective-permute-start(bf16[16,32,256]{2,1,0:T(8,128)(2,1)S(1)} %get-tuple-element.31.refs_0_), channel_id=1, source_target_pairs={{0,8},{1,9},{2,10},{3,11},{4,12},{5,13},{6,14},{7,15},{8,0},{9,1},... | collective-permute-start | bytes 786440 | tf_op jit(solution)/shard_map/ppermute | solution.py:151
  40.7 6.7 %collective-permute-done.16.refs_7_ = bf16[16,32,256]{2,1,0:T(8,128)(2,1)S(1)} collective-permute-done((bf16[16,32,256]{2,1,0:T(8,128)(2,1)S(1)}, bf16[16,32,256]{2,1,0:T(8,128)(2,1)S(1)}, u32[]{:S(2)}, u32[]{:S(2)}) %collective-permute-start.16) | collective-permute-done | bytes 262176 | tf_op jit(solution)/shard_map/ppermute | solution.py:151
  47.3 2.6 %collective-permute-start.7 = (bf16[2,256,256]{2,1,0:T(8,128)(2,1)S(1)}, bf16[2,256,256]{2,1,0:T(8,128)(2,1)}, u32[]{:S(2)}, u32[]{:S(2)}) collective-permute-start(bf16[2,256,256]{2,1,0:T(8,128)(2,1)S(1)} %broadcast_select_fusion.refs_0_), channel_id=1, source_target_pairs={{0,8},{1,9},{2,10},{3,11},{4,12},{5,13},{6,14},{7,15},{8,0},{9,1},... | collective-permute-start | bytes 786440 | tf_op jit(solution)/shard_map/ppermute | solution.py:151
  50.6 2.5 %collective-permute-done.6.refs_3_ = bf16[2,256,256]{2,1,0:T(8,128)(2,1)} collective-permute-done((bf16[2,256,256]{2,1,0:T(8,128)(2,1)}, bf16[2,256,256]{2,1,0:T(8,128)(2,1)}, u32[]{:S(2)}, u32[]{:S(2)}) %collective-permute-start.6) | collective-permute-done | bytes 262176 | tf_op jit(solution)/shard_map/ppermute | solution.py:151
  53.0 1.5 %collective-permute-start.10 = (bf16[2,256,256]{2,1,0:T(8,128)(2,1)}, bf16[2,256,256]{2,1,0:T(8,128)(2,1)}, u32[]{:S(2)}, u32[]{:S(2)}) collective-permute-start(bf16[2,256,256]{2,1,0:T(8,128)(2,1)} %collective-permute-done.6.refs_3_), channel_id=1, source_target_pairs={{0,8},{1,9},{2,10},{3,11},{4,12},{5,13},{6,14},{7,15},{8,0},{9,1},... | collective-permute-start | bytes 786440 | tf_op jit(solution)/shard_map/ppermute | solution.py:151
  56.1 4.4 %mix_envs.1 = (bf16[32,256,256]{2,1,0:T(8,128)(2,1)S(1)}, bf16[32,256,256]{2,1,0:T(8,128)(2,1)S(1)}) custom-call(s32[1]{0:T(128)} %bitcast.4.flip, s32[2]{0:T(128)S(1)} %fusion.10.dims, bf16[64,16]{1,0:T(8,128)(2,1)S(1)} %copy.22.weights, bf16[2,256,256]{2,1,0:T(8,128)(2,1)S(1)} %broadcast_select_fusion.refs_0_, ...), custom_call_target="tpu_custom_call" | custom-call | flops 2147483648 | bytes 10485760 | tf_op jit(solution)/shard_map/mix_envs/pallas_call | solution.py:103
  60.5 3.6 %pair_sums.3 = (f32[2,256,256]{2,1,0:T(8,128)S(1)}, f32[2,256,256]{2,1,0:T(8,128)S(1)}, bf16[2,256,256]{2,1,0:T(8,128)(2,1)S(1)}, bf16[2,256,256]{2,1,0:T(8,128)(2,1)S(1)}) custom-call(s32[32]{0:T(128)S(1)} %fusion.13.slots, s32[8]{0:T(128)S(1)} %select_reduce_fusion.dims, bf16[32,256,256]{2,1,0:T(8,128)(2,1)S(1)} %get-tuple-element.46.mixed, ...), custom_call_target="tpu_custom_call" | custom-call | flops 2147483648 | bytes 10485760 | tf_op jit(solution)/shard_map/pair_sums/pallas_call | solution.py:121
  65.6 3.6 %pair_sums.2 = (f32[2,256,256]{2,1,0:T(8,128)S(1)}, f32[2,256,256]{2,1,0:T(8,128)S(1)}, bf16[2,256,256]{2,1,0:T(8,128)(2,1)S(1)}, bf16[2,256,256]{2,1,0:T(8,128)(2,1)S(1)}) custom-call(s32[32]{0:T(128)S(1)} %fusion.13.slots, s32[8]{0:T(128)S(1)} %select_reduce_fusion.dims, bf16[32,256,256]{2,1,0:T(8,128)(2,1)S(1)} %get-tuple-element.30.mixed, ...), custom_call_target="tpu_custom_call" | custom-call | flops 2147483648 | bytes 10485760 | tf_op jit(solution)/shard_map/pair_sums/pallas_call | solution.py:121
  71.7 1.9 %collective-permute-start.31 = (bf16[2,256,256]{2,1,0:T(8,128)(2,1)S(1)}, bf16[2,256,256]{2,1,0:T(8,128)(2,1)S(1)}, u32[]{:S(2)}, u32[]{:S(2)}) collective-permute-start(bf16[2,256,256]{2,1,0:T(8,128)(2,1)S(1)} %add_convert_fusion.1), channel_id=1, source_target_pairs={{0,2},{1,3},{2,0},{3,1},{4,6},{5,7},{6,4},{7,5},{8,10},{9,11},{10,... | collective-permute-start | bytes 786440 | tf_op jit(solution)/shard_map/ppermute | solution.py:151
  74.8 2.4 %collective-permute-done.26 = bf16[2,256,256]{2,1,0:T(8,128)(2,1)S(1)} collective-permute-done((bf16[2,256,256]{2,1,0:T(8,128)(2,1)S(1)}, bf16[2,256,256]{2,1,0:T(8,128)(2,1)S(1)}, u32[]{:S(2)}, u32[]{:S(2)}) %collective-permute-start.26) | collective-permute-done | bytes 262176 | tf_op jit(solution)/shard_map/ppermute | solution.py:151
  77.3 1.9 %collective-permute-start.27 = (bf16[2,256,256]{2,1,0:T(8,128)(2,1)S(1)}, bf16[2,256,256]{2,1,0:T(8,128)(2,1)S(1)}, u32[]{:S(2)}, u32[]{:S(2)}) collective-permute-start(bf16[2,256,256]{2,1,0:T(8,128)(2,1)S(1)} %add_convert_fusion.2), channel_id=1, source_target_pairs={{0,2},{1,3},{2,0},{3,1},{4,6},{5,7},{6,4},{7,5},{8,10},{9,11},{10,... | collective-permute-start | bytes 786440 | tf_op jit(solution)/shard_map/ppermute | solution.py:151
  79.3 3.6 %collective-permute-done.29 = bf16[2,256,256]{2,1,0:T(8,128)(2,1)S(1)} collective-permute-done((bf16[2,256,256]{2,1,0:T(8,128)(2,1)S(1)}, bf16[2,256,256]{2,1,0:T(8,128)(2,1)S(1)}, u32[]{:S(2)}, u32[]{:S(2)}) %collective-permute-start.29) | collective-permute-done | bytes 262176 | tf_op jit(solution)/shard_map/ppermute | solution.py:151
  83.9 4.6 %collective-permute-done.25 = bf16[2,256,256]{2,1,0:T(8,128)(2,1)S(1)} collective-permute-done((bf16[2,256,256]{2,1,0:T(8,128)(2,1)S(1)}, bf16[2,256,256]{2,1,0:T(8,128)(2,1)S(1)}, u32[]{:S(2)}, u32[]{:S(2)}) %collective-permute-start.25) | collective-permute-done | bytes 262176 | tf_op jit(solution)/shard_map/ppermute | solution.py:151
  88.6 3.8 %collective-permute-start.28 = (bf16[2,256,256]{2,1,0:T(8,128)(2,1)S(1)}, bf16[2,256,256]{2,1,0:T(8,128)(2,1)S(1)}, u32[]{:S(2)}, u32[]{:S(2)}) collective-permute-start(bf16[2,256,256]{2,1,0:T(8,128)(2,1)S(1)} %fusion), channel_id=1, source_target_pairs={{4,8},{5,9},{6,10},{7,11},{8,4},{9,5},{10,6},{11,7},{20,24},{21,25... | collective-permute-start | bytes 786440 | tf_op jit(solution)/shard_map/ppermute | solution.py:151
  92.4 7.6 %collective-permute-done.28 = bf16[2,256,256]{2,1,0:T(8,128)(2,1)S(1)} collective-permute-done((bf16[2,256,256]{2,1,0:T(8,128)(2,1)S(1)}, bf16[2,256,256]{2,1,0:T(8,128)(2,1)S(1)}, u32[]{:S(2)}, u32[]{:S(2)}) %collective-permute-start.28) | collective-permute-done | bytes 262176 | tf_op jit(solution)/shard_map/ppermute | solution.py:151
  (75 shorter events, 19.6 us)
Async XLA Ops:
  1.5 11.6 %collective-permute-start = (f32[66,64]{1,0:T(8,128)S(1)}, f32[66,64]{1,0:T(8,128)S(1)}, u32[]{:S(2)}, u32[]{:S(2)}) collective-permute-start(f32[66,64]{1,0:T(8,128)S(1)} %pad_maximum_fusion), channel_id=1, source_target_pairs={{0,8},{1,9},{2,10},{3,11},{4,12},{5,13},{6,14},{7,15},{8,0},{9,1},... | collective-permute-start | bytes 50696 | tf_op jit(solution)/shard_map/ppermute | solution.py:151
  1.6 15.3 %collective-permute-start.1 = (bf16[2,256,256]{2,1,0:T(8,128)(2,1)}, bf16[2,256,256]{2,1,0:T(8,128)(2,1)S(1)}, u32[]{:S(2)}, u32[]{:S(2)}) collective-permute-start(bf16[2,256,256]{2,1,0:T(8,128)(2,1)} %bitcast.70), channel_id=1, source_target_pairs={{4,8},{5,9},{6,10},{7,11},{8,4},{9,5},{10,6},{11,7},{20,24},{21,25... | collective-permute-start | bytes 786440 | tf_op jit(solution)/shard_map/ppermute | solution.py:151
  11.8 7.7 %collective-permute-start.3 = (bf16[16,32,256]{2,1,0:T(8,128)(2,1)S(1)}, bf16[16,32,256]{2,1,0:T(8,128)(2,1)S(1)}, u32[]{:S(2)}, u32[]{:S(2)}) collective-permute-start(bf16[16,32,256]{2,1,0:T(8,128)(2,1)S(1)} %get-tuple-element.31.refs_0_), channel_id=1, source_target_pairs={{0,1},{1,0},{2,3},{3,2},{4,5},{5,4},{6,7},{7,6},{8,9},{9,8},{10,11... | collective-permute-start | bytes 786440 | tf_op jit(solution)/shard_map/ppermute | solution.py:151
  13.1 10.7 %collective-permute-start.11 = (bf16[16,32,256]{2,1,0:T(8,128)(2,1)S(1)}, bf16[16,32,256]{2,1,0:T(8,128)(2,1)S(1)}, u32[]{:S(2)}, u32[]{:S(2)}) collective-permute-start(bf16[16,32,256]{2,1,0:T(8,128)(2,1)S(1)} %get-tuple-element.55), channel_id=1, source_target_pairs={{0,2},{1,3},{2,0},{3,1},{4,6},{5,7},{6,4},{7,5},{8,10},{9,11},{10,... | collective-permute-start | bytes 786440 | tf_op jit(solution)/shard_map/ppermute | solution.py:151
  14.5 19.3 %collective-permute-start.12 = (bf16[16,32,256]{2,1,0:T(8,128)(2,1)S(1)}, bf16[16,32,256]{2,1,0:T(8,128)(2,1)S(1)}, u32[]{:S(2)}, u32[]{:S(2)}) collective-permute-start(bf16[16,32,256]{2,1,0:T(8,128)(2,1)S(1)} %get-tuple-element.54), channel_id=1, source_target_pairs={{0,4},{1,5},{2,6},{3,7},{4,0},{5,1},{6,2},{7,3},{8,12},{9,13},{10,... | collective-permute-start | bytes 786440 | tf_op jit(solution)/shard_map/ppermute | solution.py:151
  14.9 19.4 %collective-permute-start.13 = (bf16[16,32,256]{2,1,0:T(8,128)(2,1)S(1)}, bf16[16,32,256]{2,1,0:T(8,128)(2,1)S(1)}, u32[]{:S(2)}, u32[]{:S(2)}) collective-permute-start(bf16[16,32,256]{2,1,0:T(8,128)(2,1)S(1)} %get-tuple-element.53), channel_id=1, source_target_pairs={{0,6},{1,7},{2,4},{3,5},{4,2},{5,3},{6,0},{7,1},{8,14},{9,15},{10,... | collective-permute-start | bytes 786440 | tf_op jit(solution)/shard_map/ppermute | solution.py:151
  19.5 18.1 %collective-permute-start.4 = (bf16[2,256,256]{2,1,0:T(8,128)(2,1)S(1)}, bf16[2,256,256]{2,1,0:T(8,128)(2,1)}, u32[]{:S(2)}, u32[]{:S(2)}) collective-permute-start(bf16[2,256,256]{2,1,0:T(8,128)(2,1)S(1)} %broadcast_select_fusion.refs_0_), channel_id=1, source_target_pairs={{0,2},{1,3},{2,0},{3,1},{4,6},{5,7},{6,4},{7,5},{8,10},{9,11},{10,... | collective-permute-start | bytes 786440 | tf_op jit(solution)/shard_map/ppermute | solution.py:151
  20.9 18.0 %collective-permute-start.5 = (bf16[2,256,256]{2,1,0:T(8,128)(2,1)S(1)}, bf16[2,256,256]{2,1,0:T(8,128)(2,1)}, u32[]{:S(2)}, u32[]{:S(2)}) collective-permute-start(bf16[2,256,256]{2,1,0:T(8,128)(2,1)S(1)} %broadcast_select_fusion.refs_0_), channel_id=1, source_target_pairs={{0,1},{1,0},{2,3},{3,2},{4,5},{5,4},{6,7},{7,6},{8,9},{9,8},{10,11... | collective-permute-start | bytes 786440 | tf_op jit(solution)/shard_map/ppermute | solution.py:151
  23.8 15.1 %collective-permute-start.14 = (bf16[16,32,256]{2,1,0:T(8,128)(2,1)S(1)}, bf16[16,32,256]{2,1,0:T(8,128)(2,1)S(1)}, u32[]{:S(2)}, u32[]{:S(2)}) collective-permute-start(bf16[16,32,256]{2,1,0:T(8,128)(2,1)S(1)} %collective-permute-done.11.refs_2_), channel_id=1, source_target_pairs={{0,1},{1,0},{2,3},{3,2},{4,5},{5,4},{6,7},{7,6},{8,9},{9,8},{10,11... | collective-permute-start | bytes 786440 | tf_op jit(solution)/shard_map/ppermute | solution.py:151
  34.3 15.7 %collective-permute-start.17 = (bf16[16,32,256]{2,1,0:T(8,128)(2,1)S(1)}, bf16[16,32,256]{2,1,0:T(8,128)(2,1)S(1)}, u32[]{:S(2)}, u32[]{:S(2)}) collective-permute-start(bf16[16,32,256]{2,1,0:T(8,128)(2,1)S(1)} %get-tuple-element.31.refs_0_), channel_id=1, source_target_pairs={{0,8},{1,9},{2,10},{3,11},{4,12},{5,13},{6,14},{7,15},{8,0},{9,1},... | collective-permute-start | bytes 786440 | tf_op jit(solution)/shard_map/ppermute | solution.py:151
  37.6 12.4 %collective-permute-start.18 = (bf16[16,32,256]{2,1,0:T(8,128)(2,1)S(1)}, bf16[16,32,256]{2,1,0:T(8,128)(2,1)S(1)}, u32[]{:S(2)}, u32[]{:S(2)}) collective-permute-start(bf16[16,32,256]{2,1,0:T(8,128)(2,1)S(1)} %collective-permute-done.11.refs_2_), channel_id=1, source_target_pairs={{0,8},{1,9},{2,10},{3,11},{4,12},{5,13},{6,14},{7,15},{8,0},{9,1},... | collective-permute-start | bytes 786440 | tf_op jit(solution)/shard_map/ppermute | solution.py:151
  38.9 11.6 %collective-permute-start.19 = (bf16[16,32,256]{2,1,0:T(8,128)(2,1)S(1)}, bf16[16,32,256]{2,1,0:T(8,128)(2,1)S(1)}, u32[]{:S(2)}, u32[]{:S(2)}) collective-permute-start(bf16[16,32,256]{2,1,0:T(8,128)(2,1)S(1)} %collective-permute-done.12.refs_4_), channel_id=1, source_target_pairs={{0,8},{1,9},{2,10},{3,11},{4,12},{5,13},{6,14},{7,15},{8,0},{9,1},... | collective-permute-start | bytes 786440 | tf_op jit(solution)/shard_map/ppermute | solution.py:151
  38.9 8.5 %collective-permute-start.16 = (bf16[16,32,256]{2,1,0:T(8,128)(2,1)S(1)}, bf16[16,32,256]{2,1,0:T(8,128)(2,1)S(1)}, u32[]{:S(2)}, u32[]{:S(2)}) collective-permute-start(bf16[16,32,256]{2,1,0:T(8,128)(2,1)S(1)} %collective-permute-done.13.refs_6_), channel_id=1, source_target_pairs={{0,1},{1,0},{2,3},{3,2},{4,5},{5,4},{6,7},{7,6},{8,9},{9,8},{10,11... | collective-permute-start | bytes 786440 | tf_op jit(solution)/shard_map/ppermute | solution.py:151
  39.5 13.5 %collective-permute-start.6 = (bf16[2,256,256]{2,1,0:T(8,128)(2,1)}, bf16[2,256,256]{2,1,0:T(8,128)(2,1)}, u32[]{:S(2)}, u32[]{:S(2)}) collective-permute-start(bf16[2,256,256]{2,1,0:T(8,128)(2,1)} %collective-permute-done.4.refs_1_), channel_id=1, source_target_pairs={{0,1},{1,0},{2,3},{3,2},{4,5},{5,4},{6,7},{7,6},{8,9},{9,8},{10,11... | collective-permute-start | bytes 786440 | tf_op jit(solution)/shard_map/ppermute | solution.py:151
  47.3 7.5 %collective-permute-start.7 = (bf16[2,256,256]{2,1,0:T(8,128)(2,1)S(1)}, bf16[2,256,256]{2,1,0:T(8,128)(2,1)}, u32[]{:S(2)}, u32[]{:S(2)}) collective-permute-start(bf16[2,256,256]{2,1,0:T(8,128)(2,1)S(1)} %broadcast_select_fusion.refs_0_), channel_id=1, source_target_pairs={{0,8},{1,9},{2,10},{3,11},{4,12},{5,13},{6,14},{7,15},{8,0},{9,1},... | collective-permute-start | bytes 786440 | tf_op jit(solution)/shard_map/ppermute | solution.py:151
  54.8 5.7 %collective-permute-start.21 = (bf16[16,32,256]{2,1,0:T(8,128)(2,1)S(1)}, bf16[16,32,256]{2,1,0:T(8,128)(2,1)S(1)}, u32[]{:S(2)}, u32[]{:S(2)}) collective-permute-start(bf16[16,32,256]{2,1,0:T(8,128)(2,1)S(1)} %collective-permute-done.3.refs_1_), channel_id=1, source_target_pairs={{0,8},{1,9},{2,10},{3,11},{4,12},{5,13},{6,14},{7,15},{8,0},{9,1},... | collective-permute-start | bytes 786440 | tf_op jit(solution)/shard_map/ppermute | solution.py:151
  64.1 7.6 %collective-permute-start.30 = (bf16[2,256,256]{2,1,0:T(8,128)(2,1)S(1)}, bf16[2,256,256]{2,1,0:T(8,128)(2,1)S(1)}, u32[]{:S(2)}, u32[]{:S(2)}) collective-permute-start(bf16[2,256,256]{2,1,0:T(8,128)(2,1)S(1)} %get-tuple-element.52), channel_id=1, source_target_pairs={{0,16},{1,17},{2,18},{3,19},{4,20},{5,21},{6,22},{7,23},{8,24},{9,... | collective-permute-start | bytes 786440 | tf_op jit(solution)/shard_map/ppermute | solution.py:151
  65.3 11.9 %collective-permute-start.26 = (bf16[2,256,256]{2,1,0:T(8,128)(2,1)S(1)}, bf16[2,256,256]{2,1,0:T(8,128)(2,1)S(1)}, u32[]{:S(2)}, u32[]{:S(2)}) collective-permute-start(bf16[2,256,256]{2,1,0:T(8,128)(2,1)S(1)} %get-tuple-element.48), channel_id=1, source_target_pairs={{0,16},{1,17},{2,18},{3,19},{4,20},{5,21},{6,22},{7,23},{8,24},{9,... | collective-permute-start | bytes 786440 | tf_op jit(solution)/shard_map/ppermute | solution.py:151
  69.2 13.7 %collective-permute-start.29 = (bf16[2,256,256]{2,1,0:T(8,128)(2,1)S(1)}, bf16[2,256,256]{2,1,0:T(8,128)(2,1)S(1)}, u32[]{:S(2)}, u32[]{:S(2)}) collective-permute-start(bf16[2,256,256]{2,1,0:T(8,128)(2,1)S(1)} %get-tuple-element.50), channel_id=1, source_target_pairs={{0,16},{1,17},{2,18},{3,19},{4,20},{5,21},{6,22},{7,23},{8,24},{9,... | collective-permute-start | bytes 786440 | tf_op jit(solution)/shard_map/ppermute | solution.py:151
  71.7 11.2 %collective-permute-start.31 = (bf16[2,256,256]{2,1,0:T(8,128)(2,1)S(1)}, bf16[2,256,256]{2,1,0:T(8,128)(2,1)S(1)}, u32[]{:S(2)}, u32[]{:S(2)}) collective-permute-start(bf16[2,256,256]{2,1,0:T(8,128)(2,1)S(1)} %add_convert_fusion.1), channel_id=1, source_target_pairs={{0,2},{1,3},{2,0},{3,1},{4,6},{5,7},{6,4},{7,5},{8,10},{9,11},{10,... | collective-permute-start | bytes 786440 | tf_op jit(solution)/shard_map/ppermute | solution.py:151
  73.6 14.9 %collective-permute-start.25 = (bf16[2,256,256]{2,1,0:T(8,128)(2,1)S(1)}, bf16[2,256,256]{2,1,0:T(8,128)(2,1)S(1)}, u32[]{:S(2)}, u32[]{:S(2)}) collective-permute-start(bf16[2,256,256]{2,1,0:T(8,128)(2,1)S(1)} %get-tuple-element.45), channel_id=1, source_target_pairs={{0,16},{1,17},{2,18},{3,19},{4,20},{5,21},{6,22},{7,23},{8,24},{9,... | collective-permute-start | bytes 786440 | tf_op jit(solution)/shard_map/ppermute | solution.py:151
  77.3 11.2 %collective-permute-start.27 = (bf16[2,256,256]{2,1,0:T(8,128)(2,1)S(1)}, bf16[2,256,256]{2,1,0:T(8,128)(2,1)S(1)}, u32[]{:S(2)}, u32[]{:S(2)}) collective-permute-start(bf16[2,256,256]{2,1,0:T(8,128)(2,1)S(1)} %add_convert_fusion.2), channel_id=1, source_target_pairs={{0,2},{1,3},{2,0},{3,1},{4,6},{5,7},{6,4},{7,5},{8,10},{9,11},{10,... | collective-permute-start | bytes 786440 | tf_op jit(solution)/shard_map/ppermute | solution.py:151
  83.0 9.4 %collective-permute-start.32 = (bf16[2,256,256]{2,1,0:T(8,128)(2,1)S(1)}, bf16[2,256,256]{2,1,0:T(8,128)(2,1)S(1)}, u32[]{:S(2)}, u32[]{:S(2)}) collective-permute-start(bf16[2,256,256]{2,1,0:T(8,128)(2,1)S(1)} %add_convert_fusion), channel_id=1, source_target_pairs={{0,8},{1,9},{2,10},{3,11},{4,0},{5,1},{6,2},{7,3},{8,12},{9,13},{1... | collective-permute-start | bytes 786440 | tf_op jit(solution)/shard_map/ppermute | solution.py:151
  88.6 11.5 %collective-permute-start.28 = (bf16[2,256,256]{2,1,0:T(8,128)(2,1)S(1)}, bf16[2,256,256]{2,1,0:T(8,128)(2,1)S(1)}, u32[]{:S(2)}, u32[]{:S(2)}) collective-permute-start(bf16[2,256,256]{2,1,0:T(8,128)(2,1)S(1)} %fusion), channel_id=1, source_target_pairs={{4,8},{5,9},{6,10},{7,11},{8,4},{9,5},{10,6},{11,7},{20,24},{21,25... | collective-permute-start | bytes 786440 | tf_op jit(solution)/shard_map/ppermute | solution.py:151
  (10 other events, 61.2 us)

commit v4 on v3

--- a/solution.py
+++ b/solution.py
@@ -115,16 +115,15 @@
     )(flip, dims, weights, *envs)
 
 
-def pair_sums(slots, dims, mixed, own, others, groups, nb):
+def pair_sums(slots, dims, mixed, own, others, dtypes, nb):
     pairs, blk = mixed.shape[:2]
     macs = 2 * pairs * blk * blk * blk
     return pl.pallas_call(
         functools.partial(pair_kernel, len(own)),
-        out_shape=[jax.ShapeDtypeStruct((nb, blk, blk), F32)] * 2
-        + [jax.ShapeDtypeStruct((nb, blk, blk), BF16)] * (2 * groups - 2),
+        out_shape=[jax.ShapeDtypeStruct((nb, blk, blk), d) for d in dtypes],
         in_specs=[SMEM, SMEM] + [VMEM] * (1 + len(own) + len(others)),
-        out_specs=[VMEM] * (2 * groups),
-        scratch_shapes=[pltpu.VMEM((2 * groups * nb, blk, blk), F32)],
+        out_specs=[VMEM] * len(dtypes),
+        scratch_shapes=[pltpu.VMEM((len(dtypes) * nb, blk, blk), F32)],
         compiler_params=pltpu.CompilerParams(vmem_limit_bytes=VMEM_LIMIT),
         cost_estimate=pl.CostEstimate(flops=2 * macs, bytes_accessed=10 << 20, transcendentals=0),
         name="pair_sums",
@@ -184,15 +183,14 @@
     got, late[0] = lax.optimization_barrier((got, late[0]))
     envs = [jnp.where(c == top, env_blocks[0], got)]
     near = z ^ jnp.where(c == top, 0, half_z)
-    from_z, from_y = [0], [0]
+    envs += [other_y(envs[0])]
+    from_z, from_y = [0, 0], [0, 1]
     bit = 1
     while bit < half_z:
         envs += [send(v, lambda x, c, z, y: (x, c, z ^ bit, y)) for v in envs]
         from_z += [a ^ bit for a in from_z]
+        from_y = from_y * 2
         bit *= 2
-    envs += [other_y(v) for v in envs]
-    from_y = [0] * len(from_z) + [1] * len(from_z)
-    from_z = from_z * 2
     envs += [other_core(v) for v in envs]
     from_y = from_y * 2
     from_z = from_z + [a ^ half_z for a in from_z]
@@ -246,25 +244,36 @@
     own = [v for pair in own for v in pair]
     others = [v for pair in others for v in pair]
 
-    sums = {}
+    def over_x(parts):
+        kept = parts[0].astype(F32)
+        for f in range(1, nx):
+            got = send(parts[f].astype(BF16), lambda x, c, z, y: (x ^ f, c, z, y))
+            kept = kept + got.astype(F32)
+        return kept
+
+    def over_halves(terms):
+        terms, bit = dict(terms), 1
+        while bit < half_z:
+            for t in [t for t in terms if t & bit]:
+                got = send(terms.pop(t).astype(BF16), lambda x, c, z, y: (x, c, z ^ bit, y))
+                terms[t ^ bit] = terms[t ^ bit].astype(F32) + got.astype(F32)
+            bit *= 2
+        return terms[0]
+
+    first, second = {}, {}
     for t in reversed(range(half_z)):
-        parts = pair_sums(slots, slot_dims, mixed[t], own, others, nx, nb)
-        for b in range(2):
-            part = parts[b]
-            for f in range(1, nx):
-                got = send(parts[2 * f + b], lambda x, c, z, y: (x ^ f, c, z, y))
-                part = part + got.astype(F32)
-            sums[t, b] = part
-    bit = 1
-    while bit < half_z:
-        for t, b in [at for at in sums if at[0] & bit]:
-            got = send(sums.pop((t, b)).astype(BF16), lambda x, c, z, y: (x, c, z ^ bit, y))
-            sums[t ^ bit, b] = sums[t ^ bit, b] + got.astype(F32)
-        bit *= 2
-    result = jnp.where(c == top, sums[0, 0], 0.0)
+        dtypes = [F32, BF16 if t % 2 else F32] + [BF16, BF16 if t % 2 else F32] * (nx - 1)
+        parts = pair_sums(slots, slot_dims, mixed[t], own, others, dtypes, nb)
+        first[t] = over_x(parts[::2])
+        second[t] = parts[1::2]
+    sums = [
+        over_halves(first),
+        over_x([over_halves({t: v[f] for t, v in second.items()}) for f in range(nx)]),
+    ]
+    result = jnp.where(c == top, sums[0], 0.0)
     for b in range(2):
         got = send(
-            sums[0, b].astype(BF16),
+            sums[b].astype(BF16),
             lambda x, c, z, y: (x, (z // half_z) ^ b, c * half_z + z % half_z, y),
         )
         result = result + got.astype(F32)

time: 101 us -> 96.1 us (0.951)
  waiting for transfers between devices: 42.9 us -> 37.9 us
    ppermute x33, waiting for transfers between devices: 42.9 us -> 37.9 us  [send(): return lax.ppermute(value, ('sec', 'term'), perm)]
  transfers between devices with their start and end apart: 33 -> 33, of which waited for: 11 -> 10; matrix products, arithmetic and copies ran while one was open for 5% -> 6% of each run, Pallas kernels for 8% -> 8%
where the time goes in v4:
time: 96.1 us; the launch traced here: 95.8 us
  starting transfers between devices  37.9 us (39%)
  waiting for transfers between devices  37.9 us (39%)
  Pallas kernels  11.5 us (12%)
  other arithmetic  6.22 us (6%)
  local copies, waits for them, and re-layouts  1.45 us (2%)
    ppermute x33, starting transfers between devices, send(): return lax.ppermute(value, ('sec', 'term'), perm)  37.9 us
    ppermute x33, waiting for transfers between devices, send(): return lax.ppermute(value, ('sec', 'term'), perm)  37.9 us
    pallas_call x2, Pallas kernels, pair_sums(): pl.pallas_call(functools.partial(pair_kernel, len(own)), out_shape=[jax.S...  7.13 us
    pallas_call x1, Pallas kernels, mix_envs(): pl.pallas_call(functools.partial(mix_kernel, len(envs)), out_shape=[jax.S...  4.36 us
  transfers between devices with their start and end apart: 33, of which 10 were waited for; matrix products, arithmetic and copies ran while one was open for 6% of the time, Pallas kernels for 8%

profile of v4, /device:TPU:1, one launch (start us, length us, event | category | flops | bytes accessed | tf_op | source)
XLA Modules:
  0.0 95.8 jit_solution(5738295186568723067)
XLA Ops:
  1.6 5.6 %collective-permute-start.1 = (bf16[2,256,256]{2,1,0:T(8,128)(2,1)}, bf16[2,256,256]{2,1,0:T(8,128)(2,1)S(1)}, u32[]{:S(2)}, u32[]{:S(2)}) collective-permute-start(bf16[2,256,256]{2,1,0:T(8,128)(2,1)} %bitcast.70), channel_id=1, source_target_pairs={{4,8},{5,9},{6,10},{7,11},{8,4},{9,5},{10,6},{11,7},{20,24},{21,25... | collective-permute-start | bytes 786440 | tf_op jit(solution)/shard_map/ppermute | solution.py:150
  10.5 1.3 %bitcast_select_fusion = (bf16[16,32,256]{2,1,0:T(8,128)(2,1)S(1)}, bf16[16,32,256]{2,1,0:T(8,128)(2,1)S(1)}, bf16[16,32,256]{2,1,0:T(8,128)(2,1)S(1)}, bf16[16,32,256]{2,1,0:T(8,128)(2,1)S(1)}) fusion(bf16[2,16,32,256]{3,2,1,0:T(8,128)(2,1)S(1)} %collective-permute-done.2, s32[]{:T(128)S(6)} %select_n.261, bf16[2,2,16,32,256]{4,3,2,1,0:T(8,128)(2,1)} %bitcast.69, ...), kind=kLoop, calls=%fused_computation.8 | loop fusion | flops 524288 | bytes 3145768 | tf_op jit(solution)/shard_map/jit(_where)/select_n | solution.py:175
  11.8 1.3 %collective-permute-start.3 = (bf16[16,32,256]{2,1,0:T(8,128)(2,1)S(1)}, bf16[16,32,256]{2,1,0:T(8,128)(2,1)S(1)}, u32[]{:S(2)}, u32[]{:S(2)}) collective-permute-start(bf16[16,32,256]{2,1,0:T(8,128)(2,1)S(1)} %get-tuple-element.31.refs_0_), channel_id=1, source_target_pairs={{0,1},{1,0},{2,3},{3,2},{4,5},{5,4},{6,7},{7,6},{8,9},{9,8},{10,11... | collective-permute-start | bytes 786440 | tf_op jit(solution)/shard_map/ppermute | solution.py:150
  13.1 1.4 %collective-permute-start.11 = (bf16[16,32,256]{2,1,0:T(8,128)(2,1)S(1)}, bf16[16,32,256]{2,1,0:T(8,128)(2,1)S(1)}, u32[]{:S(2)}, u32[]{:S(2)}) collective-permute-start(bf16[16,32,256]{2,1,0:T(8,128)(2,1)S(1)} %get-tuple-element.55), channel_id=1, source_target_pairs={{0,2},{1,3},{2,0},{3,1},{4,6},{5,7},{6,4},{7,5},{8,10},{9,11},{10,... | collective-permute-start | bytes 786440 | tf_op jit(solution)/shard_map/ppermute | solution.py:150
  14.9 2.0 %collective-permute-start.13 = (bf16[16,32,256]{2,1,0:T(8,128)(2,1)S(1)}, bf16[16,32,256]{2,1,0:T(8,128)(2,1)S(1)}, u32[]{:S(2)}, u32[]{:S(2)}) collective-permute-start(bf16[16,32,256]{2,1,0:T(8,128)(2,1)S(1)} %get-tuple-element.53), channel_id=1, source_target_pairs={{0,6},{1,7},{2,4},{3,5},{4,2},{5,3},{6,0},{7,1},{8,14},{9,15},{10,... | collective-permute-start | bytes 786440 | tf_op jit(solution)/shard_map/ppermute | solution.py:150
  16.9 2.6 %collective-permute-done.3.refs_1_ = bf16[16,32,256]{2,1,0:T(8,128)(2,1)S(1)} collective-permute-done((bf16[16,32,256]{2,1,0:T(8,128)(2,1)S(1)}, bf16[16,32,256]{2,1,0:T(8,128)(2,1)S(1)}, u32[]{:S(2)}, u32[]{:S(2)}) %collective-permute-start.3) | collective-permute-done | bytes 262176 | tf_op jit(solution)/shard_map/ppermute | solution.py:150
  19.5 1.3 %collective-permute-start.4 = (bf16[2,256,256]{2,1,0:T(8,128)(2,1)S(1)}, bf16[2,256,256]{2,1,0:T(8,128)(2,1)}, u32[]{:S(2)}, u32[]{:S(2)}) collective-permute-start(bf16[2,256,256]{2,1,0:T(8,128)(2,1)S(1)} %broadcast_select_fusion.refs_0_), channel_id=1, source_target_pairs={{0,1},{1,0},{2,3},{3,2},{4,5},{5,4},{6,7},{7,6},{8,9},{9,8},{10,11... | collective-permute-start | bytes 786440 | tf_op jit(solution)/shard_map/ppermute | solution.py:150
  20.8 1.3 %collective-permute-start.5 = (bf16[2,256,256]{2,1,0:T(8,128)(2,1)S(1)}, bf16[2,256,256]{2,1,0:T(8,128)(2,1)}, u32[]{:S(2)}, u32[]{:S(2)}) collective-permute-start(bf16[2,256,256]{2,1,0:T(8,128)(2,1)S(1)} %broadcast_select_fusion.refs_0_), channel_id=1, source_target_pairs={{0,2},{1,3},{2,0},{3,1},{4,6},{5,7},{6,4},{7,5},{8,10},{9,11},{10,... | collective-permute-start | bytes 786440 | tf_op jit(solution)/shard_map/ppermute | solution.py:150
  22.1 1.7 %collective-permute-done.11.refs_2_ = bf16[16,32,256]{2,1,0:T(8,128)(2,1)S(1)} collective-permute-done((bf16[16,32,256]{2,1,0:T(8,128)(2,1)S(1)}, bf16[16,32,256]{2,1,0:T(8,128)(2,1)S(1)}, u32[]{:S(2)}, u32[]{:S(2)}) %collective-permute-start.11) | collective-permute-done | bytes 262176 | tf_op jit(solution)/shard_map/ppermute | solution.py:150
  24.0 9.8 %collective-permute-done.12.refs_4_ = bf16[16,32,256]{2,1,0:T(8,128)(2,1)S(1)} collective-permute-done((bf16[16,32,256]{2,1,0:T(8,128)(2,1)S(1)}, bf16[16,32,256]{2,1,0:T(8,128)(2,1)S(1)}, u32[]{:S(2)}, u32[]{:S(2)}) %collective-permute-start.12) | collective-permute-done | bytes 262176 | tf_op jit(solution)/shard_map/ppermute | solution.py:150
  34.3 3.3 %collective-permute-start.17 = (bf16[16,32,256]{2,1,0:T(8,128)(2,1)S(1)}, bf16[16,32,256]{2,1,0:T(8,128)(2,1)S(1)}, u32[]{:S(2)}, u32[]{:S(2)}) collective-permute-start(bf16[16,32,256]{2,1,0:T(8,128)(2,1)S(1)} %get-tuple-element.31.refs_0_), channel_id=1, source_target_pairs={{0,8},{1,9},{2,10},{3,11},{4,12},{5,13},{6,14},{7,15},{8,0},{9,1},... | collective-permute-start | bytes 786440 | tf_op jit(solution)/shard_map/ppermute | solution.py:150
  39.5 2.9 %collective-permute-start.6 = (bf16[2,256,256]{2,1,0:T(8,128)(2,1)}, bf16[2,256,256]{2,1,0:T(8,128)(2,1)}, u32[]{:S(2)}, u32[]{:S(2)}) collective-permute-start(bf16[2,256,256]{2,1,0:T(8,128)(2,1)} %collective-permute-done.4.refs_1_), channel_id=1, source_target_pairs={{0,2},{1,3},{2,0},{3,1},{4,6},{5,7},{6,4},{7,5},{8,10},{9,11},{10,... | collective-permute-start | bytes 786440 | tf_op jit(solution)/shard_map/ppermute | solution.py:150
  42.5 4.8 %collective-permute-done.16.refs_7_ = bf16[16,32,256]{2,1,0:T(8,128)(2,1)S(1)} collective-permute-done((bf16[16,32,256]{2,1,0:T(8,128)(2,1)S(1)}, bf16[16,32,256]{2,1,0:T(8,128)(2,1)S(1)}, u32[]{:S(2)}, u32[]{:S(2)}) %collective-permute-start.16) | collective-permute-done | bytes 262176 | tf_op jit(solution)/shard_map/ppermute | solution.py:150
  47.2 1.6 %collective-permute-start.7 = (bf16[2,256,256]{2,1,0:T(8,128)(2,1)S(1)}, bf16[2,256,256]{2,1,0:T(8,128)(2,1)}, u32[]{:S(2)}, u32[]{:S(2)}) collective-permute-start(bf16[2,256,256]{2,1,0:T(8,128)(2,1)S(1)} %broadcast_select_fusion.refs_0_), channel_id=1, source_target_pairs={{0,8},{1,9},{2,10},{3,11},{4,12},{5,13},{6,14},{7,15},{8,0},{9,1},... | collective-permute-start | bytes 786440 | tf_op jit(solution)/shard_map/ppermute | solution.py:150
  49.4 1.7 %collective-permute-start.10 = (bf16[2,256,256]{2,1,0:T(8,128)(2,1)}, bf16[2,256,256]{2,1,0:T(8,128)(2,1)}, u32[]{:S(2)}, u32[]{:S(2)}) collective-permute-start(bf16[2,256,256]{2,1,0:T(8,128)(2,1)} %collective-permute-done.6.refs_3_), channel_id=1, source_target_pairs={{0,8},{1,9},{2,10},{3,11},{4,12},{5,13},{6,14},{7,15},{8,0},{9,1},... | collective-permute-start | bytes 786440 | tf_op jit(solution)/shard_map/ppermute | solution.py:150
  52.6 4.4 %mix_envs.1 = (bf16[32,256,256]{2,1,0:T(8,128)(2,1)S(1)}, bf16[32,256,256]{2,1,0:T(8,128)(2,1)S(1)}) custom-call(s32[1]{0:T(128)} %bitcast.4.flip, s32[2]{0:T(128)S(1)} %fusion.10.dims, bf16[64,16]{1,0:T(8,128)(2,1)S(1)} %copy.22.weights, bf16[2,256,256]{2,1,0:T(8,128)(2,1)S(1)} %broadcast_select_fusion.refs_0_, ...), custom_call_target="tpu_custom_call" | custom-call | flops 2147483648 | bytes 10485760 | tf_op jit(solution)/shard_map/mix_envs/pallas_call | solution.py:103
  57.0 3.6 %pair_sums.3 = (f32[2,256,256]{2,1,0:T(8,128)S(1)}, bf16[2,256,256]{2,1,0:T(8,128)(2,1)S(1)}, bf16[2,256,256]{2,1,0:T(8,128)(2,1)S(1)}, bf16[2,256,256]{2,1,0:T(8,128)(2,1)S(1)}) custom-call(s32[32]{0:T(128)S(1)} %fusion.13.slots, s32[8]{0:T(128)S(1)} %select_reduce_fusion.dims, bf16[32,256,256]{2,1,0:T(8,128)(2,1)S(1)} %get-tuple-element.46.mixed, ...), custom_call_target="tpu_custom_call" | custom-call | flops 2147483648 | bytes 10485760 | tf_op jit(solution)/shard_map/pair_sums/pallas_call | solution.py:121
  63.4 3.5 %pair_sums.2 = (f32[2,256,256]{2,1,0:T(8,128)S(1)}, f32[2,256,256]{2,1,0:T(8,128)S(1)}, bf16[2,256,256]{2,1,0:T(8,128)(2,1)S(1)}, f32[2,256,256]{2,1,0:T(8,128)S(1)}) custom-call(s32[32]{0:T(128)S(1)} %fusion.13.slots, s32[8]{0:T(128)S(1)} %select_reduce_fusion.dims, bf16[32,256,256]{2,1,0:T(8,128)(2,1)S(1)} %get-tuple-element.30.mixed, ...), custom_call_target="tpu_custom_call" | custom-call | flops 2147483648 | bytes 10485760 | tf_op jit(solution)/shard_map/pair_sums/pallas_call | solution.py:121
  66.9 1.3 %collective-permute-done.30 = bf16[2,256,256]{2,1,0:T(8,128)(2,1)S(1)} collective-permute-done((bf16[2,256,256]{2,1,0:T(8,128)(2,1)S(1)}, bf16[2,256,256]{2,1,0:T(8,128)(2,1)S(1)}, u32[]{:S(2)}, u32[]{:S(2)}) %collective-permute-start.30) | collective-permute-done | bytes 262176 | tf_op jit(solution)/shard_map/ppermute | solution.py:150
  69.9 1.4 %collective-permute-start.27 = (bf16[2,256,256]{2,1,0:T(8,128)(2,1)S(1)}, bf16[2,256,256]{2,1,0:T(8,128)(2,1)S(1)}, u32[]{:S(2)}, u32[]{:S(2)}) collective-permute-start(bf16[2,256,256]{2,1,0:T(8,128)(2,1)S(1)} %add_convert_fusion.2), channel_id=1, source_target_pairs={{0,2},{1,3},{2,0},{3,1},{4,6},{5,7},{6,4},{7,5},{8,10},{9,11},{10,... | collective-permute-start | bytes 786440 | tf_op jit(solution)/shard_map/ppermute | solution.py:150
  71.3 2.5 %collective-permute-done.29 = bf16[2,256,256]{2,1,0:T(8,128)(2,1)S(1)} collective-permute-done((bf16[2,256,256]{2,1,0:T(8,128)(2,1)S(1)}, bf16[2,256,256]{2,1,0:T(8,128)(2,1)S(1)}, u32[]{:S(2)}, u32[]{:S(2)}) %collective-permute-start.29) | collective-permute-done | bytes 262176 | tf_op jit(solution)/shard_map/ppermute | solution.py:150
  74.9 4.9 %collective-permute-done.25 = bf16[2,256,256]{2,1,0:T(8,128)(2,1)S(1)} collective-permute-done((bf16[2,256,256]{2,1,0:T(8,128)(2,1)S(1)}, bf16[2,256,256]{2,1,0:T(8,128)(2,1)S(1)}, u32[]{:S(2)}, u32[]{:S(2)}) %collective-permute-start.25) | collective-permute-done | bytes 262176 | tf_op jit(solution)/shard_map/ppermute | solution.py:150
  79.9 5.0 %collective-permute-start.28 = (bf16[2,256,256]{2,1,0:T(8,128)(2,1)S(1)}, bf16[2,256,256]{2,1,0:T(8,128)(2,1)S(1)}, u32[]{:S(2)}, u32[]{:S(2)}) collective-permute-start(bf16[2,256,256]{2,1,0:T(8,128)(2,1)S(1)} %fusion), channel_id=1, source_target_pairs={{4,8},{5,9},{6,10},{7,11},{8,4},{9,5},{10,6},{11,7},{20,24},{21,25... | collective-permute-start | bytes 786440 | tf_op jit(solution)/shard_map/ppermute | solution.py:150
  85.0 9.8 %collective-permute-done.28 = bf16[2,256,256]{2,1,0:T(8,128)(2,1)S(1)} collective-permute-done((bf16[2,256,256]{2,1,0:T(8,128)(2,1)S(1)}, bf16[2,256,256]{2,1,0:T(8,128)(2,1)S(1)}, u32[]{:S(2)}, u32[]{:S(2)}) %collective-permute-start.28) | collective-permute-done | bytes 262176 | tf_op jit(solution)/shard_map/ppermute | solution.py:150
  (75 shorter events, 16.4 us)
Async XLA Ops:
  1.5 11.6 %collective-permute-start = (f32[66,64]{1,0:T(8,128)S(1)}, f32[66,64]{1,0:T(8,128)S(1)}, u32[]{:S(2)}, u32[]{:S(2)}) collective-permute-start(f32[66,64]{1,0:T(8,128)S(1)} %pad_maximum_fusion), channel_id=1, source_target_pairs={{0,8},{1,9},{2,10},{3,11},{4,12},{5,13},{6,14},{7,15},{8,0},{9,1},... | collective-permute-start | bytes 50696 | tf_op jit(solution)/shard_map/ppermute | solution.py:150
  1.6 15.3 %collective-permute-start.1 = (bf16[2,256,256]{2,1,0:T(8,128)(2,1)}, bf16[2,256,256]{2,1,0:T(8,128)(2,1)S(1)}, u32[]{:S(2)}, u32[]{:S(2)}) collective-permute-start(bf16[2,256,256]{2,1,0:T(8,128)(2,1)} %bitcast.70), channel_id=1, source_target_pairs={{4,8},{5,9},{6,10},{7,11},{8,4},{9,5},{10,6},{11,7},{20,24},{21,25... | collective-permute-start | bytes 786440 | tf_op jit(solution)/shard_map/ppermute | solution.py:150
  11.8 7.7 %collective-permute-start.3 = (bf16[16,32,256]{2,1,0:T(8,128)(2,1)S(1)}, bf16[16,32,256]{2,1,0:T(8,128)(2,1)S(1)}, u32[]{:S(2)}, u32[]{:S(2)}) collective-permute-start(bf16[16,32,256]{2,1,0:T(8,128)(2,1)S(1)} %get-tuple-element.31.refs_0_), channel_id=1, source_target_pairs={{0,1},{1,0},{2,3},{3,2},{4,5},{5,4},{6,7},{7,6},{8,9},{9,8},{10,11... | collective-permute-start | bytes 786440 | tf_op jit(solution)/shard_map/ppermute | solution.py:150
  13.1 10.7 %collective-permute-start.11 = (bf16[16,32,256]{2,1,0:T(8,128)(2,1)S(1)}, bf16[16,32,256]{2,1,0:T(8,128)(2,1)S(1)}, u32[]{:S(2)}, u32[]{:S(2)}) collective-permute-start(bf16[16,32,256]{2,1,0:T(8,128)(2,1)S(1)} %get-tuple-element.55), channel_id=1, source_target_pairs={{0,2},{1,3},{2,0},{3,1},{4,6},{5,7},{6,4},{7,5},{8,10},{9,11},{10,... | collective-permute-start | bytes 786440 | tf_op jit(solution)/shard_map/ppermute | solution.py:150
  14.5 19.3 %collective-permute-start.12 = (bf16[16,32,256]{2,1,0:T(8,128)(2,1)S(1)}, bf16[16,32,256]{2,1,0:T(8,128)(2,1)S(1)}, u32[]{:S(2)}, u32[]{:S(2)}) collective-permute-start(bf16[16,32,256]{2,1,0:T(8,128)(2,1)S(1)} %get-tuple-element.54), channel_id=1, source_target_pairs={{0,4},{1,5},{2,6},{3,7},{4,0},{5,1},{6,2},{7,3},{8,12},{9,13},{10,... | collective-permute-start | bytes 786440 | tf_op jit(solution)/shard_map/ppermute | solution.py:150
  14.9 19.4 %collective-permute-start.13 = (bf16[16,32,256]{2,1,0:T(8,128)(2,1)S(1)}, bf16[16,32,256]{2,1,0:T(8,128)(2,1)S(1)}, u32[]{:S(2)}, u32[]{:S(2)}) collective-permute-start(bf16[16,32,256]{2,1,0:T(8,128)(2,1)S(1)} %get-tuple-element.53), channel_id=1, source_target_pairs={{0,6},{1,7},{2,4},{3,5},{4,2},{5,3},{6,0},{7,1},{8,14},{9,15},{10,... | collective-permute-start | bytes 786440 | tf_op jit(solution)/shard_map/ppermute | solution.py:150
  19.5 18.1 %collective-permute-start.4 = (bf16[2,256,256]{2,1,0:T(8,128)(2,1)S(1)}, bf16[2,256,256]{2,1,0:T(8,128)(2,1)}, u32[]{:S(2)}, u32[]{:S(2)}) collective-permute-start(bf16[2,256,256]{2,1,0:T(8,128)(2,1)S(1)} %broadcast_select_fusion.refs_0_), channel_id=1, source_target_pairs={{0,1},{1,0},{2,3},{3,2},{4,5},{5,4},{6,7},{7,6},{8,9},{9,8},{10,11... | collective-permute-start | bytes 786440 | tf_op jit(solution)/shard_map/ppermute | solution.py:150
  20.8 16.8 %collective-permute-start.5 = (bf16[2,256,256]{2,1,0:T(8,128)(2,1)S(1)}, bf16[2,256,256]{2,1,0:T(8,128)(2,1)}, u32[]{:S(2)}, u32[]{:S(2)}) collective-permute-start(bf16[2,256,256]{2,1,0:T(8,128)(2,1)S(1)} %broadcast_select_fusion.refs_0_), channel_id=1, source_target_pairs={{0,2},{1,3},{2,0},{3,1},{4,6},{5,7},{6,4},{7,5},{8,10},{9,11},{10,... | collective-permute-start | bytes 786440 | tf_op jit(solution)/shard_map/ppermute | solution.py:150
  23.8 15.1 %collective-permute-start.14 = (bf16[16,32,256]{2,1,0:T(8,128)(2,1)S(1)}, bf16[16,32,256]{2,1,0:T(8,128)(2,1)S(1)}, u32[]{:S(2)}, u32[]{:S(2)}) collective-permute-start(bf16[16,32,256]{2,1,0:T(8,128)(2,1)S(1)} %collective-permute-done.11.refs_2_), channel_id=1, source_target_pairs={{0,1},{1,0},{2,3},{3,2},{4,5},{5,4},{6,7},{7,6},{8,9},{9,8},{10,11... | collective-permute-start | bytes 786440 | tf_op jit(solution)/shard_map/ppermute | solution.py:150
  33.8 5.7 %collective-permute-start.15 = (bf16[16,32,256]{2,1,0:T(8,128)(2,1)S(1)}, bf16[16,32,256]{2,1,0:T(8,128)(2,1)S(1)}, u32[]{:S(2)}, u32[]{:S(2)}) collective-permute-start(bf16[16,32,256]{2,1,0:T(8,128)(2,1)S(1)} %collective-permute-done.12.refs_4_), channel_id=1, source_target_pairs={{0,1},{1,0},{2,3},{3,2},{4,5},{5,4},{6,7},{7,6},{8,9},{9,8},{10,11... | collective-permute-start | bytes 786440 | tf_op jit(solution)/shard_map/ppermute | solution.py:150
  34.3 14.6 %collective-permute-start.17 = (bf16[16,32,256]{2,1,0:T(8,128)(2,1)S(1)}, bf16[16,32,256]{2,1,0:T(8,128)(2,1)S(1)}, u32[]{:S(2)}, u32[]{:S(2)}) collective-permute-start(bf16[16,32,256]{2,1,0:T(8,128)(2,1)S(1)} %get-tuple-element.31.refs_0_), channel_id=1, source_target_pairs={{0,8},{1,9},{2,10},{3,11},{4,12},{5,13},{6,14},{7,15},{8,0},{9,1},... | collective-permute-start | bytes 786440 | tf_op jit(solution)/shard_map/ppermute | solution.py:150
  37.6 11.3 %collective-permute-start.18 = (bf16[16,32,256]{2,1,0:T(8,128)(2,1)S(1)}, bf16[16,32,256]{2,1,0:T(8,128)(2,1)S(1)}, u32[]{:S(2)}, u32[]{:S(2)}) collective-permute-start(bf16[16,32,256]{2,1,0:T(8,128)(2,1)S(1)} %collective-permute-done.11.refs_2_), channel_id=1, source_target_pairs={{0,8},{1,9},{2,10},{3,11},{4,12},{5,13},{6,14},{7,15},{8,0},{9,1},... | collective-permute-start | bytes 786440 | tf_op jit(solution)/shard_map/ppermute | solution.py:150
  37.6 11.7 %collective-permute-start.19 = (bf16[16,32,256]{2,1,0:T(8,128)(2,1)S(1)}, bf16[16,32,256]{2,1,0:T(8,128)(2,1)S(1)}, u32[]{:S(2)}, u32[]{:S(2)}) collective-permute-start(bf16[16,32,256]{2,1,0:T(8,128)(2,1)S(1)} %collective-permute-done.12.refs_4_), channel_id=1, source_target_pairs={{0,8},{1,9},{2,10},{3,11},{4,12},{5,13},{6,14},{7,15},{8,0},{9,1},... | collective-permute-start | bytes 786440 | tf_op jit(solution)/shard_map/ppermute | solution.py:150
  38.9 8.4 %collective-permute-start.16 = (bf16[16,32,256]{2,1,0:T(8,128)(2,1)S(1)}, bf16[16,32,256]{2,1,0:T(8,128)(2,1)S(1)}, u32[]{:S(2)}, u32[]{:S(2)}) collective-permute-start(bf16[16,32,256]{2,1,0:T(8,128)(2,1)S(1)} %collective-permute-done.13.refs_6_), channel_id=1, source_target_pairs={{0,1},{1,0},{2,3},{3,2},{4,5},{5,4},{6,7},{7,6},{8,9},{9,8},{10,11... | collective-permute-start | bytes 786440 | tf_op jit(solution)/shard_map/ppermute | solution.py:150
  39.5 9.9 %collective-permute-start.6 = (bf16[2,256,256]{2,1,0:T(8,128)(2,1)}, bf16[2,256,256]{2,1,0:T(8,128)(2,1)}, u32[]{:S(2)}, u32[]{:S(2)}) collective-permute-start(bf16[2,256,256]{2,1,0:T(8,128)(2,1)} %collective-permute-done.4.refs_1_), channel_id=1, source_target_pairs={{0,2},{1,3},{2,0},{3,1},{4,6},{5,7},{6,4},{7,5},{8,10},{9,11},{10,... | collective-permute-start | bytes 786440 | tf_op jit(solution)/shard_map/ppermute | solution.py:150
  51.3 5.7 %collective-permute-start.21 = (bf16[16,32,256]{2,1,0:T(8,128)(2,1)S(1)}, bf16[16,32,256]{2,1,0:T(8,128)(2,1)S(1)}, u32[]{:S(2)}, u32[]{:S(2)}) collective-permute-start(bf16[16,32,256]{2,1,0:T(8,128)(2,1)S(1)} %collective-permute-done.3.refs_1_), channel_id=1, source_target_pairs={{0,8},{1,9},{2,10},{3,11},{4,12},{5,13},{6,14},{7,15},{8,0},{9,1},... | collective-permute-start | bytes 786440 | tf_op jit(solution)/shard_map/ppermute | solution.py:150
  60.6 7.6 %collective-permute-start.30 = (bf16[2,256,256]{2,1,0:T(8,128)(2,1)S(1)}, bf16[2,256,256]{2,1,0:T(8,128)(2,1)S(1)}, u32[]{:S(2)}, u32[]{:S(2)}) collective-permute-start(bf16[2,256,256]{2,1,0:T(8,128)(2,1)S(1)} %get-tuple-element.52), channel_id=1, source_target_pairs={{0,2},{1,3},{2,0},{3,1},{4,6},{5,7},{6,4},{7,5},{8,10},{9,11},{10,... | collective-permute-start | bytes 786440 | tf_op jit(solution)/shard_map/ppermute | solution.py:150
  61.9 11.9 %collective-permute-start.29 = (bf16[2,256,256]{2,1,0:T(8,128)(2,1)S(1)}, bf16[2,256,256]{2,1,0:T(8,128)(2,1)S(1)}, u32[]{:S(2)}, u32[]{:S(2)}) collective-permute-start(bf16[2,256,256]{2,1,0:T(8,128)(2,1)S(1)} %get-tuple-element.50), channel_id=1, source_target_pairs={{0,2},{1,3},{2,0},{3,1},{4,6},{5,7},{6,4},{7,5},{8,10},{9,11},{10,... | collective-permute-start | bytes 786440 | tf_op jit(solution)/shard_map/ppermute | solution.py:150
  62.2 7.7 %collective-permute-start.26 = (bf16[2,256,256]{2,1,0:T(8,128)(2,1)S(1)}, bf16[2,256,256]{2,1,0:T(8,128)(2,1)S(1)}, u32[]{:S(2)}, u32[]{:S(2)}) collective-permute-start(bf16[2,256,256]{2,1,0:T(8,128)(2,1)S(1)} %get-tuple-element.48), channel_id=1, source_target_pairs={{0,16},{1,17},{2,18},{3,19},{4,20},{5,21},{6,22},{7,23},{8,24},{9,... | collective-permute-start | bytes 786440 | tf_op jit(solution)/shard_map/ppermute | solution.py:150
  68.3 5.9 %collective-permute-start.31 = (bf16[2,256,256]{2,1,0:T(8,128)(2,1)S(1)}, bf16[2,256,256]{2,1,0:T(8,128)(2,1)S(1)}, u32[]{:S(2)}, u32[]{:S(2)}) collective-permute-start(bf16[2,256,256]{2,1,0:T(8,128)(2,1)S(1)} %add_convert_fusion.1), channel_id=1, source_target_pairs={{0,16},{1,17},{2,18},{3,19},{4,20},{5,21},{6,22},{7,23},{8,24},{9,... | collective-permute-start | bytes 786440 | tf_op jit(solution)/shard_map/ppermute | solution.py:150
  69.6 10.2 %collective-permute-start.25 = (bf16[2,256,256]{2,1,0:T(8,128)(2,1)S(1)}, bf16[2,256,256]{2,1,0:T(8,128)(2,1)S(1)}, u32[]{:S(2)}, u32[]{:S(2)}) collective-permute-start(bf16[2,256,256]{2,1,0:T(8,128)(2,1)S(1)} %get-tuple-element.45), channel_id=1, source_target_pairs={{0,16},{1,17},{2,18},{3,19},{4,20},{5,21},{6,22},{7,23},{8,24},{9,... | collective-permute-start | bytes 786440 | tf_op jit(solution)/shard_map/ppermute | solution.py:150
  69.9 9.9 %collective-permute-start.27 = (bf16[2,256,256]{2,1,0:T(8,128)(2,1)S(1)}, bf16[2,256,256]{2,1,0:T(8,128)(2,1)S(1)}, u32[]{:S(2)}, u32[]{:S(2)}) collective-permute-start(bf16[2,256,256]{2,1,0:T(8,128)(2,1)S(1)} %add_convert_fusion.2), channel_id=1, source_target_pairs={{0,2},{1,3},{2,0},{3,1},{4,6},{5,7},{6,4},{7,5},{8,10},{9,11},{10,... | collective-permute-start | bytes 786440 | tf_op jit(solution)/shard_map/ppermute | solution.py:150
  74.3 10.7 %collective-permute-start.32 = (bf16[2,256,256]{2,1,0:T(8,128)(2,1)S(1)}, bf16[2,256,256]{2,1,0:T(8,128)(2,1)S(1)}, u32[]{:S(2)}, u32[]{:S(2)}) collective-permute-start(bf16[2,256,256]{2,1,0:T(8,128)(2,1)S(1)} %add_convert_fusion), channel_id=1, source_target_pairs={{0,8},{1,9},{2,10},{3,11},{4,0},{5,1},{6,2},{7,3},{8,12},{9,13},{1... | collective-permute-start | bytes 786440 | tf_op jit(solution)/shard_map/ppermute | solution.py:150
  79.9 14.9 %collective-permute-start.28 = (bf16[2,256,256]{2,1,0:T(8,128)(2,1)S(1)}, bf16[2,256,256]{2,1,0:T(8,128)(2,1)S(1)}, u32[]{:S(2)}, u32[]{:S(2)}) collective-permute-start(bf16[2,256,256]{2,1,0:T(8,128)(2,1)S(1)} %fusion), channel_id=1, source_target_pairs={{4,8},{5,9},{6,10},{7,11},{8,4},{9,5},{10,6},{11,7},{20,24},{21,25... | collective-permute-start | bytes 786440 | tf_op jit(solution)/shard_map/ppermute | solution.py:150
  (10 other events, 52.9 us)

commit v5 on v4

--- a/solution.py
+++ b/solution.py
@@ -262,14 +262,13 @@
 
     first, second = {}, {}
     for t in reversed(range(half_z)):
-        dtypes = [F32, BF16 if t % 2 else F32] + [BF16, BF16 if t % 2 else F32] * (nx - 1)
+        odd = BF16 if t % 2 else F32
+        dtypes = [odd, F32] + [odd, BF16] * (nx - 1)
         parts = pair_sums(slots, slot_dims, mixed[t], own, others, dtypes, nb)
-        first[t] = over_x(parts[::2])
-        second[t] = parts[1::2]
-    sums = [
-        over_halves(first),
-        over_x([over_halves({t: v[f] for t, v in second.items()}) for f in range(nx)]),
-    ]
+        first[t] = over_x(parts[1::2])
+        second[t] = parts[::2]
+    sums = [over_halves({t: v[f] for t, v in second.items()}) for f in range(nx)]
+    sums = [over_x(sums), over_halves(first)]
     result = jnp.where(c == top, sums[0], 0.0)
     for b in range(2):
         got = send(

time: 96.1 us -> 95.2 us (level)
  no operation moved by 1% of the time
where the time goes in v5:
time: 95.2 us; the launch traced here: 94.9 us
  waiting for transfers between devices  37.9 us (40%)
  starting transfers between devices  37.1 us (39%)
  Pallas kernels  11.5 us (12%)
  other arithmetic  6.17 us (6%)
  local copies, waits for them, and re-layouts  1.45 us (2%)
    ppermute x33, waiting for transfers between devices, send(): return lax.ppermute(value, ('sec', 'term'), perm)  37.9 us
    ppermute x33, starting transfers between devices, send(): return lax.ppermute(value, ('sec', 'term'), perm)  37.1 us
    pallas_call x2, Pallas kernels, pair_sums(): pl.pallas_call(functools.partial(pair_kernel, len(own)), out_shape=[jax.S...  7.12 us
    pallas_call x1, Pallas kernels, mix_envs(): pl.pallas_call(functools.partial(mix_kernel, len(envs)), out_shape=[jax.S...  4.36 us
  transfers between devices with their start and end apart: 33, of which 10 were waited for; matrix products, arithmetic and copies ran while one was open for 6% of the time, Pallas kernels for 8%

profile of v5, /device:TPU:1, one launch (start us, length us, event | category | flops | bytes accessed | tf_op | source)
XLA Modules:
  0.0 94.9 jit_solution(17696079723911995886)
XLA Ops:
  1.6 5.6 %collective-permute-start.1 = (bf16[2,256,256]{2,1,0:T(8,128)(2,1)}, bf16[2,256,256]{2,1,0:T(8,128)(2,1)S(1)}, u32[]{:S(2)}, u32[]{:S(2)}) collective-permute-start(bf16[2,256,256]{2,1,0:T(8,128)(2,1)} %bitcast.70), channel_id=1, source_target_pairs={{4,8},{5,9},{6,10},{7,11},{8,4},{9,5},{10,6},{11,7},{20,24},{21,25... | collective-permute-start | bytes 786440 | tf_op jit(solution)/shard_map/ppermute | solution.py:150
  10.5 1.3 %bitcast_select_fusion = (bf16[16,32,256]{2,1,0:T(8,128)(2,1)S(1)}, bf16[16,32,256]{2,1,0:T(8,128)(2,1)S(1)}, bf16[16,32,256]{2,1,0:T(8,128)(2,1)S(1)}, bf16[16,32,256]{2,1,0:T(8,128)(2,1)S(1)}) fusion(bf16[2,16,32,256]{3,2,1,0:T(8,128)(2,1)S(1)} %collective-permute-done.2, s32[]{:T(128)S(6)} %select_n.261, bf16[2,2,16,32,256]{4,3,2,1,0:T(8,128)(2,1)} %bitcast.69, ...), kind=kLoop, calls=%fused_computation.8 | loop fusion | flops 524288 | bytes 3145768 | tf_op jit(solution)/shard_map/jit(_where)/select_n | solution.py:175
  11.8 1.3 %collective-permute-start.3 = (bf16[16,32,256]{2,1,0:T(8,128)(2,1)S(1)}, bf16[16,32,256]{2,1,0:T(8,128)(2,1)S(1)}, u32[]{:S(2)}, u32[]{:S(2)}) collective-permute-start(bf16[16,32,256]{2,1,0:T(8,128)(2,1)S(1)} %get-tuple-element.31.refs_0_), channel_id=1, source_target_pairs={{0,1},{1,0},{2,3},{3,2},{4,5},{5,4},{6,7},{7,6},{8,9},{9,8},{10,11... | collective-permute-start | bytes 786440 | tf_op jit(solution)/shard_map/ppermute | solution.py:150
  13.1 1.4 %collective-permute-start.11 = (bf16[16,32,256]{2,1,0:T(8,128)(2,1)S(1)}, bf16[16,32,256]{2,1,0:T(8,128)(2,1)S(1)}, u32[]{:S(2)}, u32[]{:S(2)}) collective-permute-start(bf16[16,32,256]{2,1,0:T(8,128)(2,1)S(1)} %get-tuple-element.55), channel_id=1, source_target_pairs={{0,2},{1,3},{2,0},{3,1},{4,6},{5,7},{6,4},{7,5},{8,10},{9,11},{10,... | collective-permute-start | bytes 786440 | tf_op jit(solution)/shard_map/ppermute | solution.py:150
  14.9 2.0 %collective-permute-start.13 = (bf16[16,32,256]{2,1,0:T(8,128)(2,1)S(1)}, bf16[16,32,256]{2,1,0:T(8,128)(2,1)S(1)}, u32[]{:S(2)}, u32[]{:S(2)}) collective-permute-start(bf16[16,32,256]{2,1,0:T(8,128)(2,1)S(1)} %get-tuple-element.53), channel_id=1, source_target_pairs={{0,6},{1,7},{2,4},{3,5},{4,2},{5,3},{6,0},{7,1},{8,14},{9,15},{10,... | collective-permute-start | bytes 786440 | tf_op jit(solution)/shard_map/ppermute | solution.py:150
  16.9 2.6 %collective-permute-done.3.refs_1_ = bf16[16,32,256]{2,1,0:T(8,128)(2,1)S(1)} collective-permute-done((bf16[16,32,256]{2,1,0:T(8,128)(2,1)S(1)}, bf16[16,32,256]{2,1,0:T(8,128)(2,1)S(1)}, u32[]{:S(2)}, u32[]{:S(2)}) %collective-permute-start.3) | collective-permute-done | bytes 262176 | tf_op jit(solution)/shard_map/ppermute | solution.py:150
  19.5 1.3 %collective-permute-start.4 = (bf16[2,256,256]{2,1,0:T(8,128)(2,1)S(1)}, bf16[2,256,256]{2,1,0:T(8,128)(2,1)}, u32[]{:S(2)}, u32[]{:S(2)}) collective-permute-start(bf16[2,256,256]{2,1,0:T(8,128)(2,1)S(1)} %broadcast_select_fusion.refs_0_), channel_id=1, source_target_pairs={{0,1},{1,0},{2,3},{3,2},{4,5},{5,4},{6,7},{7,6},{8,9},{9,8},{10,11... | collective-permute-start | bytes 786440 | tf_op jit(solution)/shard_map/ppermute | solution.py:150
  20.8 1.3 %collective-permute-start.5 = (bf16[2,256,256]{2,1,0:T(8,128)(2,1)S(1)}, bf16[2,256,256]{2,1,0:T(8,128)(2,1)}, u32[]{:S(2)}, u32[]{:S(2)}) collective-permute-start(bf16[2,256,256]{2,1,0:T(8,128)(2,1)S(1)} %broadcast_select_fusion.refs_0_), channel_id=1, source_target_pairs={{0,2},{1,3},{2,0},{3,1},{4,6},{5,7},{6,4},{7,5},{8,10},{9,11},{10,... | collective-permute-start | bytes 786440 | tf_op jit(solution)/shard_map/ppermute | solution.py:150
  22.1 1.7 %collective-permute-done.11.refs_2_ = bf16[16,32,256]{2,1,0:T(8,128)(2,1)S(1)} collective-permute-done((bf16[16,32,256]{2,1,0:T(8,128)(2,1)S(1)}, bf16[16,32,256]{2,1,0:T(8,128)(2,1)S(1)}, u32[]{:S(2)}, u32[]{:S(2)}) %collective-permute-start.11) | collective-permute-done | bytes 262176 | tf_op jit(solution)/shard_map/ppermute | solution.py:150
  24.0 9.8 %collective-permute-done.12.refs_4_ = bf16[16,32,256]{2,1,0:T(8,128)(2,1)S(1)} collective-permute-done((bf16[16,32,256]{2,1,0:T(8,128)(2,1)S(1)}, bf16[16,32,256]{2,1,0:T(8,128)(2,1)S(1)}, u32[]{:S(2)}, u32[]{:S(2)}) %collective-permute-start.12) | collective-permute-done | bytes 262176 | tf_op jit(solution)/shard_map/ppermute | solution.py:150
  34.3 3.3 %collective-permute-start.17 = (bf16[16,32,256]{2,1,0:T(8,128)(2,1)S(1)}, bf16[16,32,256]{2,1,0:T(8,128)(2,1)S(1)}, u32[]{:S(2)}, u32[]{:S(2)}) collective-permute-start(bf16[16,32,256]{2,1,0:T(8,128)(2,1)S(1)} %get-tuple-element.31.refs_0_), channel_id=1, source_target_pairs={{0,8},{1,9},{2,10},{3,11},{4,12},{5,13},{6,14},{7,15},{8,0},{9,1},... | collective-permute-start | bytes 786440 | tf_op jit(solution)/shard_map/ppermute | solution.py:150
  39.5 2.9 %collective-permute-start.6 = (bf16[2,256,256]{2,1,0:T(8,128)(2,1)}, bf16[2,256,256]{2,1,0:T(8,128)(2,1)}, u32[]{:S(2)}, u32[]{:S(2)}) collective-permute-start(bf16[2,256,256]{2,1,0:T(8,128)(2,1)} %collective-permute-done.4.refs_1_), channel_id=1, source_target_pairs={{0,2},{1,3},{2,0},{3,1},{4,6},{5,7},{6,4},{7,5},{8,10},{9,11},{10,... | collective-permute-start | bytes 786440 | tf_op jit(solution)/shard_map/ppermute | solution.py:150
  42.5 4.8 %collective-permute-done.16.refs_7_ = bf16[16,32,256]{2,1,0:T(8,128)(2,1)S(1)} collective-permute-done((bf16[16,32,256]{2,1,0:T(8,128)(2,1)S(1)}, bf16[16,32,256]{2,1,0:T(8,128)(2,1)S(1)}, u32[]{:S(2)}, u32[]{:S(2)}) %collective-permute-start.16) | collective-permute-done | bytes 262176 | tf_op jit(solution)/shard_map/ppermute | solution.py:150
  47.2 1.6 %collective-permute-start.7 = (bf16[2,256,256]{2,1,0:T(8,128)(2,1)S(1)}, bf16[2,256,256]{2,1,0:T(8,128)(2,1)}, u32[]{:S(2)}, u32[]{:S(2)}) collective-permute-start(bf16[2,256,256]{2,1,0:T(8,128)(2,1)S(1)} %broadcast_select_fusion.refs_0_), channel_id=1, source_target_pairs={{0,8},{1,9},{2,10},{3,11},{4,12},{5,13},{6,14},{7,15},{8,0},{9,1},... | collective-permute-start | bytes 786440 | tf_op jit(solution)/shard_map/ppermute | solution.py:150
  49.4 1.7 %collective-permute-start.10 = (bf16[2,256,256]{2,1,0:T(8,128)(2,1)}, bf16[2,256,256]{2,1,0:T(8,128)(2,1)}, u32[]{:S(2)}, u32[]{:S(2)}) collective-permute-start(bf16[2,256,256]{2,1,0:T(8,128)(2,1)} %collective-permute-done.6.refs_3_), channel_id=1, source_target_pairs={{0,8},{1,9},{2,10},{3,11},{4,12},{5,13},{6,14},{7,15},{8,0},{9,1},... | collective-permute-start | bytes 786440 | tf_op jit(solution)/shard_map/ppermute | solution.py:150
  52.6 4.4 %mix_envs.1 = (bf16[32,256,256]{2,1,0:T(8,128)(2,1)S(1)}, bf16[32,256,256]{2,1,0:T(8,128)(2,1)S(1)}) custom-call(s32[1]{0:T(128)} %bitcast.4.flip, s32[2]{0:T(128)S(1)} %fusion.10.dims, bf16[64,16]{1,0:T(8,128)(2,1)S(1)} %copy.22.weights, bf16[2,256,256]{2,1,0:T(8,128)(2,1)S(1)} %broadcast_select_fusion.refs_0_, ...), custom_call_target="tpu_custom_call" | custom-call | flops 2147483648 | bytes 10485760 | tf_op jit(solution)/shard_map/mix_envs/pallas_call | solution.py:103
  57.0 3.6 %pair_sums.3 = (bf16[2,256,256]{2,1,0:T(8,128)(2,1)S(1)}, f32[2,256,256]{2,1,0:T(8,128)S(1)}, bf16[2,256,256]{2,1,0:T(8,128)(2,1)S(1)}, bf16[2,256,256]{2,1,0:T(8,128)(2,1)S(1)}) custom-call(s32[32]{0:T(128)S(1)} %fusion.13.slots, s32[8]{0:T(128)S(1)} %select_reduce_fusion.dims, bf16[32,256,256]{2,1,0:T(8,128)(2,1)S(1)} %get-tuple-element.45.mixed, ...), custom_call_target="tpu_custom_call" | custom-call | flops 2147483648 | bytes 10485760 | tf_op jit(solution)/shard_map/pair_sums/pallas_call | solution.py:121
  60.6 1.3 %collective-permute-start.30 = (bf16[2,256,256]{2,1,0:T(8,128)(2,1)S(1)}, bf16[2,256,256]{2,1,0:T(8,128)(2,1)S(1)}, u32[]{:S(2)}, u32[]{:S(2)}) collective-permute-start(bf16[2,256,256]{2,1,0:T(8,128)(2,1)S(1)} %get-tuple-element.52), channel_id=1, source_target_pairs={{0,16},{1,17},{2,18},{3,19},{4,20},{5,21},{6,22},{7,23},{8,24},{9,... | collective-permute-start | bytes 786440 | tf_op jit(solution)/shard_map/ppermute | solution.py:150
  63.1 3.5 %pair_sums.2 = (f32[2,256,256]{2,1,0:T(8,128)S(1)}, f32[2,256,256]{2,1,0:T(8,128)S(1)}, f32[2,256,256]{2,1,0:T(8,128)S(1)}, bf16[2,256,256]{2,1,0:T(8,128)(2,1)S(1)}) custom-call(s32[32]{0:T(128)S(1)} %fusion.13.slots, s32[8]{0:T(128)S(1)} %select_reduce_fusion.dims, bf16[32,256,256]{2,1,0:T(8,128)(2,1)S(1)} %get-tuple-element.30.mixed, ...), custom_call_target="tpu_custom_call" | custom-call | flops 2147483648 | bytes 10485760 | tf_op jit(solution)/shard_map/pair_sums/pallas_call | solution.py:121
  68.3 1.4 %collective-permute-start.31 = (bf16[2,256,256]{2,1,0:T(8,128)(2,1)S(1)}, bf16[2,256,256]{2,1,0:T(8,128)(2,1)S(1)}, u32[]{:S(2)}, u32[]{:S(2)}) collective-permute-start(bf16[2,256,256]{2,1,0:T(8,128)(2,1)S(1)} %add_convert_fusion.1), channel_id=1, source_target_pairs={{0,2},{1,3},{2,0},{3,1},{4,6},{5,7},{6,4},{7,5},{8,10},{9,11},{10,... | collective-permute-start | bytes 786440 | tf_op jit(solution)/shard_map/ppermute | solution.py:150
  71.2 2.5 %collective-permute-done.29 = bf16[2,256,256]{2,1,0:T(8,128)(2,1)S(1)} collective-permute-done((bf16[2,256,256]{2,1,0:T(8,128)(2,1)S(1)}, bf16[2,256,256]{2,1,0:T(8,128)(2,1)S(1)}, u32[]{:S(2)}, u32[]{:S(2)}) %collective-permute-start.29) | collective-permute-done | bytes 262176 | tf_op jit(solution)/shard_map/ppermute | solution.py:150
  75.1 5.4 %collective-permute-done.25 = bf16[2,256,256]{2,1,0:T(8,128)(2,1)S(1)} collective-permute-done((bf16[2,256,256]{2,1,0:T(8,128)(2,1)S(1)}, bf16[2,256,256]{2,1,0:T(8,128)(2,1)S(1)}, u32[]{:S(2)}, u32[]{:S(2)}) %collective-permute-start.25) | collective-permute-done | bytes 262176 | tf_op jit(solution)/shard_map/ppermute | solution.py:150
  80.7 4.8 %collective-permute-start.28 = (bf16[2,256,256]{2,1,0:T(8,128)(2,1)S(1)}, bf16[2,256,256]{2,1,0:T(8,128)(2,1)S(1)}, u32[]{:S(2)}, u32[]{:S(2)}) collective-permute-start(bf16[2,256,256]{2,1,0:T(8,128)(2,1)S(1)} %fusion), channel_id=1, source_target_pairs={{4,8},{5,9},{6,10},{7,11},{8,4},{9,5},{10,6},{11,7},{20,24},{21,25... | collective-permute-start | bytes 786440 | tf_op jit(solution)/shard_map/ppermute | solution.py:150
  85.6 8.4 %collective-permute-done.28 = bf16[2,256,256]{2,1,0:T(8,128)(2,1)S(1)} collective-permute-done((bf16[2,256,256]{2,1,0:T(8,128)(2,1)S(1)}, bf16[2,256,256]{2,1,0:T(8,128)(2,1)S(1)}, u32[]{:S(2)}, u32[]{:S(2)}) %collective-permute-start.28) | collective-permute-done | bytes 262176 | tf_op jit(solution)/shard_map/ppermute | solution.py:150
  (75 shorter events, 16.7 us)
Async XLA Ops:
  1.5 11.6 %collective-permute-start = (f32[66,64]{1,0:T(8,128)S(1)}, f32[66,64]{1,0:T(8,128)S(1)}, u32[]{:S(2)}, u32[]{:S(2)}) collective-permute-start(f32[66,64]{1,0:T(8,128)S(1)} %pad_maximum_fusion), channel_id=1, source_target_pairs={{0,8},{1,9},{2,10},{3,11},{4,12},{5,13},{6,14},{7,15},{8,0},{9,1},... | collective-permute-start | bytes 50696 | tf_op jit(solution)/shard_map/ppermute | solution.py:150
  1.6 15.3 %collective-permute-start.1 = (bf16[2,256,256]{2,1,0:T(8,128)(2,1)}, bf16[2,256,256]{2,1,0:T(8,128)(2,1)S(1)}, u32[]{:S(2)}, u32[]{:S(2)}) collective-permute-start(bf16[2,256,256]{2,1,0:T(8,128)(2,1)} %bitcast.70), channel_id=1, source_target_pairs={{4,8},{5,9},{6,10},{7,11},{8,4},{9,5},{10,6},{11,7},{20,24},{21,25... | collective-permute-start | bytes 786440 | tf_op jit(solution)/shard_map/ppermute | solution.py:150
  11.8 7.7 %collective-permute-start.3 = (bf16[16,32,256]{2,1,0:T(8,128)(2,1)S(1)}, bf16[16,32,256]{2,1,0:T(8,128)(2,1)S(1)}, u32[]{:S(2)}, u32[]{:S(2)}) collective-permute-start(bf16[16,32,256]{2,1,0:T(8,128)(2,1)S(1)} %get-tuple-element.31.refs_0_), channel_id=1, source_target_pairs={{0,1},{1,0},{2,3},{3,2},{4,5},{5,4},{6,7},{7,6},{8,9},{9,8},{10,11... | collective-permute-start | bytes 786440 | tf_op jit(solution)/shard_map/ppermute | solution.py:150
  13.1 10.7 %collective-permute-start.11 = (bf16[16,32,256]{2,1,0:T(8,128)(2,1)S(1)}, bf16[16,32,256]{2,1,0:T(8,128)(2,1)S(1)}, u32[]{:S(2)}, u32[]{:S(2)}) collective-permute-start(bf16[16,32,256]{2,1,0:T(8,128)(2,1)S(1)} %get-tuple-element.55), channel_id=1, source_target_pairs={{0,2},{1,3},{2,0},{3,1},{4,6},{5,7},{6,4},{7,5},{8,10},{9,11},{10,... | collective-permute-start | bytes 786440 | tf_op jit(solution)/shard_map/ppermute | solution.py:150
  14.5 19.3 %collective-permute-start.12 = (bf16[16,32,256]{2,1,0:T(8,128)(2,1)S(1)}, bf16[16,32,256]{2,1,0:T(8,128)(2,1)S(1)}, u32[]{:S(2)}, u32[]{:S(2)}) collective-permute-start(bf16[16,32,256]{2,1,0:T(8,128)(2,1)S(1)} %get-tuple-element.54), channel_id=1, source_target_pairs={{0,4},{1,5},{2,6},{3,7},{4,0},{5,1},{6,2},{7,3},{8,12},{9,13},{10,... | collective-permute-start | bytes 786440 | tf_op jit(solution)/shard_map/ppermute | solution.py:150
  14.9 19.4 %collective-permute-start.13 = (bf16[16,32,256]{2,1,0:T(8,128)(2,1)S(1)}, bf16[16,32,256]{2,1,0:T(8,128)(2,1)S(1)}, u32[]{:S(2)}, u32[]{:S(2)}) collective-permute-start(bf16[16,32,256]{2,1,0:T(8,128)(2,1)S(1)} %get-tuple-element.53), channel_id=1, source_target_pairs={{0,6},{1,7},{2,4},{3,5},{4,2},{5,3},{6,0},{7,1},{8,14},{9,15},{10,... | collective-permute-start | bytes 786440 | tf_op jit(solution)/shard_map/ppermute | solution.py:150
  19.5 18.1 %collective-permute-start.4 = (bf16[2,256,256]{2,1,0:T(8,128)(2,1)S(1)}, bf16[2,256,256]{2,1,0:T(8,128)(2,1)}, u32[]{:S(2)}, u32[]{:S(2)}) collective-permute-start(bf16[2,256,256]{2,1,0:T(8,128)(2,1)S(1)} %broadcast_select_fusion.refs_0_), channel_id=1, source_target_pairs={{0,1},{1,0},{2,3},{3,2},{4,5},{5,4},{6,7},{7,6},{8,9},{9,8},{10,11... | collective-permute-start | bytes 786440 | tf_op jit(solution)/shard_map/ppermute | solution.py:150
  20.8 16.8 %collective-permute-start.5 = (bf16[2,256,256]{2,1,0:T(8,128)(2,1)S(1)}, bf16[2,256,256]{2,1,0:T(8,128)(2,1)}, u32[]{:S(2)}, u32[]{:S(2)}) collective-permute-start(bf16[2,256,256]{2,1,0:T(8,128)(2,1)S(1)} %broadcast_select_fusion.refs_0_), channel_id=1, source_target_pairs={{0,2},{1,3},{2,0},{3,1},{4,6},{5,7},{6,4},{7,5},{8,10},{9,11},{10,... | collective-permute-start | bytes 786440 | tf_op jit(solution)/shard_map/ppermute | solution.py:150
  23.8 15.1 %collective-permute-start.14 = (bf16[16,32,256]{2,1,0:T(8,128)(2,1)S(1)}, bf16[16,32,256]{2,1,0:T(8,128)(2,1)S(1)}, u32[]{:S(2)}, u32[]{:S(2)}) collective-permute-start(bf16[16,32,256]{2,1,0:T(8,128)(2,1)S(1)} %collective-permute-done.11.refs_2_), channel_id=1, source_target_pairs={{0,1},{1,0},{2,3},{3,2},{4,5},{5,4},{6,7},{7,6},{8,9},{9,8},{10,11... | collective-permute-start | bytes 786440 | tf_op jit(solution)/shard_map/ppermute | solution.py:150
  33.8 5.7 %collective-permute-start.15 = (bf16[16,32,256]{2,1,0:T(8,128)(2,1)S(1)}, bf16[16,32,256]{2,1,0:T(8,128)(2,1)S(1)}, u32[]{:S(2)}, u32[]{:S(2)}) collective-permute-start(bf16[16,32,256]{2,1,0:T(8,128)(2,1)S(1)} %collective-permute-done.12.refs_4_), channel_id=1, source_target_pairs={{0,1},{1,0},{2,3},{3,2},{4,5},{5,4},{6,7},{7,6},{8,9},{9,8},{10,11... | collective-permute-start | bytes 786440 | tf_op jit(solution)/shard_map/ppermute | solution.py:150
  34.3 14.6 %collective-permute-start.17 = (bf16[16,32,256]{2,1,0:T(8,128)(2,1)S(1)}, bf16[16,32,256]{2,1,0:T(8,128)(2,1)S(1)}, u32[]{:S(2)}, u32[]{:S(2)}) collective-permute-start(bf16[16,32,256]{2,1,0:T(8,128)(2,1)S(1)} %get-tuple-element.31.refs_0_), channel_id=1, source_target_pairs={{0,8},{1,9},{2,10},{3,11},{4,12},{5,13},{6,14},{7,15},{8,0},{9,1},... | collective-permute-start | bytes 786440 | tf_op jit(solution)/shard_map/ppermute | solution.py:150
  37.6 11.3 %collective-permute-start.18 = (bf16[16,32,256]{2,1,0:T(8,128)(2,1)S(1)}, bf16[16,32,256]{2,1,0:T(8,128)(2,1)S(1)}, u32[]{:S(2)}, u32[]{:S(2)}) collective-permute-start(bf16[16,32,256]{2,1,0:T(8,128)(2,1)S(1)} %collective-permute-done.11.refs_2_), channel_id=1, source_target_pairs={{0,8},{1,9},{2,10},{3,11},{4,12},{5,13},{6,14},{7,15},{8,0},{9,1},... | collective-permute-start | bytes 786440 | tf_op jit(solution)/shard_map/ppermute | solution.py:150
  37.6 11.7 %collective-permute-start.19 = (bf16[16,32,256]{2,1,0:T(8,128)(2,1)S(1)}, bf16[16,32,256]{2,1,0:T(8,128)(2,1)S(1)}, u32[]{:S(2)}, u32[]{:S(2)}) collective-permute-start(bf16[16,32,256]{2,1,0:T(8,128)(2,1)S(1)} %collective-permute-done.12.refs_4_), channel_id=1, source_target_pairs={{0,8},{1,9},{2,10},{3,11},{4,12},{5,13},{6,14},{7,15},{8,0},{9,1},... | collective-permute-start | bytes 786440 | tf_op jit(solution)/shard_map/ppermute | solution.py:150
  38.9 8.4 %collective-permute-start.16 = (bf16[16,32,256]{2,1,0:T(8,128)(2,1)S(1)}, bf16[16,32,256]{2,1,0:T(8,128)(2,1)S(1)}, u32[]{:S(2)}, u32[]{:S(2)}) collective-permute-start(bf16[16,32,256]{2,1,0:T(8,128)(2,1)S(1)} %collective-permute-done.13.refs_6_), channel_id=1, source_target_pairs={{0,1},{1,0},{2,3},{3,2},{4,5},{5,4},{6,7},{7,6},{8,9},{9,8},{10,11... | collective-permute-start | bytes 786440 | tf_op jit(solution)/shard_map/ppermute | solution.py:150
  39.5 9.9 %collective-permute-start.6 = (bf16[2,256,256]{2,1,0:T(8,128)(2,1)}, bf16[2,256,256]{2,1,0:T(8,128)(2,1)}, u32[]{:S(2)}, u32[]{:S(2)}) collective-permute-start(bf16[2,256,256]{2,1,0:T(8,128)(2,1)} %collective-permute-done.4.refs_1_), channel_id=1, source_target_pairs={{0,2},{1,3},{2,0},{3,1},{4,6},{5,7},{6,4},{7,5},{8,10},{9,11},{10,... | collective-permute-start | bytes 786440 | tf_op jit(solution)/shard_map/ppermute | solution.py:150
  51.3 5.7 %collective-permute-start.21 = (bf16[16,32,256]{2,1,0:T(8,128)(2,1)S(1)}, bf16[16,32,256]{2,1,0:T(8,128)(2,1)S(1)}, u32[]{:S(2)}, u32[]{:S(2)}) collective-permute-start(bf16[16,32,256]{2,1,0:T(8,128)(2,1)S(1)} %collective-permute-done.3.refs_1_), channel_id=1, source_target_pairs={{0,8},{1,9},{2,10},{3,11},{4,12},{5,13},{6,14},{7,15},{8,0},{9,1},... | collective-permute-start | bytes 786440 | tf_op jit(solution)/shard_map/ppermute | solution.py:150
  60.6 7.6 %collective-permute-start.30 = (bf16[2,256,256]{2,1,0:T(8,128)(2,1)S(1)}, bf16[2,256,256]{2,1,0:T(8,128)(2,1)S(1)}, u32[]{:S(2)}, u32[]{:S(2)}) collective-permute-start(bf16[2,256,256]{2,1,0:T(8,128)(2,1)S(1)} %get-tuple-element.52), channel_id=1, source_target_pairs={{0,16},{1,17},{2,18},{3,19},{4,20},{5,21},{6,22},{7,23},{8,24},{9,... | collective-permute-start | bytes 786440 | tf_op jit(solution)/shard_map/ppermute | solution.py:150
  61.9 7.9 %collective-permute-start.26 = (bf16[2,256,256]{2,1,0:T(8,128)(2,1)S(1)}, bf16[2,256,256]{2,1,0:T(8,128)(2,1)S(1)}, u32[]{:S(2)}, u32[]{:S(2)}) collective-permute-start(bf16[2,256,256]{2,1,0:T(8,128)(2,1)S(1)} %get-tuple-element.48), channel_id=1, source_target_pairs={{0,2},{1,3},{2,0},{3,1},{4,6},{5,7},{6,4},{7,5},{8,10},{9,11},{10,... | collective-permute-start | bytes 786440 | tf_op jit(solution)/shard_map/ppermute | solution.py:150
  66.6 7.1 %collective-permute-start.29 = (bf16[2,256,256]{2,1,0:T(8,128)(2,1)S(1)}, bf16[2,256,256]{2,1,0:T(8,128)(2,1)S(1)}, u32[]{:S(2)}, u32[]{:S(2)}) collective-permute-start(bf16[2,256,256]{2,1,0:T(8,128)(2,1)S(1)} %get-tuple-element.50), channel_id=1, source_target_pairs={{0,16},{1,17},{2,18},{3,19},{4,20},{5,21},{6,22},{7,23},{8,24},{9,... | collective-permute-start | bytes 786440 | tf_op jit(solution)/shard_map/ppermute | solution.py:150
  68.3 6.7 %collective-permute-start.31 = (bf16[2,256,256]{2,1,0:T(8,128)(2,1)S(1)}, bf16[2,256,256]{2,1,0:T(8,128)(2,1)S(1)}, u32[]{:S(2)}, u32[]{:S(2)}) collective-permute-start(bf16[2,256,256]{2,1,0:T(8,128)(2,1)S(1)} %add_convert_fusion.1), channel_id=1, source_target_pairs={{0,2},{1,3},{2,0},{3,1},{4,6},{5,7},{6,4},{7,5},{8,10},{9,11},{10,... | collective-permute-start | bytes 786440 | tf_op jit(solution)/shard_map/ppermute | solution.py:150
  69.7 10.9 %collective-permute-start.25 = (bf16[2,256,256]{2,1,0:T(8,128)(2,1)S(1)}, bf16[2,256,256]{2,1,0:T(8,128)(2,1)S(1)}, u32[]{:S(2)}, u32[]{:S(2)}) collective-permute-start(bf16[2,256,256]{2,1,0:T(8,128)(2,1)S(1)} %get-tuple-element.46), channel_id=1, source_target_pairs={{0,2},{1,3},{2,0},{3,1},{4,6},{5,7},{6,4},{7,5},{8,10},{9,11},{10,... | collective-permute-start | bytes 786440 | tf_op jit(solution)/shard_map/ppermute | solution.py:150
  69.9 10.7 %collective-permute-start.27 = (bf16[2,256,256]{2,1,0:T(8,128)(2,1)S(1)}, bf16[2,256,256]{2,1,0:T(8,128)(2,1)S(1)}, u32[]{:S(2)}, u32[]{:S(2)}) collective-permute-start(bf16[2,256,256]{2,1,0:T(8,128)(2,1)S(1)} %add_convert_fusion.2), channel_id=1, source_target_pairs={{0,16},{1,17},{2,18},{3,19},{4,20},{5,21},{6,22},{7,23},{8,24},{9,... | collective-permute-start | bytes 786440 | tf_op jit(solution)/shard_map/ppermute | solution.py:150
  75.1 10.5 %collective-permute-start.32 = (bf16[2,256,256]{2,1,0:T(8,128)(2,1)S(1)}, bf16[2,256,256]{2,1,0:T(8,128)(2,1)S(1)}, u32[]{:S(2)}, u32[]{:S(2)}) collective-permute-start(bf16[2,256,256]{2,1,0:T(8,128)(2,1)S(1)} %add_convert_fusion), channel_id=1, source_target_pairs={{0,8},{1,9},{2,10},{3,11},{4,0},{5,1},{6,2},{7,3},{8,12},{9,13},{1... | collective-permute-start | bytes 786440 | tf_op jit(solution)/shard_map/ppermute | solution.py:150
  80.7 13.3 %collective-permute-start.28 = (bf16[2,256,256]{2,1,0:T(8,128)(2,1)S(1)}, bf16[2,256,256]{2,1,0:T(8,128)(2,1)S(1)}, u32[]{:S(2)}, u32[]{:S(2)}) collective-permute-start(bf16[2,256,256]{2,1,0:T(8,128)(2,1)S(1)} %fusion), channel_id=1, source_target_pairs={{4,8},{5,9},{6,10},{7,11},{8,4},{9,5},{10,6},{11,7},{20,24},{21,25... | collective-permute-start | bytes 786440 | tf_op jit(solution)/shard_map/ppermute | solution.py:150
  (10 other events, 52.9 us)
